TPU v7x, 32 devices: a whole 2x2x4 slice. The times are simulated.
32 devices in a mesh: ctx: 16 (over z, y, core), head: 2 (over x).
Axes of the slice: x: 2, y: 2, z: 4, core: 2. Of those that a mesh axis runs over, the one named last changes fastest.
Arguments:
- messages: bfloat16 [65536, 1024], P('ctx', 'head'), may hold values from -6 to 6
- node_anchor: int32 [65536], P('ctx'), may hold values from 0 to 4095, as said below
- anchor_count: int32 [16], P('ctx'), may hold values from 48 to 192, as said below
- norm_gain: float32 [1024], replicated, may hold values from 0.5 to 1.5
- w_query: bfloat16 [1024, 1024], P(None, 'head'), may hold values from -16 to 16
- w_key: bfloat16 [1024, 1024], P(None, 'head'), may hold values from -0.3125 to 0.3125
- w_value: bfloat16 [1024, 1024], P(None, 'head'), may hold values from -0.1875 to 0.1875
- w_out: bfloat16 [1024, 1024], P(None, 'head'), may hold values from -0.25 to 0.25
Outputs:
- anchor_out: bfloat16 [4096, 1024], P('ctx', 'head')
Inputs may be any that keep to these rules, and one draw needn't show every extreme that they name: node_anchor[n] names a live anchor (its slot within the partition is below that partition's anchor_count); its partition is the partition of node n or one of the two partitions beside it, counted cyclically; all 128 nodes of an aligned tile of 128 nodes have the same anchor partition; every partition has tiles pooled into each of its two neighbours. `anchor_count`: some partition has exactly 192 live anchors.
All inputs are finite; a program needn't handle non-finite values.
Results may differ from a plain program's by a relative error of at most 0.006.
The roundings to bfloat16 on the way count: a program that leaves them out, or rounds other values in their place, can miss the bound.
Values may be sent and summed in bfloat16 or wider, within the bound.
No kernel may reach another device: no remote copies, remote signals or barrier semaphores. Data moves between devices by JAX's collectives and lax.ppermute only.
A program may use at most 128 MiB of HBM per device.

v0:
```python
import math

import jax
import jax.numpy as jnp
from jax import lax
from jax.sharding import PartitionSpec as P

HD = 64
ANCH_DEV = 256


EPS = 1e-06
NEG = -1e30


def from_behind(x, axis, by):
    peers = lax.axis_size(axis)
    return lax.ppermute(x, axis, [(i, (i + by) % peers) for i in range(peers)])


def pool_local(messages, node_anchor, center):
    partitions = lax.axis_size("ctx")
    owner_dev = node_anchor // ANCH_DEV
    offset = (owner_dev - center + 1 + partitions) % partitions
    local_slot = node_anchor % ANCH_DEV
    channel_count = messages.shape[1]
    tile_count = messages.shape[0] // 128
    group = math.gcd(tile_count, 4)
    steps_count = tile_count // group
    slot_blocks = local_slot.reshape(steps_count, group, 128)
    offset_blocks = offset.reshape(steps_count, group, 128)[:, :, 0]
    message_blocks = messages.reshape(steps_count, group, 128, channel_count)
    columns = jnp.arange(ANCH_DEV, dtype=jnp.int32)

    def add_block(running, pieces):
        slot_block, offset_block, message_block = pieces
        onehot = (slot_block[:, :, None] == columns[None, None, :]).astype(jnp.bfloat16)
        partial_value = jnp.einsum(
            "tnk,tnc->tkc", onehot, message_block, preferred_element_type=jnp.float32
        )
        for tile in range(group):
            where = offset_block[tile]
            current = lax.dynamic_index_in_dim(running, where, 0, keepdims=False)
            running = lax.dynamic_update_index_in_dim(
                running, current + partial_value[tile], where, 0
            )
        return (running, None)

    initial = jnp.zeros((3, ANCH_DEV, channel_count), jnp.float32)
    running, unused = lax.scan(add_block, initial, (slot_blocks, offset_blocks, message_blocks))
    return running


def make_fold(queries, shard_rows, scale):
    heads_local = queries.shape[1]

    def fold(carry, pieces, start_row):
        key_rows, value_rows, live_rows = pieces
        shards = live_rows.shape[0] // shard_rows
        key_blocks = key_rows.reshape(shards, shard_rows, heads_local, HD)
        value_blocks = value_rows.reshape(shards, shard_rows, heads_local, HD)
        live_blocks = live_rows.reshape(shards, shard_rows)

        def visit(state, block):
            highest, totals, accum = state
            key_block, value_block, live_block = block
            scores = (
                jnp.einsum("qhd,khd->hqk", queries, key_block, preferred_element_type=jnp.float32)
                * scale
            )
            alive = (live_block > 0)[None, None, :]
            scores = jnp.where(alive, scores, NEG)
            newest = jnp.maximum(highest, jnp.max(scores, axis=-1))
            weights = jnp.where(alive, jnp.exp(scores - newest[..., None]), 0.0)
            factor = jnp.exp(highest - newest)
            totals = totals * factor + jnp.sum(weights, axis=-1)
            mixed = jnp.einsum(
                "hqk,khd->hqd",
                weights.astype(jnp.bfloat16),
                value_block,
                preferred_element_type=jnp.float32,
            )
            accum = accum * factor[..., None] + mixed
            return ((newest, totals, accum), None)

        carry, unused = lax.scan(visit, carry, (key_blocks, value_blocks, live_blocks))
        return carry

    return fold


def per_device(messages, node_anchor, anchor_count, norm_gain, w_query, w_key, w_value, w_out):
    center = lax.axis_index("ctx")
    pooled_terms = pool_local(messages, node_anchor, center)
    for_previous = pooled_terms[0]
    own_rows = pooled_terms[1]
    for_next = pooled_terms[2]
    from_next = from_behind(for_previous, "ctx", -1)
    from_previous = from_behind(for_next, "ctx", 1)
    sums = own_rows + from_next + from_previous
    pooled = sums.astype(jnp.bfloat16)
    whole = lax.all_gather(pooled, "head", axis=1, tiled=True).astype(jnp.float32)
    mean_square = jnp.mean(whole * whole, axis=1, keepdims=True)
    normed = (whole * lax.rsqrt(mean_square + EPS) * norm_gain).astype(jnp.bfloat16)
    channel_count = messages.shape[1]
    local_normed = lax.dynamic_slice_in_dim(
        normed, lax.axis_index("head") * channel_count, channel_count, 1
    )
    heads_local = w_query.shape[1] // HD
    queries = jnp.dot(normed, w_query, preferred_element_type=jnp.float32).astype(jnp.bfloat16)
    keys_local = jnp.dot(normed, w_key, preferred_element_type=jnp.float32).astype(jnp.bfloat16)
    values_local = jnp.dot(normed, w_value, preferred_element_type=jnp.float32).astype(jnp.bfloat16)
    queries = queries.reshape(ANCH_DEV, heads_local, HD)
    scale = HD ** (-0.5)
    initial = (
        jnp.full((heads_local, ANCH_DEV), NEG, jnp.float32),
        jnp.zeros((heads_local, ANCH_DEV), jnp.float32),
        jnp.zeros((heads_local, ANCH_DEV, HD), jnp.float32),
    )
    live_flags = (jnp.arange(ANCH_DEV, dtype=jnp.int32) < anchor_count[0]).astype(jnp.bfloat16)
    fold = make_fold(queries, ANCH_DEV, scale)
    highest, totals, accum = fold(
        initial,
        (
            lax.all_gather(keys_local, "ctx", axis=0, tiled=True),
            lax.all_gather(values_local, "ctx", axis=0, tiled=True),
            lax.all_gather(live_flags, "ctx", axis=0, tiled=True),
        ),
        jnp.int32(0),
    )
    attended = (
        (accum / totals[..., None])
        .transpose(1, 0, 2)
        .reshape(ANCH_DEV, heads_local * HD)
        .astype(jnp.bfloat16)
    )
    branch = jnp.dot(
        lax.all_gather(attended, "head", axis=1, tiled=True),
        w_out,
        preferred_element_type=jnp.float32,
    )
    return (local_normed.astype(jnp.float32) + branch).astype(jnp.bfloat16)


def solution(mesh):
    placed = (
        P("ctx", "head"),
        P("ctx"),
        P("ctx"),
        P(),
        P(None, "head"),
        P(None, "head"),
        P(None, "head"),
        P(None, "head"),
    )
    return jax.shard_map(
        per_device, mesh=mesh, in_specs=placed, out_specs=P("ctx", "head"), check_vma=False
    )
```

profile of v0, /device:TPU:0, one launch (start us, length us, event | category | flops | bytes accessed | tf_op | source)
XLA Modules:
  0.0 397.3 jit_solution(2291451969375648319)
XLA Ops:
  8.8 138.2 %while.26 = (s32[]{:T(128)}, f32[3,256,512]{2,1,0:T(8,128)}, s32[8,4]{0,1:T(4,128)S(1)}, s32[8,4,128]{2,1,0:T(4,128)S(1)}, bf16[8,4,128,512]{3,2,1,0:T(8,128)(2,1)}, /*index=5*/s32[]{:T(128)}, s32[]{:T(128)}, s32[]{:T(128)}) while((s32[]{:T(128)}, f32[3,256,512]{2,1,0:T(8,128)}, s32[8,4]{0,1:T(4,128)S(1)}, ...), condition=%wide.region_1.2_spmd.clone, body=%wide.region_0.1_spmd.clone.sunk | while | flops 134873088 | bytes 8919861 | solution.py:50
  12.8 1.9 fusion.71
  16.6 1.9 fusion.72
  20.2 1.9 fusion.73
  24.2 1.9 fusion.74
  30.1 1.9 fusion.71
  34.0 1.9 fusion.72
  37.5 1.9 fusion.73
  41.5 1.9 fusion.74
  47.4 1.9 fusion.71
  51.3 1.9 fusion.72
  54.9 1.9 fusion.73
  58.8 1.9 fusion.74
  64.7 1.9 fusion.71
  68.5 1.9 fusion.72
  72.1 1.9 fusion.73
  76.1 1.9 fusion.74
  82.0 1.9 fusion.71
  85.8 1.9 fusion.72
  89.4 1.9 fusion.73
  93.3 1.9 fusion.74
  99.3 1.9 fusion.71
  103.1 1.9 fusion.72
  106.7 1.9 fusion.73
  110.6 1.9 fusion.74
  116.5 1.9 fusion.71
  120.3 1.9 fusion.72
  123.9 1.9 fusion.73
  127.8 1.9 fusion.74
  133.7 1.9 fusion.71
  137.6 1.9 fusion.72
  141.2 1.9 fusion.73
  145.1 1.9 fusion.74
  148.3 5.6 %collective-permute-start = (f32[256,512]{1,0:T(8,128)S(1)}, f32[256,512]{1,0:T(8,128)S(1)}, u32[]{:S(2)}, u32[]{:S(2)}) collective-permute-start(f32[256,512]{1,0:T(8,128)S(1)} %get-tuple-element.188), channel_id=1, source_target_pairs={{0,30},{2,0},{4,2},{6,4},{8,6},{10,8},{12,10},{14,12},{16,14},{18,... | collective-permute-start | bytes 1572872 | tf_op jit(solution)/shard_map/ppermute | solution.py:18
  153.9 6.7 %collective-permute-done = f32[256,512]{1,0:T(8,128)S(1)} collective-permute-done((f32[256,512]{1,0:T(8,128)S(1)}, f32[256,512]{1,0:T(8,128)S(1)}, u32[]{:S(2)}, u32[]{:S(2)}) %collective-permute-start) | collective-permute-done | bytes 524320 | tf_op jit(solution)/shard_map/ppermute | solution.py:18
  160.6 4.6 %collective-permute-done.1 = f32[256,512]{1,0:T(8,128)S(1)} collective-permute-done((f32[256,512]{1,0:T(8,128)S(1)}, f32[256,512]{1,0:T(8,128)S(1)}, u32[]{:S(2)}, u32[]{:S(2)}) %collective-permute-start.1) | collective-permute-done | bytes 524320 | tf_op jit(solution)/shard_map/ppermute | solution.py:18
  166.3 7.2 %all_gather.15 = bf16[256,1024]{1,0:T(8,128)(2,1)S(1)} all-gather(bf16[256,512]{1,0:T(8,128)(2,1)S(1)} %fusion.38), channel_id=1, replica_groups=mesh['ctx'=16,'head'=2] {'head'}, dimensions={1}, use_global_device_ids=true | all-gather | bytes 786432 | tf_op jit(solution)/shard_map/all_gather | solution.py:102
  177.0 20.5 %all-gather = bf16[16,1,256]{2,1,0:T(2,128)(2,1)S(1)} all-gather(bf16[1,1,256]{2,1,0:T(2,128)(2,1)S(1)} %reshape.60), channel_id=1, replica_groups=mesh['ctx'=16,'head'=2] {'ctx'}, dimensions={0}, use_global_device_ids=true | all-gather | bytes 8704 | tf_op jit(solution)/shard_map/all_gather | solution.py:127
  197.5 1.7 convolution_convert_fusion.1
  199.3 26.6 %all-gather.4.cloned.1.call-done = bf16[4096,512]{1,0:T(8,128)(2,1)} async-done(((bf16[256,512]{1,0:T(8,128)(2,1)}), bf16[4096,512]{1,0:T(8,128)(2,1)}) %all-gather.4.cloned.1.call-update) | async-done | bytes 4194320 | tf_op jit(solution)/shard_map/all_gather | solution.py:125
  225.9 11.3 %reshape.63 = bf16[16,256,8,64]{3,2,1,0:T(8,128)(2,1)} reshape(bf16[4096,512]{1,0:T(8,128)(2,1)} %all-gather.4.cloned.1.call-done) | data formatting | bytes 8388608 | tf_op jit(solution)/shard_map/reshape | solution.py:60
  237.2 9.1 %copy.32 = bf16[16,256,8,64]{1,3,2,0:T(8,128)(2,1)} copy(bf16[16,256,8,64]{3,2,1,0:T(8,128)(2,1)} %reshape.63) | data formatting | bytes 8388608
  246.3 31.0 %all-gather.6.cloned.1.call-done = bf16[4096,512]{1,0:T(8,128)(2,1)} async-done(((bf16[256,512]{1,0:T(8,128)(2,1)}), bf16[4096,512]{1,0:T(8,128)(2,1)}) %all-gather.6.cloned.1.call-update) | async-done | bytes 4194320 | tf_op jit(solution)/shard_map/all_gather | solution.py:126
  277.3 11.2 %reshape.64 = bf16[16,256,8,64]{3,2,1,0:T(8,128)(2,1)} reshape(bf16[4096,512]{1,0:T(8,128)(2,1)} %all-gather.6.cloned.1.call-done) | data formatting | bytes 8388608 | tf_op jit(solution)/shard_map/reshape | solution.py:61
  288.5 9.1 %copy.33 = bf16[16,256,8,64]{1,3,2,0:T(8,128)(2,1)} copy(bf16[16,256,8,64]{3,2,1,0:T(8,128)(2,1)} %reshape.64) | data formatting | bytes 8388608
  297.6 80.2 %while.27 = (s32[]{:T(128)}, f32[8,256]{1,0:T(8,128)S(1)}, f32[8,256]{1,0:T(8,128)S(1)}, f32[8,256,64]{1,2,0:T(8,128)}, bf16[16,256]{1,0:T(8,128)(2,1)S(1)}, /*i...) while((s32[]{:T(128)}, f32[8,256]{1,0:T(8,128)S(1)}, ...), condition=%wide.region_6.7_spmd.clone, body=%wide.region_3.6_spmd.clone.sunk | while | flops 141437696 | bytes 12455341 | solution.py:86
  300.2 1.7 convolution_add_fusion.3
  305.2 1.7 convolution_add_fusion.3
  310.2 1.7 convolution_add_fusion.3
  315.2 1.7 convolution_add_fusion.3
  320.2 1.7 convolution_add_fusion.3
  325.3 1.7 convolution_add_fusion.3
  330.3 1.7 convolution_add_fusion.3
  335.3 1.7 convolution_add_fusion.3
  340.3 1.7 convolution_add_fusion.3
  345.3 1.7 convolution_add_fusion.3
  350.3 1.7 convolution_add_fusion.3
  355.3 1.7 convolution_add_fusion.3
  360.3 1.7 convolution_add_fusion.3
  365.3 1.7 convolution_add_fusion.3
  370.4 1.7 convolution_add_fusion.3
  375.4 1.7 convolution_add_fusion.3
  378.9 9.1 %all_gather.19 = bf16[256,1024]{0,1:T(8,128)(2,1)S(1)} all-gather(bf16[256,512]{0,1:T(8,128)(2,1)S(1)} %bitcast.88), channel_id=1, replica_groups=mesh['ctx'=16,'head'=2] {'head'}, dimensions={1}, use_global_device_ids=true | all-gather | bytes 786432 | tf_op jit(solution)/shard_map/all_gather | solution.py:138
  388.0 2.4 fusion.33
  (223 shorter events, 78.4 us)
Async XLA Ops:
  6.5 167.4 %copy-start = (bf16[1024,512]{1,0:T(8,128)(2,1)S(1)}, bf16[1024,512]{1,0:T(8,128)(2,1)}, u32[]{:S(2)}) copy-start(bf16[1024,512]{1,0:T(8,128)(2,1)} %param.17) | copy-start | bytes 3145732
  6.5 219.4 %all-gather.4.cloned.1.call-start = ((), (), s32[]{:S(2)}) async-start(), calls=%async_computation | async-start | bytes 4456448 | tf_op jit(solution)/shard_map/all_gather | solution.py:125
  148.3 25.4 %copy-start.5 = (f32[1024]{0:T(1024)S(1)}, f32[1024]{0:T(1024)}, u32[]{:S(2)}) copy-start(f32[1024]{0:T(1024)} %param.15) | copy-start | bytes 12292
  148.3 12.3 %collective-permute-start = (f32[256,512]{1,0:T(8,128)S(1)}, f32[256,512]{1,0:T(8,128)S(1)}, u32[]{:S(2)}, u32[]{:S(2)}) collective-permute-start(f32[256,512]{1,0:T(8,128)S(1)} %get-tuple-element.188), channel_id=1, source_target_pairs={{0,30},{2,0},{4,2},{6,4},{8,6},{10,8},{12,10},{14,12},{16,14},{18,... | collective-permute-start | bytes 1572872 | tf_op jit(solution)/shard_map/ppermute | solution.py:18
  153.9 11.3 %collective-permute-start.1 = (f32[256,512]{1,0:T(8,128)S(1)}, f32[256,512]{1,0:T(8,128)S(1)}, u32[]{:S(2)}, u32[]{:S(2)}) collective-permute-start(f32[256,512]{1,0:T(8,128)S(1)} %get-tuple-element.189), channel_id=1, source_target_pairs={{0,2},{2,4},{4,6},{6,8},{8,10},{10,12},{12,14},{14,16},{16,18},{18... | collective-permute-start | bytes 1572872 | tf_op jit(solution)/shard_map/ppermute | solution.py:18
  166.3 8.8 %copy-start.2 = (bf16[1024,512]{1,0:T(8,128)(2,1)S(1)}, bf16[1024,512]{1,0:T(8,128)(2,1)}, u32[]{:S(2)}) copy-start(bf16[1024,512]{1,0:T(8,128)(2,1)} %param.18) | copy-start | bytes 3145732
  173.9 23.6 %copy-start.1 = (bf16[256,1024]{1,0:T(8,128)(2,1)}, bf16[256,1024]{1,0:T(8,128)(2,1)S(1)}, u32[]{:S(2)}) copy-start(bf16[256,1024]{1,0:T(8,128)(2,1)S(1)} %fusion.36) | copy-start | bytes 1572868
  175.1 102.2 %all-gather.6.cloned.1.call-start = ((), (), s32[]{:S(2)}) async-start(), calls=%async_computation.1 | async-start | bytes 4456448 | tf_op jit(solution)/shard_map/all_gather | solution.py:126
  299.2 1.0 copy-start.3
  301.9 0.8 copy-start.4
  304.2 1.0 copy-start.3
  306.9 0.8 copy-start.4
  309.2 1.0 copy-start.3
  311.9 0.8 copy-start.4
  314.2 1.0 copy-start.3
  316.9 0.8 copy-start.4
  319.2 1.0 copy-start.3
  321.9 0.8 copy-start.4
  324.2 1.0 copy-start.3
  326.9 0.8 copy-start.4
  329.2 1.0 copy-start.3
  331.9 0.8 copy-start.4
  334.2 1.0 copy-start.3
  336.9 0.8 copy-start.4
  339.2 1.0 copy-start.3
  342.0 0.8 copy-start.4
  344.3 1.0 copy-start.3
  347.0 0.8 copy-start.4
  349.3 1.0 copy-start.3
  352.0 0.8 copy-start.4
  354.3 1.0 copy-start.3
  357.0 0.8 copy-start.4
  359.3 1.0 copy-start.3
  362.0 0.8 copy-start.4
  364.3 1.0 copy-start.3
  367.0 0.8 copy-start.4
  369.3 1.0 copy-start.3
  372.0 0.8 copy-start.4
  374.3 1.0 copy-start.3
  377.0 0.8 copy-start.4
Sparse Core Ops, SparseCore 0:
  175.2 50.6 all-gather.3
  228.1 49.1 all-gather.5
where the time goes:
time: 403 us; the launch traced here: 397 us
  other arithmetic  75.8 us (19%)
  waiting for transfers between devices  68.9 us (17%)
  matrix products  68.2 us (17%)
  local copies, waits for them, and re-layouts  67.3 us (17%)
  loops' own time  60.5 us (15%)
  blocking collectives  36.8 us (9%)
  between operations  14.2 us (4%)
  starting transfers between devices  5.62 us (1%)
    dynamic_update_slice x32, other arithmetic, add_block(): lax.dynamic_update_index_in_dim(running, current + partial_value[tile], w...  61.6 us
    another operation x1, loops' own time, pool_local(): lax.scan(add_block, initial, (slot_blocks, offset_blocks, message_blocks))  59.5 us
    all_gather x1, waiting for transfers between devices, per_device(): lax.all_gather(values_local, 'ctx', axis=0, tiled=True)  31 us
    all_gather x1, waiting for transfers between devices, per_device(): lax.all_gather(keys_local, 'ctx', axis=0, tiled=True)  26.6 us
    dot_general x16, matrix products, visit(): jnp.einsum('hqk,khd->hqd', weights.astype(jnp.bfloat16), value_block, pre...  26.5 us
    dot_general x16, matrix products, visit(): jnp.einsum('qhd,khd->hqk', queries, key_block, preferred_element_type=jnp...  23.6 us
    all_gather x1, blocking collectives, per_device(): lax.all_gather(live_flags, 'ctx', axis=0, tiled=True)  20.5 us
    while x80, local copies, waits for them, and re-layouts  18.3 us
  transfers between devices with their start and end apart: 4, of which 4 were waited for; matrix products, arithmetic and copies ran while one was open for 6% of the time, Pallas kernels for 0%

commit v1 on v0

--- a/solution.py
+++ b/solution.py
@@ -1,21 +1,398 @@
+import functools
 import math
 
 import jax
 import jax.numpy as jnp
 from jax import lax
+from jax.experimental import pallas as pl
+from jax.experimental.pallas import tpu as pltpu
 from jax.sharding import PartitionSpec as P
 
 HD = 64
 ANCH_DEV = 256
-
+LIVE_MAX = 192
+HALF = LIVE_MAX // 2
+PAD = 16
+QROWS = 2 * LIVE_MAX + PAD
+TILE = 128
 
 EPS = 1e-06
 NEG = -1e30
-
-
-def from_behind(x, axis, by):
-    peers = lax.axis_size(axis)
-    return lax.ppermute(x, axis, [(i, (i + by) % peers) for i in range(peers)])
+MARK = 2.0**100
+MARKED = 2.0**90
+RATE = HD**-0.5 * math.log2(math.e)
+
+ALL = ("ctx", "head")
+F32 = jnp.float32
+BF16 = jnp.bfloat16
+
+
+def params(mib=32):
+    return pltpu.CompilerParams(vmem_limit_bytes=mib * 2**20)
+
+
+def vmem(count):
+    return [pl.BlockSpec(memory_space=pltpu.VMEM)] * count
+
+
+def dot(a, b, contract=((1,), (0,))):
+    return lax.dot_general(a, b, (contract, ((), ())), preferred_element_type=F32)
+
+
+def row_of(slot):
+    block = slot // 16
+    return (block % 2) * HALF + (block // 2) * 16 + slot % 16
+
+
+def pool_kernel(tiles, anchors_smem, anchors_ref, messages_ref, before_ref, own_ref, after_ref, sums):
+    step = pl.program_id(0)
+    partitions = lax.axis_size("ctx")
+    center = lax.axis_index("ctx")
+
+    @pl.when(step == 0)
+    def _():
+        sums[...] = jnp.zeros_like(sums)
+
+    rows = lax.broadcasted_iota(jnp.int32, (LIVE_MAX, TILE), 0)
+    for tile in range(tiles):
+        index = step * tiles + tile
+        owner = anchors_smem[index * TILE] // ANCH_DEV
+        side = lax.rem(owner - center + 1 + partitions, partitions)
+        slot = row_of(anchors_ref[pl.ds(index, 1), :] % ANCH_DEV)
+        onehot = jnp.where(rows == slot, 1.0, 0.0).astype(BF16)
+        part = dot(onehot, messages_ref[tile * TILE : (tile + 1) * TILE, :])
+        sums[side] += part
+
+    @pl.when(step == pl.num_programs(0) - 1)
+    def _():
+        before_ref[...] = sums[0]
+        own_ref[...] = sums[1]
+        after_ref[...] = sums[2]
+
+
+def pool(messages, node_anchor):
+    nodes, channels = messages.shape
+    steps = 8
+    tiles = nodes // TILE // steps
+    shape = jax.ShapeDtypeStruct((LIVE_MAX, channels), F32)
+    whole = pl.BlockSpec((LIVE_MAX, channels), lambda i, a: (0, 0))
+    return pl.pallas_call(
+        functools.partial(pool_kernel, tiles),
+        grid_spec=pltpu.PrefetchScalarGridSpec(
+            num_scalar_prefetch=1,
+            grid=(steps,),
+            in_specs=[
+                pl.BlockSpec((nodes // TILE, TILE), lambda i, a: (0, 0)),
+                pl.BlockSpec((tiles * TILE, channels), lambda i, a: (i, 0)),
+            ],
+            out_specs=[whole] * 3,
+            scratch_shapes=[pltpu.VMEM((3, LIVE_MAX, channels), F32)],
+        ),
+        out_shape=[shape] * 3,
+        compiler_params=params(),
+        name="pool",
+    )(node_anchor, node_anchor.reshape(nodes // TILE, TILE), messages)
+
+
+def settle_kernel(count_ref, own_ref, before_ref, after_ref, keep_ref, send_ref):
+    core = lax.rem(lax.axis_index("ctx"), 2)
+    count = count_ref[0]
+
+    def half(which):
+        at = pl.ds(pl.multiple_of(which * HALF, 16), HALF)
+        total = own_ref[at, :] + before_ref[at, :] + after_ref[at, :]
+        row = lax.broadcasted_iota(jnp.int32, total.shape, 0)
+        slot = (2 * (row // 16) + which) * 16 + row % 16
+        return jnp.where(slot < count, total, MARK).astype(BF16)
+
+    keep_ref[...] = half(core)
+    send_ref[...] = half(1 - core)
+
+
+def settle(count, own, before, after):
+    channels = own.shape[1]
+    shape = jax.ShapeDtypeStruct((HALF, channels), BF16)
+    return pl.pallas_call(
+        settle_kernel,
+        in_specs=[pl.BlockSpec(memory_space=pltpu.SMEM)] + vmem(3),
+        out_specs=vmem(2),
+        out_shape=[shape] * 2,
+        compiler_params=params(),
+        name="settle",
+    )(count, own, before, after)
+
+
+def normalise(mine, other, gain_ref, x):
+    channels = mine.shape[1]
+    mine, other = mine.astype(F32), other.astype(F32)
+    dead = mine[:, :1] > MARKED
+    mine = jnp.where(dead, 0.0, mine)
+    other = jnp.where(dead, 0.0, other)
+    square = jnp.sum(mine * mine + other * other, axis=1, keepdims=True)
+    inverse = lax.rsqrt(square * (1.0 / (2 * channels)) + EPS)
+    mine = (mine * inverse * gain_ref[x]).astype(BF16)
+    other = (other * inverse * gain_ref[1 - x]).astype(BF16)
+    return mine, other, dead
+
+
+def project(mine, other, w_ref, x):
+    return (dot(mine, w_ref[x]) + dot(other, w_ref[1 - x])).astype(BF16)
+
+
+def query_kernel(own_ref, first_ref, second_ref, gain_ref, wq_ref, swap_ref, normed_ref):
+    core = lax.rem(lax.axis_index("ctx"), 2)
+    x = lax.axis_index("head")
+    other = jnp.where(core == 0, second_ref[:LIVE_MAX, :], first_ref[...])
+    mine, other, unused = normalise(own_ref[...], other, gain_ref, x)
+    swap_ref[:LIVE_MAX, :] = project(mine, other, wq_ref, x)
+    swap_ref[LIVE_MAX:, :] = mine[HALF:]
+    normed_ref[...] = mine[:HALF]
+
+
+def make_queries(own, first, second, gain, wq):
+    channels = own.shape[1]
+    return pl.pallas_call(
+        query_kernel,
+        in_specs=vmem(5),
+        out_specs=vmem(2),
+        out_shape=[
+            jax.ShapeDtypeStruct((LIVE_MAX + HALF, channels), BF16),
+            jax.ShapeDtypeStruct((HALF, channels), BF16),
+        ],
+        compiler_params=params(),
+        cost_estimate=pl.CostEstimate(flops=4 * 10**8, bytes_accessed=2 * 10**6, transcendentals=0),
+        name="queries",
+    )(own, first, second, gain, wq)
+
+
+def attend_kernel(first_call, *refs):
+    if first_call:
+        qm, qr, own_ref, first_ref, second_ref, gain_ref, wk_ref, wv_ref, out_ref = refs
+        state_ref = None
+    else:
+        qm, qr, own_ref, first_ref, second_ref, gain_ref, wk_ref, wv_ref, state_ref, out_ref = refs
+    core = lax.rem(lax.axis_index("ctx"), 2)
+    x = lax.axis_index("head")
+    channels = own_ref.shape[1]
+    heads = channels // HD
+    one, two = first_ref[...], second_ref[:LIVE_MAX, :]
+    mine = jnp.concatenate([own_ref[...], jnp.where(core == 0, one, two)], axis=0)
+    other = jnp.concatenate([jnp.where(core == 0, two, one), second_ref[LIVE_MAX:, :]], axis=0)
+    mine, other, dead = normalise(mine, other, gain_ref, x)
+    keys = project(mine, other, wk_ref, x)
+    values = project(mine, other, wv_ref, x)
+    shut = jnp.where(dead, NEG, 0.0).astype(BF16)
+
+    lane_k = lax.broadcasted_iota(jnp.int32, (keys.shape[0], 128), 1)
+    lane_q = lax.broadcasted_iota(jnp.int32, (QROWS, 128), 1)
+    lane_a = lax.broadcasted_iota(jnp.int32, (QROWS, 128), 1)
+    tops = jnp.full((QROWS, 128), 0.0, F32) if first_call else state_ref[:, channels:]
+    stats = tops
+    for pair in range(heads // 2):
+        at = slice(pair * 128, (pair + 1) * 128)
+        query = jnp.concatenate(
+            [qm[:HALF, at], qr[HALF:LIVE_MAX, at], jnp.zeros((PAD, 128), BF16), qr[:HALF, at], qm[HALF:LIVE_MAX, at]],
+            axis=0,
+        )
+        value = values[:, at]
+        mixed, fades = [], []
+        for side in range(2):
+            head = 2 * pair + side
+            inside_q = (lane_q // HD) == side
+            hot = jnp.where(lane_q == (1 - side) * HD, 1.0, 0.0).astype(BF16)
+            q = jnp.where(inside_q, query, hot)
+            k = jnp.where((lane_k // HD) == side, keys[:, at], shut)
+            scores = dot(q, k, ((1,), (1,)))
+            top = jnp.max(scores, axis=1, keepdims=True)
+            if not first_call:
+                old_top = stats[:, head : head + 1]
+                top = jnp.maximum(top, old_top)
+                fade = jnp.exp2((old_top - top) * RATE)
+                fades.append(fade)
+            weights = jnp.exp2((scores - top) * RATE)
+            total = jnp.sum(weights, axis=1, keepdims=True)
+            if not first_call:
+                total = total + stats[:, heads + head : heads + head + 1] * fade
+            stats = jnp.where(lane_a == head, top, stats)
+            stats = jnp.where(lane_a == heads + head, total, stats)
+            mixed.append(dot(weights.astype(BF16), value))
+        inside = lane_a < HD
+        merged = jnp.where(inside, mixed[0], mixed[1])
+        if not first_call:
+            merged = merged + state_ref[:, at] * jnp.where(inside, fades[0], fades[1])
+        out_ref[:, at] = merged
+    out_ref[:, channels:] = stats
+
+
+def attend(qm, qr, own, first, second, gain, wk, wv, state=None):
+    channels = own.shape[1]
+    args = [qm, qr, own, first, second, gain, wk, wv] + ([] if state is None else [state])
+    keys = 2 * LIVE_MAX
+    return pl.pallas_call(
+        functools.partial(attend_kernel, state is None),
+        in_specs=vmem(len(args)),
+        out_specs=pl.BlockSpec(memory_space=pltpu.VMEM),
+        out_shape=jax.ShapeDtypeStruct((QROWS, channels + 128), F32),
+        input_output_aliases={} if state is None else {len(args) - 1: 0},
+        compiler_params=params(),
+        cost_estimate=pl.CostEstimate(
+            flops=2 * 10**9, bytes_accessed=4 * 10**6, transcendentals=QROWS * keys * channels // HD
+        ),
+        name="attend",
+    )(*args)
+
+
+def combine_kernel(mine_ref, other_ref, out_ref):
+    rows, width = other_ref.shape
+    channels = width - 128
+    heads = channels // HD
+    lane = lax.broadcasted_iota(jnp.int32, (rows, 128), 1)
+
+    def theirs(at):
+        return jnp.concatenate([other_ref[PAD:, at], other_ref[:PAD, at]], axis=0)
+
+    mine_stats = mine_ref[:rows, channels:]
+    other_stats = theirs(slice(channels, width))
+    for pair in range(heads // 2):
+        at = slice(pair * 128, (pair + 1) * 128)
+        scale_mine, scale_other = [], []
+        for head in (2 * pair, 2 * pair + 1):
+            a, b = mine_stats[:, head : head + 1], other_stats[:, head : head + 1]
+            top = jnp.maximum(a, b)
+            a, b = jnp.exp2((a - top) * RATE), jnp.exp2((b - top) * RATE)
+            total = (
+                mine_stats[:, heads + head : heads + head + 1] * a
+                + other_stats[:, heads + head : heads + head + 1] * b
+            )
+            scale_mine.append(a / total)
+            scale_other.append(b / total)
+        inside = lane < HD
+        out_ref[:, at] = (
+            mine_ref[:rows, at] * jnp.where(inside, scale_mine[0], scale_mine[1])
+            + theirs(at) * jnp.where(inside, scale_other[0], scale_other[1])
+        ).astype(BF16)
+
+
+def combine(mine, other):
+    rows = other.shape[0]
+    return pl.pallas_call(
+        combine_kernel,
+        in_specs=vmem(2),
+        out_specs=pl.BlockSpec(memory_space=pltpu.VMEM),
+        out_shape=jax.ShapeDtypeStruct((rows, other.shape[1] - 128), BF16),
+        compiler_params=params(),
+        name="combine",
+    )(mine, other)
+
+
+def own_branch_kernel(attended_ref, w_ref, out_ref):
+    out_ref[...] = dot(attended_ref[...], w_ref[lax.axis_index("head")])
+
+
+def own_branch(attended, w_out):
+    return pl.pallas_call(
+        own_branch_kernel,
+        in_specs=vmem(2),
+        out_specs=pl.BlockSpec(memory_space=pltpu.VMEM),
+        out_shape=jax.ShapeDtypeStruct((attended.shape[0], w_out.shape[2]), F32),
+        compiler_params=params(),
+        cost_estimate=pl.CostEstimate(flops=10**8, bytes_accessed=10**6, transcendentals=0),
+        name="own_branch",
+    )(attended, w_out)
+
+
+def finish_kernel(branch_ref, attended_ref, w_ref, normed_ref, swapped_ref, out_ref):
+    core = lax.rem(lax.axis_index("ctx"), 2)
+    branch = branch_ref[...] + dot(attended_ref[...], w_ref[1 - lax.axis_index("head")])
+    near = (branch[:HALF] + normed_ref[...].astype(F32)).astype(BF16)
+    far = (branch[HALF:LIVE_MAX] + swapped_ref[LIVE_MAX:, :].astype(F32)).astype(BF16)
+    even = jnp.where(core == 0, near, far)
+    odd = jnp.where(core == 0, far, near)
+    for block in range(HALF // 16):
+        out_ref[32 * block : 32 * block + 16, :] = even[16 * block : 16 * block + 16]
+        out_ref[32 * block + 16 : 32 * block + 32, :] = odd[16 * block : 16 * block + 16]
+    rest = out_ref.shape[0] - LIVE_MAX
+    out_ref[LIVE_MAX:, :] = jnp.broadcast_to(branch[LIVE_MAX : LIVE_MAX + 1], (rest, branch.shape[1])).astype(BF16)
+
+
+def finish(branch, attended, w_out, normed, swapped):
+    return pl.pallas_call(
+        finish_kernel,
+        in_specs=vmem(5),
+        out_specs=pl.BlockSpec(memory_space=pltpu.VMEM),
+        out_shape=jax.ShapeDtypeStruct((ANCH_DEV, branch.shape[1]), BF16),
+        compiler_params=params(),
+        name="finish",
+    )(branch, attended, w_out, normed, swapped)
+
+
+def pairs(move):
+    found = []
+    for z in range(4):
+        for y in range(2):
+            for core in range(2):
+                for x in range(2):
+                    to_z, to_y, to_core, to_x = move(z, y, core, x)
+                    found.append((((z * 2 + y) * 2 + core) * 2 + x, ((to_z * 2 + to_y) * 2 + to_core) * 2 + to_x))
+    return found
+
+
+def send(array, move):
+    return lax.ppermute(array, ALL, pairs(move))
+
+
+def across_core(z, y, core, x):
+    return z, y, 1 - core, x
+
+
+def across_x(z, y, core, x):
+    return z, y, core, 1 - x
+
+
+def across_first(z, y, core, x):
+    return (z, 1 - y, core, x) if core == 0 else (z, y, core, 1 - x)
+
+
+def across_second(z, y, core, x):
+    return (z, 1 - y, core, x) if core == 1 else (z, y, core, 1 - x)
+
+
+def across_z(step):
+    return lambda z, y, core, x: (z ^ step, y, core, x)
+
+
+def halves(w):
+    return w.reshape(2, w.shape[0] // 2, w.shape[1])
+
+
+def block_plan(messages, node_anchor, anchor_count, norm_gain, w_query, w_key, w_value, w_out):
+    channels = messages.shape[1]
+    before, own, after = pool(messages, node_anchor)
+    from_next = shift(before, -1)
+    from_previous = shift(after, 1)
+    keep, away = settle(anchor_count, own, from_next, from_previous)
+    mine = jnp.concatenate([keep, send(away, across_core)], axis=0)
+    slices = [mine] + [send(mine, across_z(step)) for step in (1, 2, 3)]
+    gain = norm_gain.reshape(2, 1, channels)
+    wq, wk, wv, wo = halves(w_query), halves(w_key), halves(w_value), halves(w_out)
+    state = None
+    for index, rows in enumerate(slices):
+        first = send(rows, across_first)
+        second = send(jnp.concatenate([rows, first], axis=0), across_second)
+        if index == 0:
+            swap, normed = make_queries(rows, first, second, gain, wq)
+            swapped = send(swap, across_core)
+        state = attend(swap, swapped, rows, first, second, gain, wk, wv, state)
+    other = send(state[LIVE_MAX:], across_core)
+    attended = combine(state, other)
+    attended_other = send(attended, across_x)
+    branch = own_branch(attended, wo)
+    return finish(branch, attended_other, wo, normed, swapped)
+
+
+def shift(x, by):
+    peers = lax.axis_size("ctx")
+    return lax.ppermute(x, "ctx", [(i, (i + by) % peers) for i in range(peers)])
 
 
 def pool_local(messages, node_anchor, center):
@@ -89,14 +466,14 @@
     return fold
 
 
-def per_device(messages, node_anchor, anchor_count, norm_gain, w_query, w_key, w_value, w_out):
+def general_plan(messages, node_anchor, anchor_count, norm_gain, w_query, w_key, w_value, w_out):
     center = lax.axis_index("ctx")
     pooled_terms = pool_local(messages, node_anchor, center)
     for_previous = pooled_terms[0]
     own_rows = pooled_terms[1]
     for_next = pooled_terms[2]
-    from_next = from_behind(for_previous, "ctx", -1)
-    from_previous = from_behind(for_next, "ctx", 1)
+    from_next = shift(for_previous, -1)
+    from_previous = shift(for_next, 1)
     sums = own_rows + from_next + from_previous
     pooled = sums.astype(jnp.bfloat16)
     whole = lax.all_gather(pooled, "head", axis=1, tiled=True).astype(jnp.float32)
@@ -153,6 +530,6 @@
         P(None, "head"),
         P(None, "head"),
     )
-    return jax.shard_map(
-        per_device, mesh=mesh, in_specs=placed, out_specs=P("ctx", "head"), check_vma=False
-    )
+    sizes = (mesh.shape["ctx"], mesh.shape["head"])
+    plan = block_plan if sizes == (16, 2) else general_plan
+    return jax.shard_map(plan, mesh=mesh, in_specs=placed, out_specs=P("ctx", "head"), check_vma=False)

time: 403 us -> 101 us (0.25); the launches traced: 397 us -> 100 us
  other arithmetic: 75.8 us -> 0.11 us
  matrix products: 68.2 us -> 0 us
  local copies, waits for them, and re-layouts: 67.3 us -> 2.98 us
  loops' own time: 60.5 us -> 0 us
  Pallas kernels: 0 us -> 37.3 us
  blocking collectives: 36.8 us -> 0 us
  waiting for transfers between devices: 68.9 us -> 36.7 us
  starting transfers between devices: 5.62 us -> 22.3 us
  between operations: 14.2 us -> 0.86 us
    dot_general x44 -> x0, matrix products: 68.2 us -> none  [the longest x16 26.5 us: visit(): jnp.einsum('hqk,khd->hqd', weights.astype(jnp.bfloat16), value_block, pre...]
    dynamic_update_slice x32 -> x0, other arithmetic: 61.6 us -> none  [add_block(): lax.dynamic_update_index_in_dim(running, current + partial_value[tile], w...]
    another operation x2 -> x0, loops' own time: 60.5 us -> none  [the longest x1 59.5 us: pool_local(): lax.scan(add_block, initial, (slot_blocks, offset_blocks, message_blocks))]
    all_gather x2 -> x0, waiting for transfers between devices: 57.6 us -> none  [the longest x1 31 us: per_device(): lax.all_gather(values_local, 'ctx', axis=0, tiled=True)]
    pallas_call x0 -> x10, Pallas kernels: none -> 37.3 us  [the longest x4 30.5 us: attend(): pl.pallas_call(functools.partial(attend_kernel, state is None), in_specs=...]
    all_gather x3 -> x0, blocking collectives: 36.8 us -> none  [the longest x1 20.5 us: per_device(): lax.all_gather(live_flags, 'ctx', axis=0, tiled=True)]
    ppermute x2 -> x17, waiting for transfers between devices: 11.3 us -> 36.7 us  [the longest x15 27.5 us: send(): return lax.ppermute(array, ALL, pairs(move))]
    reshape x2 -> x0, local copies, waits for them, and re-layouts: 22.5 us -> none  [the longest x1 11.3 us: fold(): key_blocks = key_rows.reshape(shards, shard_rows, heads_local, HD)]
  transfers between devices with their start and end apart: 4 -> 17, of which waited for: 4 -> 10; matrix products, arithmetic and copies ran while one was open for 6% -> 0% of each run, Pallas kernels for 0% -> 22%
where the time goes in v1:
time: 101 us; the launch traced here: 100 us
  Pallas kernels  37.3 us (37%)
  waiting for transfers between devices  36.7 us (36%)
  starting transfers between devices  22.3 us (22%)
  local copies, waits for them, and re-layouts  2.98 us (3%)
    pallas_call x4, Pallas kernels, attend(): pl.pallas_call(functools.partial(attend_kernel, state is None), in_specs=...  30.5 us
    ppermute x15, waiting for transfers between devices, send(): return lax.ppermute(array, ALL, pairs(move))  27.5 us
    ppermute x15, starting transfers between devices, send(): return lax.ppermute(array, ALL, pairs(move))  16.8 us
    ppermute x2, waiting for transfers between devices, shift(): return lax.ppermute(x, 'ctx', [(i, (i + by) % peers) for i in range(peers)])  9.24 us
    ppermute x2, starting transfers between devices, shift(): return lax.ppermute(x, 'ctx', [(i, (i + by) % peers) for i in range(peers)])  5.5 us
    pallas_call x1, Pallas kernels, pool(): pl.pallas_call(functools.partial(pool_kernel, tiles), grid_spec=pltpu.Pre...  4.06 us
    unnamed x15, local copies, waits for them, and re-layouts  2.94 us
  transfers between devices with their start and end apart: 17, of which 10 were waited for; matrix products, arithmetic and copies ran while one was open for 0% of the time, Pallas kernels for 22%

profile of v1, /device:TPU:0, one launch (start us, length us, event | category | flops | bytes accessed | tf_op | source)
XLA Modules:
  0.0 100.3 jit_solution(7281966397749928373)
XLA Ops:
  0.0 0.0 copy-start
  0.0 2.2 %copy-done = bf16[4096,512]{1,0:T(8,128)(2,1)S(1)} copy-done((bf16[4096,512]{1,0:T(8,128)(2,1)S(1)}, bf16[4096,512]{1,0:T(8,128)(2,1)}, u32[]{:S(2)}) %copy-start) | copy-done | bytes 4194328
  2.2 0.0 copy-start.3
  2.2 0.7 copy-done.3
  2.9 0.0 copy-start.2
  2.9 0.0 copy-start.4
  2.9 4.1 %pool.1 = (f32[192,512]{1,0:T(8,128)S(1)}, f32[192,512]{1,0:T(8,128)S(1)}, f32[192,512]{1,0:T(8,128)S(1)}) custom-call(s32[4096]{0:T(1024)S(1)} %copy-done.3, s32[32,128]{1,0:T(8,128)S(1)} %bitcast.9, bf16[4096,512]{1,0:T(8,128)(2,1)S(1)} %copy-done), custom_call_target="tpu_custom_call" | custom-call | tf_op jit(solution)/shard_map/pool/pallas_call | solution.py:79
  7.0 0.0 copy-start.5
  7.0 0.0 copy-start.6
  7.0 5.5 %collective-permute-start = (f32[192,512]{1,0:T(8,128)S(1)}, f32[192,512]{1,0:T(8,128)S(1)}, u32[]{:S(2)}, u32[]{:S(2)}) collective-permute-start(f32[192,512]{1,0:T(8,128)S(1)} %get-tuple-element.13), channel_id=1, source_target_pairs={{0,30},{2,0},{4,2},{6,4},{8,6},{10,8},{12,10},{14,12},{16,14},{18,... | collective-permute-start | bytes 1179656 | tf_op jit(solution)/shard_map/ppermute | solution.py:395
  12.5 0.0 collective-permute-start.1
  13.2 4.6 %collective-permute-done.before_ref = f32[192,512]{1,0:T(8,128)S(1)} collective-permute-done((f32[192,512]{1,0:T(8,128)S(1)}, f32[192,512]{1,0:T(8,128)S(1)}, u32[]{:S(2)}, u32[]{:S(2)}) %collective-permute-start) | collective-permute-done | bytes 393248 | tf_op jit(solution)/shard_map/ppermute | solution.py:395
  17.8 4.6 %collective-permute-done.1.after_ref = f32[192,512]{1,0:T(8,128)S(1)} collective-permute-done((f32[192,512]{1,0:T(8,128)S(1)}, f32[192,512]{1,0:T(8,128)S(1)}, u32[]{:S(2)}, u32[]{:S(2)}) %collective-permute-start.1) | collective-permute-done | bytes 393248 | tf_op jit(solution)/shard_map/ppermute | solution.py:395
  22.4 0.1 settle.1
  22.5 0.1 collective-permute-start.2
  22.6 1.3 %collective-permute-done.2 = bf16[96,512]{1,0:T(8,128)(2,1)S(1)} collective-permute-done((bf16[96,512]{1,0:T(8,128)(2,1)S(1)}, bf16[96,512]{1,0:T(8,128)(2,1)S(1)}, u32[]{:S(2)}, u32[]{:S(2)}) %collective-permute-start.2) | collective-permute-done | bytes 98336 | tf_op jit(solution)/shard_map/ppermute | solution.py:341
  23.9 0.1 collective-permute-start.3
  23.9 5.7 %collective-permute-done.3.first_ref.refs_3_ = bf16[192,512]{1,0:T(8,128)(2,1)S(1)} collective-permute-done((bf16[192,512]{1,0:T(8,128)(2,1)S(1)}, bf16[192,512]{1,0:T(8,128)(2,1)S(1)}, u32[]{:S(2)}, u32[]{:S(2)}) %collective-permute-start.3) | collective-permute-done | bytes 196640 | tf_op jit(solution)/shard_map/ppermute | solution.py:341
  29.6 1.6 %collective-permute-start.4 = (bf16[384,512]{1,0:T(8,128)(2,1)S(1)}, bf16[384,512]{1,0:T(8,128)(2,1)S(1)}, u32[]{:S(2)}, u32[]{:S(2)}) collective-permute-start(bf16[384,512]{1,0:T(8,128)(2,1)S(1)} %pad_maximum_fusion), channel_id=1, source_target_pairs={{0,1},{1,0},{2,6},{3,7},{4,5},{5,4},{6,2},{7,3},{8,9},{9,8},{10,14... | collective-permute-start | bytes 1179656 | tf_op jit(solution)/shard_map/ppermute | solution.py:341
  31.2 0.0 collective-permute-start.12
  31.2 1.2 %collective-permute-start.9 = (bf16[192,512]{1,0:T(8,128)(2,1)S(1)}, bf16[192,512]{1,0:T(8,128)(2,1)S(1)}, u32[]{:S(2)}, u32[]{:S(2)}) collective-permute-start(bf16[192,512]{1,0:T(8,128)(2,1)S(1)} %constant_dynamic-update-slice_fusion.own_ref.refs_2_), channel_id=1, source_target_pairs={{0,16},{1,17},{2,18},{3,19},{4,20},{5,21},{6,22},{7,23},{8,24},{9,... | collective-permute-start | bytes 589832 | tf_op jit(solution)/shard_map/ppermute | solution.py:341
  32.4 3.1 %collective-permute-start.6 = (bf16[192,512]{1,0:T(8,128)(2,1)S(1)}, bf16[192,512]{1,0:T(8,128)(2,1)S(1)}, u32[]{:S(2)}, u32[]{:S(2)}) collective-permute-start(bf16[192,512]{1,0:T(8,128)(2,1)S(1)} %constant_dynamic-update-slice_fusion.own_ref.refs_2_), channel_id=1, source_target_pairs={{0,24},{1,25},{2,26},{3,27},{4,28},{5,29},{6,30},{7,31},{8,16},{9,... | collective-permute-start | bytes 589832 | tf_op jit(solution)/shard_map/ppermute | solution.py:341
  35.6 3.0 %collective-permute-done.12.refs_2_ = bf16[192,512]{1,0:T(8,128)(2,1)S(1)} collective-permute-done((bf16[192,512]{1,0:T(8,128)(2,1)S(1)}, bf16[192,512]{1,0:T(8,128)(2,1)S(1)}, u32[]{:S(2)}, u32[]{:S(2)}) %collective-permute-start.12) | collective-permute-done | bytes 196640 | tf_op jit(solution)/shard_map/ppermute | solution.py:341
  38.6 3.3 %collective-permute-start.13 = (bf16[192,512]{1,0:T(8,128)(2,1)S(1)}, bf16[192,512]{1,0:T(8,128)(2,1)S(1)}, u32[]{:S(2)}, u32[]{:S(2)}) collective-permute-start(bf16[192,512]{1,0:T(8,128)(2,1)S(1)} %collective-permute-done.12.refs_2_), channel_id=1, source_target_pairs={{0,4},{1,5},{2,3},{3,2},{4,0},{5,1},{6,7},{7,6},{8,12},{9,13},{10,... | collective-permute-start | bytes 589832 | tf_op jit(solution)/shard_map/ppermute | solution.py:341
  41.8 5.5 %collective-permute-done.9.refs_2_ = bf16[192,512]{1,0:T(8,128)(2,1)S(1)} collective-permute-done((bf16[192,512]{1,0:T(8,128)(2,1)S(1)}, bf16[192,512]{1,0:T(8,128)(2,1)S(1)}, u32[]{:S(2)}, u32[]{:S(2)}) %collective-permute-start.9) | collective-permute-done | bytes 196640 | tf_op jit(solution)/shard_map/ppermute | solution.py:341
  47.4 0.9 collective-permute-start.10
  48.3 0.0 collective-permute-done.6.refs_2_
  48.3 1.1 %collective-permute-start.7 = (bf16[192,512]{1,0:T(8,128)(2,1)S(1)}, bf16[192,512]{1,0:T(8,128)(2,1)S(1)}, u32[]{:S(2)}, u32[]{:S(2)}) collective-permute-start(bf16[192,512]{1,0:T(8,128)(2,1)S(1)} %collective-permute-done.6.refs_2_), channel_id=1, source_target_pairs={{0,4},{1,5},{2,3},{3,2},{4,0},{5,1},{6,7},{7,6},{8,12},{9,13},{10,... | collective-permute-start | bytes 589832 | tf_op jit(solution)/shard_map/ppermute | solution.py:341
  49.4 0.0 collective-permute-done.4.second_ref.refs_4_
  49.4 0.0 copy-done.2
  49.4 0.0 copy-done.4
  49.4 0.6 queries.1
  50.1 0.1 collective-permute-start.5
  50.1 0.0 collective-permute-done.13.refs_3_
  50.2 1.6 %collective-permute-start.14 = (bf16[384,512]{1,0:T(8,128)(2,1)S(1)}, bf16[384,512]{1,0:T(8,128)(2,1)S(1)}, u32[]{:S(2)}, u32[]{:S(2)}) collective-permute-start(bf16[384,512]{1,0:T(8,128)(2,1)S(1)} %pad_maximum_fusion.3), channel_id=1, source_target_pairs={{0,1},{1,0},{2,6},{3,7},{4,5},{5,4},{6,2},{7,3},{8,9},{9,8},{10,14... | collective-permute-start | bytes 1179656 | tf_op jit(solution)/shard_map/ppermute | solution.py:341
  51.7 1.3 %collective-permute-done.10.refs_3_ = bf16[192,512]{1,0:T(8,128)(2,1)S(1)} collective-permute-done((bf16[192,512]{1,0:T(8,128)(2,1)S(1)}, bf16[192,512]{1,0:T(8,128)(2,1)S(1)}, u32[]{:S(2)}, u32[]{:S(2)}) %collective-permute-start.10) | collective-permute-done | bytes 196640 | tf_op jit(solution)/shard_map/ppermute | solution.py:341
  53.1 1.6 %collective-permute-start.11 = (bf16[384,512]{1,0:T(8,128)(2,1)S(1)}, bf16[384,512]{1,0:T(8,128)(2,1)S(1)}, u32[]{:S(2)}, u32[]{:S(2)}) collective-permute-start(bf16[384,512]{1,0:T(8,128)(2,1)S(1)} %pad_maximum_fusion.2), channel_id=1, source_target_pairs={{0,1},{1,0},{2,6},{3,7},{4,5},{5,4},{6,2},{7,3},{8,9},{9,8},{10,14... | collective-permute-start | bytes 1179656 | tf_op jit(solution)/shard_map/ppermute | solution.py:341
  54.6 2.3 %collective-permute-done.7.refs_3_ = bf16[192,512]{1,0:T(8,128)(2,1)S(1)} collective-permute-done((bf16[192,512]{1,0:T(8,128)(2,1)S(1)}, bf16[192,512]{1,0:T(8,128)(2,1)S(1)}, u32[]{:S(2)}, u32[]{:S(2)}) %collective-permute-start.7) | collective-permute-done | bytes 196640 | tf_op jit(solution)/shard_map/ppermute | solution.py:341
  57.0 1.6 %collective-permute-start.8 = (bf16[384,512]{1,0:T(8,128)(2,1)S(1)}, bf16[384,512]{1,0:T(8,128)(2,1)S(1)}, u32[]{:S(2)}, u32[]{:S(2)}) collective-permute-start(bf16[384,512]{1,0:T(8,128)(2,1)S(1)} %pad_maximum_fusion.1), channel_id=1, source_target_pairs={{0,1},{1,0},{2,6},{3,7},{4,5},{5,4},{6,2},{7,3},{8,9},{9,8},{10,14... | collective-permute-start | bytes 1179656 | tf_op jit(solution)/shard_map/ppermute | solution.py:341
  58.5 0.0 collective-permute-done.5.refs_1_.swapped_ref
  58.5 0.0 copy-done.5
  58.5 0.0 copy-done.6
  58.5 3.4 %attend.4.refs_8_ = f32[400,640]{1,0:T(8,128)S(1)} custom-call(bf16[288,512]{1,0:T(8,128)(2,1)S(1)} %get-tuple-element.17.refs_0_, bf16[288,512]{1,0:T(8,128)(2,1)S(1)} %collective-permute-done.5.refs_1_.swapped_ref, bf16[192,512]{1,0:T(8,128)(2,1)S(1)} %constant_dynamic-update-slice_fusion.own_ref.refs_2_, ...), custom_call_target="tpu_custom_call" | custom-call | flops 2000000000 | bytes 4000000 | tf_op jit(solution)/shard_map/attend/pallas_call | solution.py:231
  62.0 0.0 collective-permute-done.14.refs_4_
  62.0 9.0 %attend.5.refs_8_ = f32[400,640]{1,0:T(8,128)S(1)} custom-call(bf16[288,512]{1,0:T(8,128)(2,1)S(1)} %get-tuple-element.17.refs_0_, bf16[288,512]{1,0:T(8,128)(2,1)S(1)} %collective-permute-done.5.refs_1_.swapped_ref, bf16[192,512]{1,0:T(8,128)(2,1)S(1)} %collective-permute-done.12.refs_2_, ...), custom_call_target="tpu_custom_call", output_to_operand_aliasing={{}: (8, {})} | custom-call | flops 2000000000 | bytes 4000000 | tf_op jit(solution)/shard_map/attend/pallas_call | solution.py:231
  71.0 0.0 collective-permute-done.11.refs_4_
  71.0 9.1 %attend.6.refs_8_ = f32[400,640]{1,0:T(8,128)S(1)} custom-call(bf16[288,512]{1,0:T(8,128)(2,1)S(1)} %get-tuple-element.17.refs_0_, bf16[288,512]{1,0:T(8,128)(2,1)S(1)} %collective-permute-done.5.refs_1_.swapped_ref, bf16[192,512]{1,0:T(8,128)(2,1)S(1)} %collective-permute-done.9.refs_2_, ...), custom_call_target="tpu_custom_call", output_to_operand_aliasing={{}: (8, {})} | custom-call | flops 2000000000 | bytes 4000000 | tf_op jit(solution)/shard_map/attend/pallas_call | solution.py:231
  80.1 0.0 copy-start.1
  80.2 0.0 collective-permute-done.8.refs_4_
  80.2 9.0 %attend.7.mine_ref = f32[400,640]{1,0:T(8,128)S(1)} custom-call(bf16[288,512]{1,0:T(8,128)(2,1)S(1)} %get-tuple-element.17.refs_0_, bf16[288,512]{1,0:T(8,128)(2,1)S(1)} %collective-permute-done.5.refs_1_.swapped_ref, bf16[192,512]{1,0:T(8,128)(2,1)S(1)} %collective-permute-done.6.refs_2_, ...), custom_call_target="tpu_custom_call", output_to_operand_aliasing={{}: (8, {})} | custom-call | flops 2000000000 | bytes 4000000 | tf_op jit(solution)/shard_map/attend/pallas_call | solution.py:231
  89.2 0.1 collective-permute-start.15
  89.3 1.9 %collective-permute-done.15.other_ref = f32[208,640]{1,0:T(8,128)S(1)} collective-permute-done((f32[208,640]{1,0:T(8,128)S(1)}, f32[208,640]{1,0:T(8,128)S(1)}, u32[]{:S(2)}, u32[]{:S(2)}) %collective-permute-start.15) | collective-permute-done | bytes 532512 | tf_op jit(solution)/shard_map/ppermute | solution.py:341
  91.2 0.7 combine.1.attended_ref
  91.9 0.6 collective-permute-start.16
  92.5 0.0 copy-done.1
  92.5 0.3 own_branch.1.branch_ref
  92.8 6.5 %collective-permute-done.16.attended_ref = bf16[208,512]{1,0:T(8,128)(2,1)S(1)} collective-permute-done((bf16[208,512]{1,0:T(8,128)(2,1)S(1)}, bf16[208,512]{1,0:T(8,128)(2,1)S(1)}, u32[]{:S(2)}, u32[]{:S(2)}) %collective-permute-start.16) | collective-permute-done | bytes 213024 | tf_op jit(solution)/shard_map/ppermute | solution.py:341
  99.3 1.0 %finish.1 = bf16[256,512]{1,0:T(8,128)(2,1)} custom-call(f32[208,512]{1,0:T(8,128)S(1)} %own_branch.1.branch_ref, bf16[208,512]{1,0:T(8,128)(2,1)S(1)} %collective-permute-done.16.attended_ref, bf16[2,512,512]{2,1,0:T(8,128)(2,1)S(1)} %bitcast.7, bf16[96,512]{1,0:T(8,128)(2,1)S(1)} %get-tuple-element.18.normed_ref, ...), custom_call_target="tpu_custom_call" | custom-call | tf_op jit(solution)/shard_map/finish/pallas_call | solution.py:319
  (7 shorter events, 0.2 us)
Async XLA Ops:
  0.0 2.2 %copy-start = (bf16[4096,512]{1,0:T(8,128)(2,1)S(1)}, bf16[4096,512]{1,0:T(8,128)(2,1)}, u32[]{:S(2)}) copy-start(bf16[4096,512]{1,0:T(8,128)(2,1)} %messages_ref.1) | copy-start | bytes 12582916
  2.2 0.7 copy-start.3
  2.9 46.5 %copy-start.2 = (bf16[1024,512]{1,0:T(8,128)(2,1)S(1)}, bf16[1024,512]{1,0:T(8,128)(2,1)}, u32[]{:S(2)}) copy-start(bf16[1024,512]{1,0:T(8,128)(2,1)} %param.12) | copy-start | bytes 3145732
  2.9 46.5 %copy-start.4 = (f32[1024]{0:T(1024)S(1)}, f32[1024]{0:T(1024)}, u32[]{:S(2)}) copy-start(f32[1024]{0:T(1024)} %param.11) | copy-start | bytes 12292
  7.0 51.6 %copy-start.5 = (bf16[1024,512]{1,0:T(8,128)(2,1)S(1)}, bf16[1024,512]{1,0:T(8,128)(2,1)}, u32[]{:S(2)}) copy-start(bf16[1024,512]{1,0:T(8,128)(2,1)} %param.13) | copy-start | bytes 3145732
  7.0 51.5 %copy-start.6 = (bf16[1024,512]{1,0:T(8,128)(2,1)S(1)}, bf16[1024,512]{1,0:T(8,128)(2,1)}, u32[]{:S(2)}) copy-start(bf16[1024,512]{1,0:T(8,128)(2,1)} %param.14) | copy-start | bytes 3145732
  7.0 10.8 %collective-permute-start = (f32[192,512]{1,0:T(8,128)S(1)}, f32[192,512]{1,0:T(8,128)S(1)}, u32[]{:S(2)}, u32[]{:S(2)}) collective-permute-start(f32[192,512]{1,0:T(8,128)S(1)} %get-tuple-element.13), channel_id=1, source_target_pairs={{0,30},{2,0},{4,2},{6,4},{8,6},{10,8},{12,10},{14,12},{16,14},{18,... | collective-permute-start | bytes 1179656 | tf_op jit(solution)/shard_map/ppermute | solution.py:395
  12.5 9.9 %collective-permute-start.1 = (f32[192,512]{1,0:T(8,128)S(1)}, f32[192,512]{1,0:T(8,128)S(1)}, u32[]{:S(2)}, u32[]{:S(2)}) collective-permute-start(f32[192,512]{1,0:T(8,128)S(1)} %get-tuple-element.14), channel_id=1, source_target_pairs={{0,2},{2,4},{4,6},{6,8},{8,10},{10,12},{12,14},{14,16},{16,18},{18... | collective-permute-start | bytes 1179656 | tf_op jit(solution)/shard_map/ppermute | solution.py:395
  22.5 1.4 %collective-permute-start.2 = (bf16[96,512]{1,0:T(8,128)(2,1)S(1)}, bf16[96,512]{1,0:T(8,128)(2,1)S(1)}, u32[]{:S(2)}, u32[]{:S(2)}) collective-permute-start(bf16[96,512]{1,0:T(8,128)(2,1)S(1)} %get-tuple-element.16), channel_id=1, source_target_pairs={{0,2},{1,3},{2,0},{3,1},{4,6},{5,7},{6,4},{7,5},{8,10},{9,11},{10,... | collective-permute-start | bytes 294920 | tf_op jit(solution)/shard_map/ppermute | solution.py:341
  23.9 5.7 %collective-permute-start.3 = (bf16[192,512]{1,0:T(8,128)(2,1)S(1)}, bf16[192,512]{1,0:T(8,128)(2,1)S(1)}, u32[]{:S(2)}, u32[]{:S(2)}) collective-permute-start(bf16[192,512]{1,0:T(8,128)(2,1)S(1)} %constant_dynamic-update-slice_fusion.own_ref.refs_2_), channel_id=1, source_target_pairs={{0,4},{1,5},{2,3},{3,2},{4,0},{5,1},{6,7},{7,6},{8,12},{9,13},{10,... | collective-permute-start | bytes 589832 | tf_op jit(solution)/shard_map/ppermute | solution.py:341
  29.6 19.8 %collective-permute-start.4 = (bf16[384,512]{1,0:T(8,128)(2,1)S(1)}, bf16[384,512]{1,0:T(8,128)(2,1)S(1)}, u32[]{:S(2)}, u32[]{:S(2)}) collective-permute-start(bf16[384,512]{1,0:T(8,128)(2,1)S(1)} %pad_maximum_fusion), channel_id=1, source_target_pairs={{0,1},{1,0},{2,6},{3,7},{4,5},{5,4},{6,2},{7,3},{8,9},{9,8},{10,14... | collective-permute-start | bytes 1179656 | tf_op jit(solution)/shard_map/ppermute | solution.py:341
  31.2 7.4 %collective-permute-start.12 = (bf16[192,512]{1,0:T(8,128)(2,1)S(1)}, bf16[192,512]{1,0:T(8,128)(2,1)S(1)}, u32[]{:S(2)}, u32[]{:S(2)}) collective-permute-start(bf16[192,512]{1,0:T(8,128)(2,1)S(1)} %constant_dynamic-update-slice_fusion.own_ref.refs_2_), channel_id=1, source_target_pairs={{0,8},{1,9},{2,10},{3,11},{4,12},{5,13},{6,14},{7,15},{8,0},{9,1},... | collective-permute-start | bytes 589832 | tf_op jit(solution)/shard_map/ppermute | solution.py:341
  31.2 16.2 %collective-permute-start.9 = (bf16[192,512]{1,0:T(8,128)(2,1)S(1)}, bf16[192,512]{1,0:T(8,128)(2,1)S(1)}, u32[]{:S(2)}, u32[]{:S(2)}) collective-permute-start(bf16[192,512]{1,0:T(8,128)(2,1)S(1)} %constant_dynamic-update-slice_fusion.own_ref.refs_2_), channel_id=1, source_target_pairs={{0,16},{1,17},{2,18},{3,19},{4,20},{5,21},{6,22},{7,23},{8,24},{9,... | collective-permute-start | bytes 589832 | tf_op jit(solution)/shard_map/ppermute | solution.py:341
  32.4 15.9 %collective-permute-start.6 = (bf16[192,512]{1,0:T(8,128)(2,1)S(1)}, bf16[192,512]{1,0:T(8,128)(2,1)S(1)}, u32[]{:S(2)}, u32[]{:S(2)}) collective-permute-start(bf16[192,512]{1,0:T(8,128)(2,1)S(1)} %constant_dynamic-update-slice_fusion.own_ref.refs_2_), channel_id=1, source_target_pairs={{0,24},{1,25},{2,26},{3,27},{4,28},{5,29},{6,30},{7,31},{8,16},{9,... | collective-permute-start | bytes 589832 | tf_op jit(solution)/shard_map/ppermute | solution.py:341
  38.6 11.6 %collective-permute-start.13 = (bf16[192,512]{1,0:T(8,128)(2,1)S(1)}, bf16[192,512]{1,0:T(8,128)(2,1)S(1)}, u32[]{:S(2)}, u32[]{:S(2)}) collective-permute-start(bf16[192,512]{1,0:T(8,128)(2,1)S(1)} %collective-permute-done.12.refs_2_), channel_id=1, source_target_pairs={{0,4},{1,5},{2,3},{3,2},{4,0},{5,1},{6,7},{7,6},{8,12},{9,13},{10,... | collective-permute-start | bytes 589832 | tf_op jit(solution)/shard_map/ppermute | solution.py:341
  47.4 5.7 %collective-permute-start.10 = (bf16[192,512]{1,0:T(8,128)(2,1)S(1)}, bf16[192,512]{1,0:T(8,128)(2,1)S(1)}, u32[]{:S(2)}, u32[]{:S(2)}) collective-permute-start(bf16[192,512]{1,0:T(8,128)(2,1)S(1)} %collective-permute-done.9.refs_2_), channel_id=1, source_target_pairs={{0,4},{1,5},{2,3},{3,2},{4,0},{5,1},{6,7},{7,6},{8,12},{9,13},{10,... | collective-permute-start | bytes 589832 | tf_op jit(solution)/shard_map/ppermute | solution.py:341
  48.3 8.6 %collective-permute-start.7 = (bf16[192,512]{1,0:T(8,128)(2,1)S(1)}, bf16[192,512]{1,0:T(8,128)(2,1)S(1)}, u32[]{:S(2)}, u32[]{:S(2)}) collective-permute-start(bf16[192,512]{1,0:T(8,128)(2,1)S(1)} %collective-permute-done.6.refs_2_), channel_id=1, source_target_pairs={{0,4},{1,5},{2,3},{3,2},{4,0},{5,1},{6,7},{7,6},{8,12},{9,13},{10,... | collective-permute-start | bytes 589832 | tf_op jit(solution)/shard_map/ppermute | solution.py:341
  50.1 8.5 %collective-permute-start.5 = (bf16[288,512]{1,0:T(8,128)(2,1)S(1)}, bf16[288,512]{1,0:T(8,128)(2,1)S(1)}, u32[]{:S(2)}, u32[]{:S(2)}) collective-permute-start(bf16[288,512]{1,0:T(8,128)(2,1)S(1)} %get-tuple-element.17.refs_0_), channel_id=1, source_target_pairs={{0,2},{1,3},{2,0},{3,1},{4,6},{5,7},{6,4},{7,5},{8,10},{9,11},{10,... | collective-permute-start | bytes 884744 | tf_op jit(solution)/shard_map/ppermute | solution.py:341
  50.2 11.8 %collective-permute-start.14 = (bf16[384,512]{1,0:T(8,128)(2,1)S(1)}, bf16[384,512]{1,0:T(8,128)(2,1)S(1)}, u32[]{:S(2)}, u32[]{:S(2)}) collective-permute-start(bf16[384,512]{1,0:T(8,128)(2,1)S(1)} %pad_maximum_fusion.3), channel_id=1, source_target_pairs={{0,1},{1,0},{2,6},{3,7},{4,5},{5,4},{6,2},{7,3},{8,9},{9,8},{10,14... | collective-permute-start | bytes 1179656 | tf_op jit(solution)/shard_map/ppermute | solution.py:341
  53.1 17.9 %collective-permute-start.11 = (bf16[384,512]{1,0:T(8,128)(2,1)S(1)}, bf16[384,512]{1,0:T(8,128)(2,1)S(1)}, u32[]{:S(2)}, u32[]{:S(2)}) collective-permute-start(bf16[384,512]{1,0:T(8,128)(2,1)S(1)} %pad_maximum_fusion.2), channel_id=1, source_target_pairs={{0,1},{1,0},{2,6},{3,7},{4,5},{5,4},{6,2},{7,3},{8,9},{9,8},{10,14... | collective-permute-start | bytes 1179656 | tf_op jit(solution)/shard_map/ppermute | solution.py:341
  57.0 23.2 %collective-permute-start.8 = (bf16[384,512]{1,0:T(8,128)(2,1)S(1)}, bf16[384,512]{1,0:T(8,128)(2,1)S(1)}, u32[]{:S(2)}, u32[]{:S(2)}) collective-permute-start(bf16[384,512]{1,0:T(8,128)(2,1)S(1)} %pad_maximum_fusion.1), channel_id=1, source_target_pairs={{0,1},{1,0},{2,6},{3,7},{4,5},{5,4},{6,2},{7,3},{8,9},{9,8},{10,14... | collective-permute-start | bytes 1179656 | tf_op jit(solution)/shard_map/ppermute | solution.py:341
  80.1 12.4 %copy-start.1 = (bf16[1024,512]{1,0:T(8,128)(2,1)S(1)}, bf16[1024,512]{1,0:T(8,128)(2,1)}, u32[]{:S(2)}) copy-start(bf16[1024,512]{1,0:T(8,128)(2,1)} %param.15) | copy-start | bytes 3145732
  89.2 2.0 %collective-permute-start.15 = (f32[208,640]{1,0:T(8,128)S(1)}, f32[208,640]{1,0:T(8,128)S(1)}, u32[]{:S(2)}, u32[]{:S(2)}) collective-permute-start(f32[208,640]{1,0:T(8,128)S(1)} %slice.4), channel_id=1, source_target_pairs={{0,2},{1,3},{2,0},{3,1},{4,6},{5,7},{6,4},{7,5},{8,10},{9,11},{10,... | collective-permute-start | bytes 1597448 | tf_op jit(solution)/shard_map/ppermute | solution.py:341
  91.9 7.4 %collective-permute-start.16 = (bf16[208,512]{1,0:T(8,128)(2,1)S(1)}, bf16[208,512]{1,0:T(8,128)(2,1)S(1)}, u32[]{:S(2)}, u32[]{:S(2)}) collective-permute-start(bf16[208,512]{1,0:T(8,128)(2,1)S(1)} %combine.1.attended_ref), channel_id=1, source_target_pairs={{0,1},{1,0},{2,3},{3,2},{4,5},{5,4},{6,7},{7,6},{8,9},{9,8},{10,11... | collective-permute-start | bytes 638984 | tf_op jit(solution)/shard_map/ppermute | solution.py:341

commit v2 on v1

--- a/solution.py
+++ b/solution.py
@@ -13,7 +13,8 @@
 LIVE_MAX = 192
 HALF = LIVE_MAX // 2
 PAD = 16
-QROWS = 2 * LIVE_MAX + PAD
+QROWS = 2 * LIVE_MAX
+SPILL = 128 - HALF
 TILE = 128
 
 EPS = 1e-06
@@ -180,48 +181,48 @@
     other = jnp.concatenate([jnp.where(core == 0, two, one), second_ref[LIVE_MAX:, :]], axis=0)
     mine, other, dead = normalise(mine, other, gain_ref, x)
     keys = project(mine, other, wk_ref, x)
-    values = project(mine, other, wv_ref, x)
+    values = project(mine, other, wv_ref, x).T
     shut = jnp.where(dead, NEG, 0.0).astype(BF16)
+
+    live = jnp.sum(jnp.where(dead, 0.0, 1.0), axis=0, keepdims=True)
+    value_sum = jnp.sum(values.astype(F32), axis=1, keepdims=True)
+    if not first_call:
+        live = live + state_ref[channels + 2 * heads : channels + 2 * heads + 1, QROWS : QROWS + 1]
+        value_sum = value_sum + state_ref[:channels, QROWS : QROWS + 1]
+    out_ref[:channels, QROWS:] = jnp.broadcast_to(value_sum, (channels, 128))
+    out_ref[channels:, QROWS:] = jnp.broadcast_to(live, (out_ref.shape[0] - channels, 128))
 
     lane_k = lax.broadcasted_iota(jnp.int32, (keys.shape[0], 128), 1)
     lane_q = lax.broadcasted_iota(jnp.int32, (QROWS, 128), 1)
-    lane_a = lax.broadcasted_iota(jnp.int32, (QROWS, 128), 1)
-    tops = jnp.full((QROWS, 128), 0.0, F32) if first_call else state_ref[:, channels:]
-    stats = tops
     for pair in range(heads // 2):
         at = slice(pair * 128, (pair + 1) * 128)
         query = jnp.concatenate(
-            [qm[:HALF, at], qr[HALF:LIVE_MAX, at], jnp.zeros((PAD, 128), BF16), qr[:HALF, at], qm[HALF:LIVE_MAX, at]],
+            [qm[:HALF, at], qr[HALF:LIVE_MAX, at], qm[HALF + SPILL : LIVE_MAX, at], qr[:HALF, at], qm[HALF : HALF + SPILL, at]],
             axis=0,
         )
-        value = values[:, at]
-        mixed, fades = [], []
         for side in range(2):
             head = 2 * pair + side
-            inside_q = (lane_q // HD) == side
             hot = jnp.where(lane_q == (1 - side) * HD, 1.0, 0.0).astype(BF16)
-            q = jnp.where(inside_q, query, hot)
+            q = jnp.where((lane_q // HD) == side, query, hot)
             k = jnp.where((lane_k // HD) == side, keys[:, at], shut)
-            scores = dot(q, k, ((1,), (1,)))
-            top = jnp.max(scores, axis=1, keepdims=True)
+            scores = dot(k, q, ((1,), (1,)))
+            top = jnp.max(scores, axis=0, keepdims=True)
+            at_top = slice(channels + head, channels + head + 1)
+            at_total = slice(channels + heads + head, channels + heads + head + 1)
             if not first_call:
-                old_top = stats[:, head : head + 1]
+                old_top = state_ref[at_top, :QROWS]
                 top = jnp.maximum(top, old_top)
                 fade = jnp.exp2((old_top - top) * RATE)
-                fades.append(fade)
             weights = jnp.exp2((scores - top) * RATE)
-            total = jnp.sum(weights, axis=1, keepdims=True)
+            total = jnp.sum(weights, axis=0, keepdims=True)
+            at_head = slice(head * HD, (head + 1) * HD)
+            mixed = dot(values[at_head], weights.astype(BF16))
             if not first_call:
-                total = total + stats[:, heads + head : heads + head + 1] * fade
-            stats = jnp.where(lane_a == head, top, stats)
-            stats = jnp.where(lane_a == heads + head, total, stats)
-            mixed.append(dot(weights.astype(BF16), value))
-        inside = lane_a < HD
-        merged = jnp.where(inside, mixed[0], mixed[1])
-        if not first_call:
-            merged = merged + state_ref[:, at] * jnp.where(inside, fades[0], fades[1])
-        out_ref[:, at] = merged
-    out_ref[:, channels:] = stats
+                total = total + state_ref[at_total, :QROWS] * fade
+                mixed = mixed + state_ref[at_head, :QROWS] * fade
+            out_ref[at_head, :QROWS] = mixed
+            out_ref[at_top, :QROWS] = top
+            out_ref[at_total, :QROWS] = total
 
 
 def attend(qm, qr, own, first, second, gain, wk, wv, state=None):
@@ -232,7 +233,7 @@
         functools.partial(attend_kernel, state is None),
         in_specs=vmem(len(args)),
         out_specs=pl.BlockSpec(memory_space=pltpu.VMEM),
-        out_shape=jax.ShapeDtypeStruct((QROWS, channels + 128), F32),
+        out_shape=jax.ShapeDtypeStruct((channels + 2 * (channels // HD) + 8, QROWS + 128), F32),
         input_output_aliases={} if state is None else {len(args) - 1: 0},
         compiler_params=params(),
         cost_estimate=pl.CostEstimate(
@@ -243,43 +244,38 @@
 
 
 def combine_kernel(mine_ref, other_ref, out_ref):
-    rows, width = other_ref.shape
-    channels = width - 128
+    channels = out_ref.shape[1]
     heads = channels // HD
-    lane = lax.broadcasted_iota(jnp.int32, (rows, 128), 1)
+    width = 256
+    lane = lax.broadcasted_iota(jnp.int32, (HD, width), 1)
 
     def theirs(at):
-        return jnp.concatenate([other_ref[PAD:, at], other_ref[:PAD, at]], axis=0)
-
-    mine_stats = mine_ref[:rows, channels:]
-    other_stats = theirs(slice(channels, width))
-    for pair in range(heads // 2):
-        at = slice(pair * 128, (pair + 1) * 128)
-        scale_mine, scale_other = [], []
-        for head in (2 * pair, 2 * pair + 1):
-            a, b = mine_stats[:, head : head + 1], other_stats[:, head : head + 1]
-            top = jnp.maximum(a, b)
-            a, b = jnp.exp2((a - top) * RATE), jnp.exp2((b - top) * RATE)
-            total = (
-                mine_stats[:, heads + head : heads + head + 1] * a
-                + other_stats[:, heads + head : heads + head + 1] * b
-            )
-            scale_mine.append(a / total)
-            scale_other.append(b / total)
-        inside = lane < HD
-        out_ref[:, at] = (
-            mine_ref[:rows, at] * jnp.where(inside, scale_mine[0], scale_mine[1])
-            + theirs(at) * jnp.where(inside, scale_other[0], scale_other[1])
-        ).astype(BF16)
+        middle = other_ref[at, :128]
+        return jnp.concatenate([other_ref[at, 128:256], middle[:, 64:], middle[:, :64]], axis=1)
+
+    at = slice(channels + 2 * heads, channels + 2 * heads + 1)
+    live = mine_ref[at, QROWS : QROWS + 1] + other_ref[at, 256:257]
+    for head in range(heads):
+        at_top = slice(channels + head, channels + head + 1)
+        at_total = slice(channels + heads + head, channels + heads + head + 1)
+        at = slice(head * HD, (head + 1) * HD)
+        a, b = mine_ref[at_top, :width], theirs(at_top)
+        top = jnp.maximum(a, b)
+        a, b = jnp.exp2((a - top) * RATE), jnp.exp2((b - top) * RATE)
+        total = mine_ref[at_total, :width] * a + theirs(at_total) * b
+        mixed = (mine_ref[at, :width] * a + theirs(at) * b) / total
+        mean = (mine_ref[at, QROWS : QROWS + 1] + other_ref[at, 256:257]) / live
+        mixed = jnp.where(lane < LIVE_MAX, mixed, mean)
+        out_ref[:, at] = mixed.T[: LIVE_MAX + PAD].astype(BF16)
 
 
 def combine(mine, other):
-    rows = other.shape[0]
+    channels = other.shape[0] // (HD + 2) * HD
     return pl.pallas_call(
         combine_kernel,
         in_specs=vmem(2),
         out_specs=pl.BlockSpec(memory_space=pltpu.VMEM),
-        out_shape=jax.ShapeDtypeStruct((rows, other.shape[1] - 128), BF16),
+        out_shape=jax.ShapeDtypeStruct((LIVE_MAX + PAD, channels), BF16),
         compiler_params=params(),
         name="combine",
     )(mine, other)
@@ -383,7 +379,7 @@
             swap, normed = make_queries(rows, first, second, gain, wq)
             swapped = send(swap, across_core)
         state = attend(swap, swapped, rows, first, second, gain, wk, wv, state)
-    other = send(state[LIVE_MAX:], across_core)
+    other = send(state[:, 128:], across_core)
     attended = combine(state, other)
     attended_other = send(attended, across_x)
     branch = own_branch(attended, wo)

time: 101 us -> 89.4 us (0.89)
  Pallas kernels: 37.3 us -> 25.8 us
    pallas_call x4, Pallas kernels: 30.5 us -> 18.4 us  [attend(): pl.pallas_call(functools.partial(attend_kernel, state is None), in_specs=...]
  transfers between devices with their start and end apart: 17 -> 17, of which waited for: 10 -> 10; matrix products, arithmetic and copies ran while one was open for 0% -> 0% of each run, Pallas kernels for 22% -> 16%
where the time goes in v2:
time: 89.4 us; the launch traced here: 89.2 us
  waiting for transfers between devices  37.1 us (41%)
  Pallas kernels  25.8 us (29%)
  starting transfers between devices  22.3 us (25%)
  local copies, waits for them, and re-layouts  3.02 us (3%)
    ppermute x15, waiting for transfers between devices, send(): return lax.ppermute(array, ALL, pairs(move))  27.9 us
    pallas_call x4, Pallas kernels, attend(): pl.pallas_call(functools.partial(attend_kernel, state is None), in_specs=...  18.4 us
    ppermute x15, starting transfers between devices, send(): return lax.ppermute(array, ALL, pairs(move))  16.8 us
    ppermute x2, waiting for transfers between devices, shift(): return lax.ppermute(x, 'ctx', [(i, (i + by) % peers) for i in range(peers)])  9.24 us
    ppermute x2, starting transfers between devices, shift(): return lax.ppermute(x, 'ctx', [(i, (i + by) % peers) for i in range(peers)])  5.5 us
    pallas_call x1, Pallas kernels, pool(): pl.pallas_call(functools.partial(pool_kernel, tiles), grid_spec=pltpu.Pre...  4.06 us
    unnamed x15, local copies, waits for them, and re-layouts  2.94 us
  transfers between devices with their start and end apart: 17, of which 10 were waited for; matrix products, arithmetic and copies ran while one was open for 0% of the time, Pallas kernels for 16%

profile of v2, /device:TPU:0, one launch (start us, length us, event | category | flops | bytes accessed | tf_op | source)
XLA Modules:
  0.0 89.2 jit_solution(5756311582789515475)
XLA Ops:
  0.0 0.0 copy-start
  0.0 2.2 %copy-done = bf16[4096,512]{1,0:T(8,128)(2,1)S(1)} copy-done((bf16[4096,512]{1,0:T(8,128)(2,1)S(1)}, bf16[4096,512]{1,0:T(8,128)(2,1)}, u32[]{:S(2)}) %copy-start) | copy-done | bytes 4194328
  2.2 0.0 copy-start.3
  2.2 0.7 copy-done.3
  2.9 4.1 %pool.1 = (f32[192,512]{1,0:T(8,128)S(1)}, f32[192,512]{1,0:T(8,128)S(1)}, f32[192,512]{1,0:T(8,128)S(1)}) custom-call(s32[4096]{0:T(1024)S(1)} %copy-done.3, s32[32,128]{1,0:T(8,128)S(1)} %bitcast.9, bf16[4096,512]{1,0:T(8,128)(2,1)S(1)} %copy-done), custom_call_target="tpu_custom_call" | custom-call | tf_op jit(solution)/shard_map/pool/pallas_call | solution.py:80
  7.0 5.5 %collective-permute-start = (f32[192,512]{1,0:T(8,128)S(1)}, f32[192,512]{1,0:T(8,128)S(1)}, u32[]{:S(2)}, u32[]{:S(2)}) collective-permute-start(f32[192,512]{1,0:T(8,128)S(1)} %get-tuple-element.13), channel_id=1, source_target_pairs={{0,30},{2,0},{4,2},{6,4},{8,6},{10,8},{12,10},{14,12},{16,14},{18,... | collective-permute-start | bytes 1179656 | tf_op jit(solution)/shard_map/ppermute | solution.py:391
  12.5 0.0 collective-permute-start.1
  13.1 4.6 %collective-permute-done.before_ref = f32[192,512]{1,0:T(8,128)S(1)} collective-permute-done((f32[192,512]{1,0:T(8,128)S(1)}, f32[192,512]{1,0:T(8,128)S(1)}, u32[]{:S(2)}, u32[]{:S(2)}) %collective-permute-start) | collective-permute-done | bytes 393248 | tf_op jit(solution)/shard_map/ppermute | solution.py:391
  17.8 4.6 %collective-permute-done.1.after_ref = f32[192,512]{1,0:T(8,128)S(1)} collective-permute-done((f32[192,512]{1,0:T(8,128)S(1)}, f32[192,512]{1,0:T(8,128)S(1)}, u32[]{:S(2)}, u32[]{:S(2)}) %collective-permute-start.1) | collective-permute-done | bytes 393248 | tf_op jit(solution)/shard_map/ppermute | solution.py:391
  22.4 0.0 copy-start.2
  22.4 0.0 copy-start.4
  22.4 0.1 settle.1
  22.5 0.1 collective-permute-start.2
  22.6 1.3 %collective-permute-done.2 = bf16[96,512]{1,0:T(8,128)(2,1)S(1)} collective-permute-done((bf16[96,512]{1,0:T(8,128)(2,1)S(1)}, bf16[96,512]{1,0:T(8,128)(2,1)S(1)}, u32[]{:S(2)}, u32[]{:S(2)}) %collective-permute-start.2) | collective-permute-done | bytes 98336 | tf_op jit(solution)/shard_map/ppermute | solution.py:337
  23.8 0.1 collective-permute-start.3
  23.9 5.7 %collective-permute-done.3.first_ref.refs_3_ = bf16[192,512]{1,0:T(8,128)(2,1)S(1)} collective-permute-done((bf16[192,512]{1,0:T(8,128)(2,1)S(1)}, bf16[192,512]{1,0:T(8,128)(2,1)S(1)}, u32[]{:S(2)}, u32[]{:S(2)}) %collective-permute-start.3) | collective-permute-done | bytes 196640 | tf_op jit(solution)/shard_map/ppermute | solution.py:337
  29.6 1.6 %collective-permute-start.4 = (bf16[384,512]{1,0:T(8,128)(2,1)S(1)}, bf16[384,512]{1,0:T(8,128)(2,1)S(1)}, u32[]{:S(2)}, u32[]{:S(2)}) collective-permute-start(bf16[384,512]{1,0:T(8,128)(2,1)S(1)} %pad_maximum_fusion), channel_id=1, source_target_pairs={{0,1},{1,0},{2,6},{3,7},{4,5},{5,4},{6,2},{7,3},{8,9},{9,8},{10,14... | collective-permute-start | bytes 1179656 | tf_op jit(solution)/shard_map/ppermute | solution.py:337
  31.2 0.0 collective-permute-start.12
  31.2 1.2 %collective-permute-start.9 = (bf16[192,512]{1,0:T(8,128)(2,1)S(1)}, bf16[192,512]{1,0:T(8,128)(2,1)S(1)}, u32[]{:S(2)}, u32[]{:S(2)}) collective-permute-start(bf16[192,512]{1,0:T(8,128)(2,1)S(1)} %constant_dynamic-update-slice_fusion.own_ref.refs_2_), channel_id=1, source_target_pairs={{0,16},{1,17},{2,18},{3,19},{4,20},{5,21},{6,22},{7,23},{8,24},{9,... | collective-permute-start | bytes 589832 | tf_op jit(solution)/shard_map/ppermute | solution.py:337
  32.4 3.1 %collective-permute-start.6 = (bf16[192,512]{1,0:T(8,128)(2,1)S(1)}, bf16[192,512]{1,0:T(8,128)(2,1)S(1)}, u32[]{:S(2)}, u32[]{:S(2)}) collective-permute-start(bf16[192,512]{1,0:T(8,128)(2,1)S(1)} %constant_dynamic-update-slice_fusion.own_ref.refs_2_), channel_id=1, source_target_pairs={{0,24},{1,25},{2,26},{3,27},{4,28},{5,29},{6,30},{7,31},{8,16},{9,... | collective-permute-start | bytes 589832 | tf_op jit(solution)/shard_map/ppermute | solution.py:337
  35.5 3.0 %collective-permute-done.12.refs_2_ = bf16[192,512]{1,0:T(8,128)(2,1)S(1)} collective-permute-done((bf16[192,512]{1,0:T(8,128)(2,1)S(1)}, bf16[192,512]{1,0:T(8,128)(2,1)S(1)}, u32[]{:S(2)}, u32[]{:S(2)}) %collective-permute-start.12) | collective-permute-done | bytes 196640 | tf_op jit(solution)/shard_map/ppermute | solution.py:337
  38.5 3.3 %collective-permute-start.13 = (bf16[192,512]{1,0:T(8,128)(2,1)S(1)}, bf16[192,512]{1,0:T(8,128)(2,1)S(1)}, u32[]{:S(2)}, u32[]{:S(2)}) collective-permute-start(bf16[192,512]{1,0:T(8,128)(2,1)S(1)} %collective-permute-done.12.refs_2_), channel_id=1, source_target_pairs={{0,4},{1,5},{2,3},{3,2},{4,0},{5,1},{6,7},{7,6},{8,12},{9,13},{10,... | collective-permute-start | bytes 589832 | tf_op jit(solution)/shard_map/ppermute | solution.py:337
  41.8 5.5 %collective-permute-done.9.refs_2_ = bf16[192,512]{1,0:T(8,128)(2,1)S(1)} collective-permute-done((bf16[192,512]{1,0:T(8,128)(2,1)S(1)}, bf16[192,512]{1,0:T(8,128)(2,1)S(1)}, u32[]{:S(2)}, u32[]{:S(2)}) %collective-permute-start.9) | collective-permute-done | bytes 196640 | tf_op jit(solution)/shard_map/ppermute | solution.py:337
  47.4 0.9 %collective-permute-start.10 = (bf16[192,512]{1,0:T(8,128)(2,1)S(1)}, bf16[192,512]{1,0:T(8,128)(2,1)S(1)}, u32[]{:S(2)}, u32[]{:S(2)}) collective-permute-start(bf16[192,512]{1,0:T(8,128)(2,1)S(1)} %collective-permute-done.9.refs_2_), channel_id=1, source_target_pairs={{0,4},{1,5},{2,3},{3,2},{4,0},{5,1},{6,7},{7,6},{8,12},{9,13},{10,... | collective-permute-start | bytes 589832 | tf_op jit(solution)/shard_map/ppermute | solution.py:337
  48.3 0.0 collective-permute-done.6.refs_2_
  48.3 1.1 %collective-permute-start.7 = (bf16[192,512]{1,0:T(8,128)(2,1)S(1)}, bf16[192,512]{1,0:T(8,128)(2,1)S(1)}, u32[]{:S(2)}, u32[]{:S(2)}) collective-permute-start(bf16[192,512]{1,0:T(8,128)(2,1)S(1)} %collective-permute-done.6.refs_2_), channel_id=1, source_target_pairs={{0,4},{1,5},{2,3},{3,2},{4,0},{5,1},{6,7},{7,6},{8,12},{9,13},{10,... | collective-permute-start | bytes 589832 | tf_op jit(solution)/shard_map/ppermute | solution.py:337
  49.4 0.0 collective-permute-done.4.second_ref.refs_4_
  49.4 0.0 copy-done.2
  49.4 0.0 copy-done.4
  49.4 0.6 queries.1
  50.0 0.0 copy-start.5
  50.0 0.0 copy-start.6
  50.1 0.1 collective-permute-start.5
  50.1 0.0 collective-permute-done.13.refs_3_
  50.2 1.6 %collective-permute-start.14 = (bf16[384,512]{1,0:T(8,128)(2,1)S(1)}, bf16[384,512]{1,0:T(8,128)(2,1)S(1)}, u32[]{:S(2)}, u32[]{:S(2)}) collective-permute-start(bf16[384,512]{1,0:T(8,128)(2,1)S(1)} %pad_maximum_fusion.3), channel_id=1, source_target_pairs={{0,1},{1,0},{2,6},{3,7},{4,5},{5,4},{6,2},{7,3},{8,9},{9,8},{10,14... | collective-permute-start | bytes 1179656 | tf_op jit(solution)/shard_map/ppermute | solution.py:337
  51.7 1.3 %collective-permute-done.10.refs_3_ = bf16[192,512]{1,0:T(8,128)(2,1)S(1)} collective-permute-done((bf16[192,512]{1,0:T(8,128)(2,1)S(1)}, bf16[192,512]{1,0:T(8,128)(2,1)S(1)}, u32[]{:S(2)}, u32[]{:S(2)}) %collective-permute-start.10) | collective-permute-done | bytes 196640 | tf_op jit(solution)/shard_map/ppermute | solution.py:337
  53.1 1.6 %collective-permute-start.11 = (bf16[384,512]{1,0:T(8,128)(2,1)S(1)}, bf16[384,512]{1,0:T(8,128)(2,1)S(1)}, u32[]{:S(2)}, u32[]{:S(2)}) collective-permute-start(bf16[384,512]{1,0:T(8,128)(2,1)S(1)} %pad_maximum_fusion.2), channel_id=1, source_target_pairs={{0,1},{1,0},{2,6},{3,7},{4,5},{5,4},{6,2},{7,3},{8,9},{9,8},{10,14... | collective-permute-start | bytes 1179656 | tf_op jit(solution)/shard_map/ppermute | solution.py:337
  54.6 2.3 %collective-permute-done.7.refs_3_ = bf16[192,512]{1,0:T(8,128)(2,1)S(1)} collective-permute-done((bf16[192,512]{1,0:T(8,128)(2,1)S(1)}, bf16[192,512]{1,0:T(8,128)(2,1)S(1)}, u32[]{:S(2)}, u32[]{:S(2)}) %collective-permute-start.7) | collective-permute-done | bytes 196640 | tf_op jit(solution)/shard_map/ppermute | solution.py:337
  56.9 1.6 %collective-permute-start.8 = (bf16[384,512]{1,0:T(8,128)(2,1)S(1)}, bf16[384,512]{1,0:T(8,128)(2,1)S(1)}, u32[]{:S(2)}, u32[]{:S(2)}) collective-permute-start(bf16[384,512]{1,0:T(8,128)(2,1)S(1)} %pad_maximum_fusion.1), channel_id=1, source_target_pairs={{0,1},{1,0},{2,6},{3,7},{4,5},{5,4},{6,2},{7,3},{8,9},{9,8},{10,14... | collective-permute-start | bytes 1179656 | tf_op jit(solution)/shard_map/ppermute | solution.py:337
  58.5 0.0 collective-permute-done.5.refs_1_.swapped_ref
  58.5 0.0 copy-done.5
  58.5 0.0 copy-done.6
  58.5 4.4 %attend.4.refs_8_ = f32[536,512]{1,0:T(8,128)S(1)} custom-call(bf16[288,512]{1,0:T(8,128)(2,1)S(1)} %get-tuple-element.17.refs_0_, bf16[288,512]{1,0:T(8,128)(2,1)S(1)} %collective-permute-done.5.refs_1_.swapped_ref, bf16[192,512]{1,0:T(8,128)(2,1)S(1)} %constant_dynamic-update-slice_fusion.own_ref.refs_2_, ...), custom_call_target="tpu_custom_call" | custom-call | flops 2000000000 | bytes 4000000 | tf_op jit(solution)/shard_map/attend/pallas_call | solution.py:232
  62.9 0.0 collective-permute-done.14.refs_4_
  62.9 4.6 %attend.5.refs_8_ = f32[536,512]{1,0:T(8,128)S(1)} custom-call(bf16[288,512]{1,0:T(8,128)(2,1)S(1)} %get-tuple-element.17.refs_0_, bf16[288,512]{1,0:T(8,128)(2,1)S(1)} %collective-permute-done.5.refs_1_.swapped_ref, bf16[192,512]{1,0:T(8,128)(2,1)S(1)} %collective-permute-done.12.refs_2_, ...), custom_call_target="tpu_custom_call", output_to_operand_aliasing={{}: (8, {})} | custom-call | flops 2000000000 | bytes 4000000 | tf_op jit(solution)/shard_map/attend/pallas_call | solution.py:232
  67.5 0.0 collective-permute-done.11.refs_4_
  67.6 4.8 %attend.6.refs_8_ = f32[536,512]{1,0:T(8,128)S(1)} custom-call(bf16[288,512]{1,0:T(8,128)(2,1)S(1)} %get-tuple-element.17.refs_0_, bf16[288,512]{1,0:T(8,128)(2,1)S(1)} %collective-permute-done.5.refs_1_.swapped_ref, bf16[192,512]{1,0:T(8,128)(2,1)S(1)} %collective-permute-done.9.refs_2_, ...), custom_call_target="tpu_custom_call", output_to_operand_aliasing={{}: (8, {})} | custom-call | flops 2000000000 | bytes 4000000 | tf_op jit(solution)/shard_map/attend/pallas_call | solution.py:232
  72.3 0.0 collective-permute-done.8.refs_4_
  72.4 4.6 %attend.7.mine_ref = f32[536,512]{1,0:T(8,128)S(1)} custom-call(bf16[288,512]{1,0:T(8,128)(2,1)S(1)} %get-tuple-element.17.refs_0_, bf16[288,512]{1,0:T(8,128)(2,1)S(1)} %collective-permute-done.5.refs_1_.swapped_ref, bf16[192,512]{1,0:T(8,128)(2,1)S(1)} %collective-permute-done.6.refs_2_, ...), custom_call_target="tpu_custom_call", output_to_operand_aliasing={{}: (8, {})} | custom-call | flops 2000000000 | bytes 4000000 | tf_op jit(solution)/shard_map/attend/pallas_call | solution.py:232
  77.0 0.1 slice.4
  77.0 0.0 copy-start.1
  77.0 0.1 collective-permute-start.15
  77.1 2.3 %collective-permute-done.15.other_ref = f32[536,384]{1,0:T(8,128)S(1)} collective-permute-done((f32[536,384]{1,0:T(8,128)S(1)}, f32[536,384]{1,0:T(8,128)S(1)}, u32[]{:S(2)}, u32[]{:S(2)}) %collective-permute-start.15) | collective-permute-done | bytes 823328 | tf_op jit(solution)/shard_map/ppermute | solution.py:337
  79.5 1.3 %combine.1.attended_ref = bf16[208,512]{1,0:T(8,128)(2,1)S(1)} custom-call(f32[536,512]{1,0:T(8,128)S(1)} %attend.7.mine_ref, f32[536,384]{1,0:T(8,128)S(1)} %collective-permute-done.15.other_ref), custom_call_target="tpu_custom_call" | custom-call | tf_op jit(solution)/shard_map/combine/pallas_call | solution.py:274
  80.8 0.6 collective-permute-start.16
  81.4 0.0 copy-done.1
  81.4 0.3 own_branch.1.branch_ref
  81.7 6.5 %collective-permute-done.16.attended_ref = bf16[208,512]{1,0:T(8,128)(2,1)S(1)} collective-permute-done((bf16[208,512]{1,0:T(8,128)(2,1)S(1)}, bf16[208,512]{1,0:T(8,128)(2,1)S(1)}, u32[]{:S(2)}, u32[]{:S(2)}) %collective-permute-start.16) | collective-permute-done | bytes 213024 | tf_op jit(solution)/shard_map/ppermute | solution.py:337
  88.2 1.0 %finish.1 = bf16[256,512]{1,0:T(8,128)(2,1)} custom-call(f32[208,512]{1,0:T(8,128)S(1)} %own_branch.1.branch_ref, bf16[208,512]{1,0:T(8,128)(2,1)S(1)} %collective-permute-done.16.attended_ref, bf16[2,512,512]{2,1,0:T(8,128)(2,1)S(1)} %bitcast.7, bf16[96,512]{1,0:T(8,128)(2,1)S(1)} %get-tuple-element.18.normed_ref, ...), custom_call_target="tpu_custom_call" | custom-call | tf_op jit(solution)/shard_map/finish/pallas_call | solution.py:315
  (6 shorter events, 0.1 us)
Async XLA Ops:
  0.0 2.2 %copy-start = (bf16[4096,512]{1,0:T(8,128)(2,1)S(1)}, bf16[4096,512]{1,0:T(8,128)(2,1)}, u32[]{:S(2)}) copy-start(bf16[4096,512]{1,0:T(8,128)(2,1)} %messages_ref.1) | copy-start | bytes 12582916
  2.2 0.7 copy-start.3
  7.0 10.8 %collective-permute-start = (f32[192,512]{1,0:T(8,128)S(1)}, f32[192,512]{1,0:T(8,128)S(1)}, u32[]{:S(2)}, u32[]{:S(2)}) collective-permute-start(f32[192,512]{1,0:T(8,128)S(1)} %get-tuple-element.13), channel_id=1, source_target_pairs={{0,30},{2,0},{4,2},{6,4},{8,6},{10,8},{12,10},{14,12},{16,14},{18,... | collective-permute-start | bytes 1179656 | tf_op jit(solution)/shard_map/ppermute | solution.py:391
  12.5 9.9 %collective-permute-start.1 = (f32[192,512]{1,0:T(8,128)S(1)}, f32[192,512]{1,0:T(8,128)S(1)}, u32[]{:S(2)}, u32[]{:S(2)}) collective-permute-start(f32[192,512]{1,0:T(8,128)S(1)} %get-tuple-element.14), channel_id=1, source_target_pairs={{0,2},{2,4},{4,6},{6,8},{8,10},{10,12},{12,14},{14,16},{16,18},{18... | collective-permute-start | bytes 1179656 | tf_op jit(solution)/shard_map/ppermute | solution.py:391
  22.4 27.0 %copy-start.2 = (bf16[1024,512]{1,0:T(8,128)(2,1)S(1)}, bf16[1024,512]{1,0:T(8,128)(2,1)}, u32[]{:S(2)}) copy-start(bf16[1024,512]{1,0:T(8,128)(2,1)} %param.12) | copy-start | bytes 3145732
  22.4 27.0 %copy-start.4 = (f32[1024]{0:T(1024)S(1)}, f32[1024]{0:T(1024)}, u32[]{:S(2)}) copy-start(f32[1024]{0:T(1024)} %param.11) | copy-start | bytes 12292
  22.5 1.4 %collective-permute-start.2 = (bf16[96,512]{1,0:T(8,128)(2,1)S(1)}, bf16[96,512]{1,0:T(8,128)(2,1)S(1)}, u32[]{:S(2)}, u32[]{:S(2)}) collective-permute-start(bf16[96,512]{1,0:T(8,128)(2,1)S(1)} %get-tuple-element.16), channel_id=1, source_target_pairs={{0,2},{1,3},{2,0},{3,1},{4,6},{5,7},{6,4},{7,5},{8,10},{9,11},{10,... | collective-permute-start | bytes 294920 | tf_op jit(solution)/shard_map/ppermute | solution.py:337
  23.8 5.7 %collective-permute-start.3 = (bf16[192,512]{1,0:T(8,128)(2,1)S(1)}, bf16[192,512]{1,0:T(8,128)(2,1)S(1)}, u32[]{:S(2)}, u32[]{:S(2)}) collective-permute-start(bf16[192,512]{1,0:T(8,128)(2,1)S(1)} %constant_dynamic-update-slice_fusion.own_ref.refs_2_), channel_id=1, source_target_pairs={{0,4},{1,5},{2,3},{3,2},{4,0},{5,1},{6,7},{7,6},{8,12},{9,13},{10,... | collective-permute-start | bytes 589832 | tf_op jit(solution)/shard_map/ppermute | solution.py:337
  29.6 19.8 %collective-permute-start.4 = (bf16[384,512]{1,0:T(8,128)(2,1)S(1)}, bf16[384,512]{1,0:T(8,128)(2,1)S(1)}, u32[]{:S(2)}, u32[]{:S(2)}) collective-permute-start(bf16[384,512]{1,0:T(8,128)(2,1)S(1)} %pad_maximum_fusion), channel_id=1, source_target_pairs={{0,1},{1,0},{2,6},{3,7},{4,5},{5,4},{6,2},{7,3},{8,9},{9,8},{10,14... | collective-permute-start | bytes 1179656 | tf_op jit(solution)/shard_map/ppermute | solution.py:337
  31.2 7.4 %collective-permute-start.12 = (bf16[192,512]{1,0:T(8,128)(2,1)S(1)}, bf16[192,512]{1,0:T(8,128)(2,1)S(1)}, u32[]{:S(2)}, u32[]{:S(2)}) collective-permute-start(bf16[192,512]{1,0:T(8,128)(2,1)S(1)} %constant_dynamic-update-slice_fusion.own_ref.refs_2_), channel_id=1, source_target_pairs={{0,8},{1,9},{2,10},{3,11},{4,12},{5,13},{6,14},{7,15},{8,0},{9,1},... | collective-permute-start | bytes 589832 | tf_op jit(solution)/shard_map/ppermute | solution.py:337
  31.2 16.2 %collective-permute-start.9 = (bf16[192,512]{1,0:T(8,128)(2,1)S(1)}, bf16[192,512]{1,0:T(8,128)(2,1)S(1)}, u32[]{:S(2)}, u32[]{:S(2)}) collective-permute-start(bf16[192,512]{1,0:T(8,128)(2,1)S(1)} %constant_dynamic-update-slice_fusion.own_ref.refs_2_), channel_id=1, source_target_pairs={{0,16},{1,17},{2,18},{3,19},{4,20},{5,21},{6,22},{7,23},{8,24},{9,... | collective-permute-start | bytes 589832 | tf_op jit(solution)/shard_map/ppermute | solution.py:337
  32.4 15.9 %collective-permute-start.6 = (bf16[192,512]{1,0:T(8,128)(2,1)S(1)}, bf16[192,512]{1,0:T(8,128)(2,1)S(1)}, u32[]{:S(2)}, u32[]{:S(2)}) collective-permute-start(bf16[192,512]{1,0:T(8,128)(2,1)S(1)} %constant_dynamic-update-slice_fusion.own_ref.refs_2_), channel_id=1, source_target_pairs={{0,24},{1,25},{2,26},{3,27},{4,28},{5,29},{6,30},{7,31},{8,16},{9,... | collective-permute-start | bytes 589832 | tf_op jit(solution)/shard_map/ppermute | solution.py:337
  38.5 11.6 %collective-permute-start.13 = (bf16[192,512]{1,0:T(8,128)(2,1)S(1)}, bf16[192,512]{1,0:T(8,128)(2,1)S(1)}, u32[]{:S(2)}, u32[]{:S(2)}) collective-permute-start(bf16[192,512]{1,0:T(8,128)(2,1)S(1)} %collective-permute-done.12.refs_2_), channel_id=1, source_target_pairs={{0,4},{1,5},{2,3},{3,2},{4,0},{5,1},{6,7},{7,6},{8,12},{9,13},{10,... | collective-permute-start | bytes 589832 | tf_op jit(solution)/shard_map/ppermute | solution.py:337
  47.4 5.7 %collective-permute-start.10 = (bf16[192,512]{1,0:T(8,128)(2,1)S(1)}, bf16[192,512]{1,0:T(8,128)(2,1)S(1)}, u32[]{:S(2)}, u32[]{:S(2)}) collective-permute-start(bf16[192,512]{1,0:T(8,128)(2,1)S(1)} %collective-permute-done.9.refs_2_), channel_id=1, source_target_pairs={{0,4},{1,5},{2,3},{3,2},{4,0},{5,1},{6,7},{7,6},{8,12},{9,13},{10,... | collective-permute-start | bytes 589832 | tf_op jit(solution)/shard_map/ppermute | solution.py:337
  48.3 8.6 %collective-permute-start.7 = (bf16[192,512]{1,0:T(8,128)(2,1)S(1)}, bf16[192,512]{1,0:T(8,128)(2,1)S(1)}, u32[]{:S(2)}, u32[]{:S(2)}) collective-permute-start(bf16[192,512]{1,0:T(8,128)(2,1)S(1)} %collective-permute-done.6.refs_2_), channel_id=1, source_target_pairs={{0,4},{1,5},{2,3},{3,2},{4,0},{5,1},{6,7},{7,6},{8,12},{9,13},{10,... | collective-permute-start | bytes 589832 | tf_op jit(solution)/shard_map/ppermute | solution.py:337
  50.0 8.4 %copy-start.5 = (bf16[1024,512]{1,0:T(8,128)(2,1)S(1)}, bf16[1024,512]{1,0:T(8,128)(2,1)}, u32[]{:S(2)}) copy-start(bf16[1024,512]{1,0:T(8,128)(2,1)} %param.13) | copy-start | bytes 3145732
  50.0 8.4 %copy-start.6 = (bf16[1024,512]{1,0:T(8,128)(2,1)S(1)}, bf16[1024,512]{1,0:T(8,128)(2,1)}, u32[]{:S(2)}) copy-start(bf16[1024,512]{1,0:T(8,128)(2,1)} %param.14) | copy-start | bytes 3145732
  50.1 8.4 %collective-permute-start.5 = (bf16[288,512]{1,0:T(8,128)(2,1)S(1)}, bf16[288,512]{1,0:T(8,128)(2,1)S(1)}, u32[]{:S(2)}, u32[]{:S(2)}) collective-permute-start(bf16[288,512]{1,0:T(8,128)(2,1)S(1)} %get-tuple-element.17.refs_0_), channel_id=1, source_target_pairs={{0,2},{1,3},{2,0},{3,1},{4,6},{5,7},{6,4},{7,5},{8,10},{9,11},{10,... | collective-permute-start | bytes 884744 | tf_op jit(solution)/shard_map/ppermute | solution.py:337
  50.2 12.8 %collective-permute-start.14 = (bf16[384,512]{1,0:T(8,128)(2,1)S(1)}, bf16[384,512]{1,0:T(8,128)(2,1)S(1)}, u32[]{:S(2)}, u32[]{:S(2)}) collective-permute-start(bf16[384,512]{1,0:T(8,128)(2,1)S(1)} %pad_maximum_fusion.3), channel_id=1, source_target_pairs={{0,1},{1,0},{2,6},{3,7},{4,5},{5,4},{6,2},{7,3},{8,9},{9,8},{10,14... | collective-permute-start | bytes 1179656 | tf_op jit(solution)/shard_map/ppermute | solution.py:337
  53.1 14.5 %collective-permute-start.11 = (bf16[384,512]{1,0:T(8,128)(2,1)S(1)}, bf16[384,512]{1,0:T(8,128)(2,1)S(1)}, u32[]{:S(2)}, u32[]{:S(2)}) collective-permute-start(bf16[384,512]{1,0:T(8,128)(2,1)S(1)} %pad_maximum_fusion.2), channel_id=1, source_target_pairs={{0,1},{1,0},{2,6},{3,7},{4,5},{5,4},{6,2},{7,3},{8,9},{9,8},{10,14... | collective-permute-start | bytes 1179656 | tf_op jit(solution)/shard_map/ppermute | solution.py:337
  56.9 15.4 %collective-permute-start.8 = (bf16[384,512]{1,0:T(8,128)(2,1)S(1)}, bf16[384,512]{1,0:T(8,128)(2,1)S(1)}, u32[]{:S(2)}, u32[]{:S(2)}) collective-permute-start(bf16[384,512]{1,0:T(8,128)(2,1)S(1)} %pad_maximum_fusion.1), channel_id=1, source_target_pairs={{0,1},{1,0},{2,6},{3,7},{4,5},{5,4},{6,2},{7,3},{8,9},{9,8},{10,14... | collective-permute-start | bytes 1179656 | tf_op jit(solution)/shard_map/ppermute | solution.py:337
  77.0 4.4 %copy-start.1 = (bf16[1024,512]{1,0:T(8,128)(2,1)S(1)}, bf16[1024,512]{1,0:T(8,128)(2,1)}, u32[]{:S(2)}) copy-start(bf16[1024,512]{1,0:T(8,128)(2,1)} %param.15) | copy-start | bytes 3145732
  77.0 2.4 %collective-permute-start.15 = (f32[536,384]{1,0:T(8,128)S(1)}, f32[536,384]{1,0:T(8,128)S(1)}, u32[]{:S(2)}, u32[]{:S(2)}) collective-permute-start(f32[536,384]{1,0:T(8,128)S(1)} %slice.4), channel_id=1, source_target_pairs={{0,2},{1,3},{2,0},{3,1},{4,6},{5,7},{6,4},{7,5},{8,10},{9,11},{10,... | collective-permute-start | bytes 2469896 | tf_op jit(solution)/shard_map/ppermute | solution.py:337
  80.8 7.4 %collective-permute-start.16 = (bf16[208,512]{1,0:T(8,128)(2,1)S(1)}, bf16[208,512]{1,0:T(8,128)(2,1)S(1)}, u32[]{:S(2)}, u32[]{:S(2)}) collective-permute-start(bf16[208,512]{1,0:T(8,128)(2,1)S(1)} %combine.1.attended_ref), channel_id=1, source_target_pairs={{0,1},{1,0},{2,3},{3,2},{4,5},{5,4},{6,7},{7,6},{8,9},{9,8},{10,11... | collective-permute-start | bytes 638984 | tf_op jit(solution)/shard_map/ppermute | solution.py:337

commit v3 on v2

--- a/solution.py
+++ b/solution.py
@@ -11,10 +11,9 @@
 HD = 64
 ANCH_DEV = 256
 LIVE_MAX = 192
-HALF = LIVE_MAX // 2
 PAD = 16
 QROWS = 2 * LIVE_MAX
-SPILL = 128 - HALF
+SENT = 256
 TILE = 128
 
 EPS = 1e-06
@@ -40,11 +39,6 @@
     return lax.dot_general(a, b, (contract, ((), ())), preferred_element_type=F32)
 
 
-def row_of(slot):
-    block = slot // 16
-    return (block % 2) * HALF + (block // 2) * 16 + slot % 16
-
-
 def pool_kernel(tiles, anchors_smem, anchors_ref, messages_ref, before_ref, own_ref, after_ref, sums):
     step = pl.program_id(0)
     partitions = lax.axis_size("ctx")
@@ -59,7 +53,7 @@
         index = step * tiles + tile
         owner = anchors_smem[index * TILE] // ANCH_DEV
         side = lax.rem(owner - center + 1 + partitions, partitions)
-        slot = row_of(anchors_ref[pl.ds(index, 1), :] % ANCH_DEV)
+        slot = anchors_ref[pl.ds(index, 1), :] % ANCH_DEV
         onehot = jnp.where(rows == slot, 1.0, 0.0).astype(BF16)
         part = dot(onehot, messages_ref[tile * TILE : (tile + 1) * TILE, :])
         sums[side] += part
@@ -90,37 +84,43 @@
             scratch_shapes=[pltpu.VMEM((3, LIVE_MAX, channels), F32)],
         ),
         out_shape=[shape] * 3,
-        compiler_params=params(),
+        compiler_params=params(60),
         name="pool",
     )(node_anchor, node_anchor.reshape(nodes // TILE, TILE), messages)
 
 
-def settle_kernel(count_ref, own_ref, before_ref, after_ref, keep_ref, send_ref):
-    core = lax.rem(lax.axis_index("ctx"), 2)
-    count = count_ref[0]
-
-    def half(which):
-        at = pl.ds(pl.multiple_of(which * HALF, 16), HALF)
-        total = own_ref[at, :] + before_ref[at, :] + after_ref[at, :]
-        row = lax.broadcasted_iota(jnp.int32, total.shape, 0)
-        slot = (2 * (row // 16) + which) * 16 + row % 16
-        return jnp.where(slot < count, total, MARK).astype(BF16)
-
-    keep_ref[...] = half(core)
-    send_ref[...] = half(1 - core)
+def settle_kernel(count_ref, own_ref, before_ref, after_ref, out_ref):
+    total = own_ref[...] + before_ref[...] + after_ref[...]
+    slot = lax.broadcasted_iota(jnp.int32, total.shape, 0)
+    out_ref[...] = jnp.where(slot < count_ref[0], total, MARK).astype(BF16)
 
 
 def settle(count, own, before, after):
-    channels = own.shape[1]
-    shape = jax.ShapeDtypeStruct((HALF, channels), BF16)
     return pl.pallas_call(
         settle_kernel,
         in_specs=[pl.BlockSpec(memory_space=pltpu.SMEM)] + vmem(3),
-        out_specs=vmem(2),
-        out_shape=[shape] * 2,
+        out_specs=pl.BlockSpec(memory_space=pltpu.VMEM),
+        out_shape=jax.ShapeDtypeStruct(own.shape, BF16),
         compiler_params=params(),
         name="settle",
     )(count, own, before, after)
+
+
+def join_kernel(a_ref, b_ref, *rest):
+    rows = a_ref.shape[0]
+    rest[-1][:rows, :] = a_ref[...]
+    rest[-1][rows:, :] = b_ref[...]
+
+
+def join(a, b, *after):
+    return pl.pallas_call(
+        join_kernel,
+        in_specs=vmem(2) + [pl.BlockSpec(memory_space=pl.ANY)] * len(after),
+        out_specs=pl.BlockSpec(memory_space=pltpu.VMEM),
+        out_shape=jax.ShapeDtypeStruct((a.shape[0] + b.shape[0], a.shape[1]), a.dtype),
+        compiler_params=params(),
+        name="join",
+    )(a, b, *after)
 
 
 def normalise(mine, other, gain_ref, x):
@@ -140,14 +140,13 @@
     return (dot(mine, w_ref[x]) + dot(other, w_ref[1 - x])).astype(BF16)
 
 
-def query_kernel(own_ref, first_ref, second_ref, gain_ref, wq_ref, swap_ref, normed_ref):
+def query_kernel(own_ref, first_ref, second_ref, gain_ref, wq_ref, query_ref, normed_ref):
     core = lax.rem(lax.axis_index("ctx"), 2)
     x = lax.axis_index("head")
     other = jnp.where(core == 0, second_ref[:LIVE_MAX, :], first_ref[...])
     mine, other, unused = normalise(own_ref[...], other, gain_ref, x)
-    swap_ref[:LIVE_MAX, :] = project(mine, other, wq_ref, x)
-    swap_ref[LIVE_MAX:, :] = mine[HALF:]
-    normed_ref[...] = mine[:HALF]
+    query_ref[...] = project(mine, other, wq_ref, x)
+    normed_ref[...] = mine
 
 
 def make_queries(own, first, second, gain, wq):
@@ -156,10 +155,7 @@
         query_kernel,
         in_specs=vmem(5),
         out_specs=vmem(2),
-        out_shape=[
-            jax.ShapeDtypeStruct((LIVE_MAX + HALF, channels), BF16),
-            jax.ShapeDtypeStruct((HALF, channels), BF16),
-        ],
+        out_shape=[jax.ShapeDtypeStruct((LIVE_MAX, channels), BF16)] * 2,
         compiler_params=params(),
         cost_estimate=pl.CostEstimate(flops=4 * 10**8, bytes_accessed=2 * 10**6, transcendentals=0),
         name="queries",
@@ -181,23 +177,27 @@
     other = jnp.concatenate([jnp.where(core == 0, two, one), second_ref[LIVE_MAX:, :]], axis=0)
     mine, other, dead = normalise(mine, other, gain_ref, x)
     keys = project(mine, other, wk_ref, x)
-    values = project(mine, other, wv_ref, x).T
+    values = project(mine, other, wv_ref, x)
     shut = jnp.where(dead, NEG, 0.0).astype(BF16)
 
     live = jnp.sum(jnp.where(dead, 0.0, 1.0), axis=0, keepdims=True)
-    value_sum = jnp.sum(values.astype(F32), axis=1, keepdims=True)
-    if not first_call:
-        live = live + state_ref[channels + 2 * heads : channels + 2 * heads + 1, QROWS : QROWS + 1]
-        value_sum = value_sum + state_ref[:channels, QROWS : QROWS + 1]
-    out_ref[:channels, QROWS:] = jnp.broadcast_to(value_sum, (channels, 128))
-    out_ref[channels:, QROWS:] = jnp.broadcast_to(live, (out_ref.shape[0] - channels, 128))
+    live = jnp.broadcast_to(live, (1, SENT))
+    value_sum = jnp.sum(values.astype(F32), axis=0, keepdims=True)
+    extra = channels + 2 * heads
+    for part in range(channels // SENT):
+        at = value_sum[:, part * SENT : (part + 1) * SENT]
+        row = slice(extra + part, extra + part + 1)
+        out_ref[row, QROWS - SENT :] = at if first_call else at + state_ref[row, QROWS - SENT :]
+    row = slice(extra + channels // SENT, extra + channels // SENT + 1)
+    out_ref[row, QROWS - SENT :] = live if first_call else live + state_ref[row, QROWS - SENT :]
+    values = values.T
 
     lane_k = lax.broadcasted_iota(jnp.int32, (keys.shape[0], 128), 1)
     lane_q = lax.broadcasted_iota(jnp.int32, (QROWS, 128), 1)
     for pair in range(heads // 2):
         at = slice(pair * 128, (pair + 1) * 128)
         query = jnp.concatenate(
-            [qm[:HALF, at], qr[HALF:LIVE_MAX, at], qm[HALF + SPILL : LIVE_MAX, at], qr[:HALF, at], qm[HALF : HALF + SPILL, at]],
+            [qm[:, at], qr[128:, at], qr[:128, at]],
             axis=0,
         )
         for side in range(2):
@@ -233,7 +233,7 @@
         functools.partial(attend_kernel, state is None),
         in_specs=vmem(len(args)),
         out_specs=pl.BlockSpec(memory_space=pltpu.VMEM),
-        out_shape=jax.ShapeDtypeStruct((channels + 2 * (channels // HD) + 8, QROWS + 128), F32),
+        out_shape=jax.ShapeDtypeStruct((channels + 2 * (channels // HD) + 8, QROWS), F32),
         input_output_aliases={} if state is None else {len(args) - 1: 0},
         compiler_params=params(),
         cost_estimate=pl.CostEstimate(
@@ -246,27 +246,28 @@
 def combine_kernel(mine_ref, other_ref, out_ref):
     channels = out_ref.shape[1]
     heads = channels // HD
-    width = 256
-    lane = lax.broadcasted_iota(jnp.int32, (HD, width), 1)
 
     def theirs(at):
         middle = other_ref[at, :128]
-        return jnp.concatenate([other_ref[at, 128:256], middle[:, 64:], middle[:, :64]], axis=1)
-
-    at = slice(channels + 2 * heads, channels + 2 * heads + 1)
-    live = mine_ref[at, QROWS : QROWS + 1] + other_ref[at, 256:257]
+        return jnp.concatenate([other_ref[at, 128:], middle[:, 64:], middle[:, :64]], axis=1)
+
     for head in range(heads):
         at_top = slice(channels + head, channels + head + 1)
         at_total = slice(channels + heads + head, channels + heads + head + 1)
         at = slice(head * HD, (head + 1) * HD)
-        a, b = mine_ref[at_top, :width], theirs(at_top)
+        a, b = mine_ref[at_top, :SENT], theirs(at_top)
         top = jnp.maximum(a, b)
         a, b = jnp.exp2((a - top) * RATE), jnp.exp2((b - top) * RATE)
-        total = mine_ref[at_total, :width] * a + theirs(at_total) * b
-        mixed = (mine_ref[at, :width] * a + theirs(at) * b) / total
-        mean = (mine_ref[at, QROWS : QROWS + 1] + other_ref[at, 256:257]) / live
-        mixed = jnp.where(lane < LIVE_MAX, mixed, mean)
-        out_ref[:, at] = mixed.T[: LIVE_MAX + PAD].astype(BF16)
+        total = mine_ref[at_total, :SENT] * a + theirs(at_total) * b
+        mixed = (mine_ref[at, :SENT] * a + theirs(at) * b) / total
+        out_ref[:LIVE_MAX, at] = mixed.T[:LIVE_MAX].astype(BF16)
+    extra = channels + 2 * heads
+    sums = mine_ref[extra : extra + 8, QROWS - SENT :] + other_ref[extra : extra + 8, :]
+    parts = channels // SENT
+    live = sums[parts : parts + 1, :]
+    for part in range(parts):
+        mean = (sums[part : part + 1, :] / live).astype(BF16)
+        out_ref[LIVE_MAX:, part * SENT : (part + 1) * SENT] = jnp.broadcast_to(mean, (PAD, SENT))
 
 
 def combine(mine, other):
@@ -297,29 +298,22 @@
     )(attended, w_out)
 
 
-def finish_kernel(branch_ref, attended_ref, w_ref, normed_ref, swapped_ref, out_ref):
-    core = lax.rem(lax.axis_index("ctx"), 2)
+def finish_kernel(branch_ref, attended_ref, w_ref, normed_ref, out_ref):
     branch = branch_ref[...] + dot(attended_ref[...], w_ref[1 - lax.axis_index("head")])
-    near = (branch[:HALF] + normed_ref[...].astype(F32)).astype(BF16)
-    far = (branch[HALF:LIVE_MAX] + swapped_ref[LIVE_MAX:, :].astype(F32)).astype(BF16)
-    even = jnp.where(core == 0, near, far)
-    odd = jnp.where(core == 0, far, near)
-    for block in range(HALF // 16):
-        out_ref[32 * block : 32 * block + 16, :] = even[16 * block : 16 * block + 16]
-        out_ref[32 * block + 16 : 32 * block + 32, :] = odd[16 * block : 16 * block + 16]
+    out_ref[:LIVE_MAX, :] = (branch[:LIVE_MAX] + normed_ref[...].astype(F32)).astype(BF16)
     rest = out_ref.shape[0] - LIVE_MAX
     out_ref[LIVE_MAX:, :] = jnp.broadcast_to(branch[LIVE_MAX : LIVE_MAX + 1], (rest, branch.shape[1])).astype(BF16)
 
 
-def finish(branch, attended, w_out, normed, swapped):
+def finish(branch, attended, w_out, normed):
     return pl.pallas_call(
         finish_kernel,
-        in_specs=vmem(5),
+        in_specs=vmem(4),
         out_specs=pl.BlockSpec(memory_space=pltpu.VMEM),
         out_shape=jax.ShapeDtypeStruct((ANCH_DEV, branch.shape[1]), BF16),
         compiler_params=params(),
         name="finish",
-    )(branch, attended, w_out, normed, swapped)
+    )(branch, attended, w_out, normed)
 
 
 def pairs(move):
@@ -366,24 +360,24 @@
     before, own, after = pool(messages, node_anchor)
     from_next = shift(before, -1)
     from_previous = shift(after, 1)
-    keep, away = settle(anchor_count, own, from_next, from_previous)
-    mine = jnp.concatenate([keep, send(away, across_core)], axis=0)
-    slices = [mine] + [send(mine, across_z(step)) for step in (1, 2, 3)]
+    mine = settle(anchor_count, own, from_next, from_previous)
     gain = norm_gain.reshape(2, 1, channels)
     wq, wk, wv, wo = halves(w_query), halves(w_key), halves(w_value), halves(w_out)
-    state = None
+    slices = [mine] + [send(mine, across_z(step)) for step in (1, 2, 3)]
+    states = []
     for index, rows in enumerate(slices):
         first = send(rows, across_first)
-        second = send(jnp.concatenate([rows, first], axis=0), across_second)
+        second = send(join(rows, first, *states[: max(index - 1, 0)][-1:]), across_second)
         if index == 0:
-            swap, normed = make_queries(rows, first, second, gain, wq)
-            swapped = send(swap, across_core)
-        state = attend(swap, swapped, rows, first, second, gain, wk, wv, state)
-    other = send(state[:, 128:], across_core)
+            query, normed = make_queries(rows, first, second, gain, wq)
+            swapped = send(query, across_core)
+        states.append(attend(query, swapped, rows, first, second, gain, wk, wv, *states[-1:]))
+    state = states[-1]
+    other = send(state[:, QROWS - SENT :], across_core)
     attended = combine(state, other)
     attended_other = send(attended, across_x)
     branch = own_branch(attended, wo)
-    return finish(branch, attended_other, wo, normed, swapped)
+    return finish(branch, attended_other, wo, normed)
 
 
 def shift(x, by):

time: 89.4 us -> 83.8 us (0.937)
  starting transfers between devices: 22.3 us -> 14.3 us
  Pallas kernels: 25.8 us -> 29.7 us
  local copies, waits for them, and re-layouts: 3.02 us -> 1.05 us
    ppermute x15 -> x14, starting transfers between devices: 16.8 us -> 8.81 us  [send(): return lax.ppermute(array, ALL, pairs(move))]
    pallas_call x1, Pallas kernels: 4.06 us -> 8.37 us  [pool(): pl.pallas_call(functools.partial(pool_kernel, tiles), grid_spec=pltpu.Pre...]
    unnamed x15 -> x12, local copies, waits for them, and re-layouts: 2.94 us -> 1.02 us
    ppermute x15 -> x14, waiting for transfers between devices: 27.9 us -> 28.2 us  [send(): return lax.ppermute(array, ALL, pairs(move))]
  transfers between devices with their start and end apart: 17 -> 16, of which waited for: 10 -> 9; matrix products, arithmetic and copies ran while one was open for 0% -> 0% of each run, Pallas kernels for 16% -> 17%
where the time goes in v3:
time: 83.8 us; the launch traced here: 83.4 us
  waiting for transfers between devices  37.6 us (45%)
  Pallas kernels  29.7 us (35%)
  starting transfers between devices  14.3 us (17%)
  local copies, waits for them, and re-layouts  1.05 us (1%)
    ppermute x14, waiting for transfers between devices, send(): return lax.ppermute(array, ALL, pairs(move))  28.2 us
    pallas_call x4, Pallas kernels, attend(): pl.pallas_call(functools.partial(attend_kernel, state is None), in_specs=...  18.3 us
    ppermute x2, waiting for transfers between devices, shift(): return lax.ppermute(x, 'ctx', [(i, (i + by) % peers) for i in range(peers)])  9.45 us
    ppermute x14, starting transfers between devices, send(): return lax.ppermute(array, ALL, pairs(move))  8.81 us
    pallas_call x1, Pallas kernels, pool(): pl.pallas_call(functools.partial(pool_kernel, tiles), grid_spec=pltpu.Pre...  8.37 us
    ppermute x2, starting transfers between devices, shift(): return lax.ppermute(x, 'ctx', [(i, (i + by) % peers) for i in range(peers)])  5.46 us
  transfers between devices with their start and end apart: 16, of which 9 were waited for; matrix products, arithmetic and copies ran while one was open for 0% of the time, Pallas kernels for 17%

profile of v3, /device:TPU:0, one launch (start us, length us, event | category | flops | bytes accessed | tf_op | source)
XLA Modules:
  0.0 83.4 jit_solution(12281092511925699296)
XLA Ops:
  0.0 0.0 copy-start.3
  0.0 0.0 copy-start.1
  0.0 0.0 copy-start.4
  0.0 0.0 copy-start.5
  0.0 8.4 %pool.1 = (f32[192,512]{1,0:T(8,128)}, f32[192,512]{1,0:T(8,128)}, f32[192,512]{1,0:T(8,128)}) custom-call(s32[4096]{0:T(1024)} %anchors_smem.1, s32[32,128]{1,0:T(8,128)} %bitcast.22, bf16[4096,512]{1,0:T(8,128)(2,1)} %messages_ref.1), custom_call_target="tpu_custom_call" | custom-call | tf_op jit(solution)/shard_map/pool/pallas_call | solution.py:74
  8.4 5.5 %collective-permute-start = (f32[192,512]{1,0:T(8,128)}, f32[192,512]{1,0:T(8,128)S(1)}, u32[]{:S(2)}, u32[]{:S(2)}) collective-permute-start(f32[192,512]{1,0:T(8,128)} %get-tuple-element.11), channel_id=1, source_target_pairs={{0,30},{2,0},{4,2},{6,4},{8,6},{10,8},{12,10},{14,12},{16,14},{18,... | collective-permute-start | bytes 1179656 | tf_op jit(solution)/shard_map/ppermute | solution.py:385
  13.8 0.0 collective-permute-start.1
  14.5 5.0 %collective-permute-done.before_ref = f32[192,512]{1,0:T(8,128)S(1)} collective-permute-done((f32[192,512]{1,0:T(8,128)}, f32[192,512]{1,0:T(8,128)S(1)}, u32[]{:S(2)}, u32[]{:S(2)}) %collective-permute-start) | collective-permute-done | bytes 393248 | tf_op jit(solution)/shard_map/ppermute | solution.py:385
  19.5 4.5 %collective-permute-done.1.after_ref = f32[192,512]{1,0:T(8,128)S(1)} collective-permute-done((f32[192,512]{1,0:T(8,128)}, f32[192,512]{1,0:T(8,128)S(1)}, u32[]{:S(2)}, u32[]{:S(2)}) %collective-permute-start.1) | collective-permute-done | bytes 393248 | tf_op jit(solution)/shard_map/ppermute | solution.py:385
  24.0 0.0 copy-start.2
  24.0 1.0 %copy-done.2 = f32[192,512]{1,0:T(8,128)S(1)} copy-done((f32[192,512]{1,0:T(8,128)S(1)}, f32[192,512]{1,0:T(8,128)}, u32[]{:S(2)}) %copy-start.2) | copy-done | bytes 393240
  24.9 0.1 settle.1.a_ref.own_ref.refs_2_
  25.0 0.1 collective-permute-start.2
  25.1 0.6 collective-permute-start.7
  25.7 6.8 %collective-permute-done.2.b_ref.first_ref.refs_3_ = bf16[192,512]{1,0:T(8,128)(2,1)S(1)} collective-permute-done((bf16[192,512]{1,0:T(8,128)(2,1)S(1)}, bf16[192,512]{1,0:T(8,128)(2,1)S(1)}, u32[]{:S(2)}, u32[]{:S(2)}) %collective-permute-start.2) | collective-permute-done | bytes 196640 | tf_op jit(solution)/shard_map/ppermute | solution.py:331
  32.5 1.7 %collective-permute-start.3 = (bf16[384,512]{1,0:T(8,128)(2,1)S(1)}, bf16[384,512]{1,0:T(8,128)(2,1)S(1)}, u32[]{:S(2)}, u32[]{:S(2)}) collective-permute-start(bf16[384,512]{1,0:T(8,128)(2,1)S(1)} %join.4), channel_id=1, source_target_pairs={{0,1},{1,0},{2,6},{3,7},{4,5},{5,4},{6,2},{7,3},{8,9},{9,8},{10,14... | collective-permute-start | bytes 1179656 | tf_op jit(solution)/shard_map/ppermute | solution.py:331
  34.2 0.0 collective-permute-done.7.a_ref.refs_2_
  34.2 0.0 collective-permute-start.8
  34.2 0.0 collective-permute-start.11
  34.2 1.1 %collective-permute-start.5 = (bf16[192,512]{1,0:T(8,128)(2,1)S(1)}, bf16[192,512]{1,0:T(8,128)(2,1)S(1)}, u32[]{:S(2)}, u32[]{:S(2)}) collective-permute-start(bf16[192,512]{1,0:T(8,128)(2,1)S(1)} %settle.1.a_ref.own_ref.refs_2_), channel_id=1, source_target_pairs={{0,24},{1,25},{2,26},{3,27},{4,28},{5,29},{6,30},{7,31},{8,16},{9,... | collective-permute-start | bytes 589832 | tf_op jit(solution)/shard_map/ppermute | solution.py:331
  35.3 6.5 %collective-permute-done.8.b_ref.refs_3_ = bf16[192,512]{1,0:T(8,128)(2,1)S(1)} collective-permute-done((bf16[192,512]{1,0:T(8,128)(2,1)S(1)}, bf16[192,512]{1,0:T(8,128)(2,1)S(1)}, u32[]{:S(2)}, u32[]{:S(2)}) %collective-permute-start.8) | collective-permute-done | bytes 196640 | tf_op jit(solution)/shard_map/ppermute | solution.py:331
  41.8 0.7 collective-permute-start.9
  42.5 0.0 collective-permute-done.3.second_ref.refs_4_
  42.5 0.0 copy-done.3
  42.5 0.0 copy-done.1
  42.5 0.6 queries.1
  43.1 0.1 collective-permute-start.4
  43.2 3.3 %collective-permute-done.11.a_ref.refs_2_ = bf16[192,512]{1,0:T(8,128)(2,1)S(1)} collective-permute-done((bf16[192,512]{1,0:T(8,128)(2,1)S(1)}, bf16[192,512]{1,0:T(8,128)(2,1)S(1)}, u32[]{:S(2)}, u32[]{:S(2)}) %collective-permute-start.11) | collective-permute-done | bytes 196640 | tf_op jit(solution)/shard_map/ppermute | solution.py:331
  46.5 1.2 %collective-permute-start.12 = (bf16[192,512]{1,0:T(8,128)(2,1)S(1)}, bf16[192,512]{1,0:T(8,128)(2,1)S(1)}, u32[]{:S(2)}, u32[]{:S(2)}) collective-permute-start(bf16[192,512]{1,0:T(8,128)(2,1)S(1)} %collective-permute-done.11.a_ref.refs_2_), channel_id=1, source_target_pairs={{0,4},{1,5},{2,3},{3,2},{4,0},{5,1},{6,7},{7,6},{8,12},{9,13},{10,... | collective-permute-start | bytes 589832 | tf_op jit(solution)/shard_map/ppermute | solution.py:331
  47.7 0.0 collective-permute-done.5.a_ref.refs_2_
  47.7 0.9 %collective-permute-start.6 = (bf16[192,512]{1,0:T(8,128)(2,1)S(1)}, bf16[192,512]{1,0:T(8,128)(2,1)S(1)}, u32[]{:S(2)}, u32[]{:S(2)}) collective-permute-start(bf16[192,512]{1,0:T(8,128)(2,1)S(1)} %collective-permute-done.5.a_ref.refs_2_), channel_id=1, source_target_pairs={{0,4},{1,5},{2,3},{3,2},{4,0},{5,1},{6,7},{7,6},{8,12},{9,13},{10,... | collective-permute-start | bytes 589832 | tf_op jit(solution)/shard_map/ppermute | solution.py:331
  48.5 0.0 collective-permute-done.4.refs_1_
  48.5 0.0 copy-done.4
  48.5 0.0 copy-done.5
  48.6 4.5 %attend.4.refs_8_.rest_0_ = f32[536,384]{1,0:T(8,128)S(1)} custom-call(bf16[192,512]{1,0:T(8,128)(2,1)S(1)} %get-tuple-element.13.refs_0_, bf16[192,512]{1,0:T(8,128)(2,1)S(1)} %collective-permute-done.4.refs_1_, bf16[192,512]{1,0:T(8,128)(2,1)S(1)} %settle.1.a_ref.own_ref.refs_2_, bf16[192,512]{1,0:T(8,128)(2,1)S(1)} %collective-permute-done.2.b_ref.first_ref.refs_3_, ...), custom_call_target="tpu_custom_call" | custom-call | flops 2000000000 | bytes 4000000 | tf_op jit(solution)/shard_map/attend/pallas_call | solution.py:232
  53.0 0.0 collective-permute-done.12.b_ref.refs_3_
  53.1 1.8 %collective-permute-start.13 = (bf16[384,512]{1,0:T(8,128)(2,1)S(1)}, bf16[384,512]{1,0:T(8,128)(2,1)S(1)}, u32[]{:S(2)}, u32[]{:S(2)}) collective-permute-start(bf16[384,512]{1,0:T(8,128)(2,1)S(1)} %join.7), channel_id=1, source_target_pairs={{0,1},{1,0},{2,6},{3,7},{4,5},{5,4},{6,2},{7,3},{8,9},{9,8},{10,14... | collective-permute-start | bytes 1179656 | tf_op jit(solution)/shard_map/ppermute | solution.py:331
  54.9 0.0 collective-permute-done.9.refs_4_
  54.9 4.6 %attend.5.rest_0_.refs_8_ = f32[536,384]{1,0:T(8,128)S(1)} custom-call(bf16[192,512]{1,0:T(8,128)(2,1)S(1)} %get-tuple-element.13.refs_0_, bf16[192,512]{1,0:T(8,128)(2,1)S(1)} %collective-permute-done.4.refs_1_, bf16[192,512]{1,0:T(8,128)(2,1)S(1)} %collective-permute-done.7.a_ref.refs_2_, ...), custom_call_target="tpu_custom_call", output_to_operand_aliasing={{}: (8, {})} | custom-call | flops 2000000000 | bytes 4000000 | tf_op jit(solution)/shard_map/attend/pallas_call | solution.py:232
  59.4 0.0 collective-permute-done.6.b_ref.refs_3_
  59.5 0.3 collective-permute-start.10
  59.8 1.1 %collective-permute-done.13.refs_4_ = bf16[384,512]{1,0:T(8,128)(2,1)S(1)} collective-permute-done((bf16[384,512]{1,0:T(8,128)(2,1)S(1)}, bf16[384,512]{1,0:T(8,128)(2,1)S(1)}, u32[]{:S(2)}, u32[]{:S(2)}) %collective-permute-start.13) | collective-permute-done | bytes 393248 | tf_op jit(solution)/shard_map/ppermute | solution.py:331
  60.9 4.6 %attend.6.refs_8_ = f32[536,384]{1,0:T(8,128)S(1)} custom-call(bf16[192,512]{1,0:T(8,128)(2,1)S(1)} %get-tuple-element.13.refs_0_, bf16[192,512]{1,0:T(8,128)(2,1)S(1)} %collective-permute-done.4.refs_1_, bf16[192,512]{1,0:T(8,128)(2,1)S(1)} %collective-permute-done.11.a_ref.refs_2_, ...), custom_call_target="tpu_custom_call", output_to_operand_aliasing={{}: (8, {})} | custom-call | flops 2000000000 | bytes 4000000 | tf_op jit(solution)/shard_map/attend/pallas_call | solution.py:232
  65.5 0.0 copy-start
  65.5 1.9 %collective-permute-done.10.refs_4_ = bf16[384,512]{1,0:T(8,128)(2,1)S(1)} collective-permute-done((bf16[384,512]{1,0:T(8,128)(2,1)S(1)}, bf16[384,512]{1,0:T(8,128)(2,1)S(1)}, u32[]{:S(2)}, u32[]{:S(2)}) %collective-permute-start.10) | collective-permute-done | bytes 393248 | tf_op jit(solution)/shard_map/ppermute | solution.py:331
  67.3 4.7 %attend.7.mine_ref = f32[536,384]{1,0:T(8,128)S(1)} custom-call(bf16[192,512]{1,0:T(8,128)(2,1)S(1)} %get-tuple-element.13.refs_0_, bf16[192,512]{1,0:T(8,128)(2,1)S(1)} %collective-permute-done.4.refs_1_, bf16[192,512]{1,0:T(8,128)(2,1)S(1)} %collective-permute-done.5.a_ref.refs_2_, ...), custom_call_target="tpu_custom_call", output_to_operand_aliasing={{}: (8, {})} | custom-call | flops 2000000000 | bytes 4000000 | tf_op jit(solution)/shard_map/attend/pallas_call | solution.py:232
  72.1 0.1 collective-permute-start.14
  72.2 1.9 %collective-permute-done.14.other_ref = f32[536,256]{1,0:T(8,128)S(1)} collective-permute-done((f32[536,256]{1,0:T(8,128)S(1)}, f32[536,256]{1,0:T(8,128)S(1)}, u32[]{:S(2)}, u32[]{:S(2)}) %collective-permute-start.14) | collective-permute-done | bytes 548896 | tf_op jit(solution)/shard_map/ppermute | solution.py:331
  74.1 0.9 %combine.1.attended_ref = bf16[208,512]{1,0:T(8,128)(2,1)S(1)} custom-call(f32[536,384]{1,0:T(8,128)S(1)} %attend.7.mine_ref, f32[536,256]{1,0:T(8,128)S(1)} %collective-permute-done.14.other_ref), custom_call_target="tpu_custom_call" | custom-call | tf_op jit(solution)/shard_map/combine/pallas_call | solution.py:275
  75.1 0.4 collective-permute-start.15
  75.5 0.0 copy-done
  75.5 0.3 own_branch.1.branch_ref
  75.7 6.7 %collective-permute-done.15.attended_ref = bf16[208,512]{1,0:T(8,128)(2,1)S(1)} collective-permute-done((bf16[208,512]{1,0:T(8,128)(2,1)S(1)}, bf16[208,512]{1,0:T(8,128)(2,1)S(1)}, u32[]{:S(2)}, u32[]{:S(2)}) %collective-permute-start.15) | collective-permute-done | bytes 213024 | tf_op jit(solution)/shard_map/ppermute | solution.py:331
  82.5 1.0 %finish.1 = bf16[256,512]{1,0:T(8,128)(2,1)} custom-call(f32[208,512]{1,0:T(8,128)S(1)} %own_branch.1.branch_ref, bf16[208,512]{1,0:T(8,128)(2,1)S(1)} %collective-permute-done.15.attended_ref, bf16[2,512,512]{2,1,0:T(8,128)(2,1)S(1)} %bitcast.7, bf16[192,512]{1,0:T(8,128)(2,1)S(1)} %get-tuple-element.14.normed_ref), custom_call_target="tpu_custom_call" | custom-call | tf_op jit(solution)/shard_map/finish/pallas_call | solution.py:309
  (5 shorter events, 0.1 us)
Async XLA Ops:
  0.0 42.5 %copy-start.3 = (f32[1024]{0:T(1024)S(1)}, f32[1024]{0:T(1024)}, u32[]{:S(2)}) copy-start(f32[1024]{0:T(1024)} %param.11) | copy-start | bytes 12292
  0.0 42.5 %copy-start.1 = (bf16[1024,512]{1,0:T(8,128)(2,1)S(1)}, bf16[1024,512]{1,0:T(8,128)(2,1)}, u32[]{:S(2)}) copy-start(bf16[1024,512]{1,0:T(8,128)(2,1)} %param.12) | copy-start | bytes 3145732
  0.0 48.5 %copy-start.4 = (bf16[1024,512]{1,0:T(8,128)(2,1)S(1)}, bf16[1024,512]{1,0:T(8,128)(2,1)}, u32[]{:S(2)}) copy-start(bf16[1024,512]{1,0:T(8,128)(2,1)} %param.13) | copy-start | bytes 3145732
  0.0 48.5 %copy-start.5 = (bf16[1024,512]{1,0:T(8,128)(2,1)S(1)}, bf16[1024,512]{1,0:T(8,128)(2,1)}, u32[]{:S(2)}) copy-start(bf16[1024,512]{1,0:T(8,128)(2,1)} %param.14) | copy-start | bytes 3145732
  8.4 11.1 %collective-permute-start = (f32[192,512]{1,0:T(8,128)}, f32[192,512]{1,0:T(8,128)S(1)}, u32[]{:S(2)}, u32[]{:S(2)}) collective-permute-start(f32[192,512]{1,0:T(8,128)} %get-tuple-element.11), channel_id=1, source_target_pairs={{0,30},{2,0},{4,2},{6,4},{8,6},{10,8},{12,10},{14,12},{16,14},{18,... | collective-permute-start | bytes 1179656 | tf_op jit(solution)/shard_map/ppermute | solution.py:385
  13.8 10.1 %collective-permute-start.1 = (f32[192,512]{1,0:T(8,128)}, f32[192,512]{1,0:T(8,128)S(1)}, u32[]{:S(2)}, u32[]{:S(2)}) collective-permute-start(f32[192,512]{1,0:T(8,128)} %get-tuple-element.12), channel_id=1, source_target_pairs={{0,2},{2,4},{4,6},{6,8},{8,10},{10,12},{12,14},{14,16},{16,18},{18... | collective-permute-start | bytes 1179656 | tf_op jit(solution)/shard_map/ppermute | solution.py:385
  24.0 1.0 %copy-start.2 = (f32[192,512]{1,0:T(8,128)S(1)}, f32[192,512]{1,0:T(8,128)}, u32[]{:S(2)}) copy-start(f32[192,512]{1,0:T(8,128)} %get-tuple-element.10.own_ref) | copy-start | bytes 1179652
  25.0 7.5 %collective-permute-start.2 = (bf16[192,512]{1,0:T(8,128)(2,1)S(1)}, bf16[192,512]{1,0:T(8,128)(2,1)S(1)}, u32[]{:S(2)}, u32[]{:S(2)}) collective-permute-start(bf16[192,512]{1,0:T(8,128)(2,1)S(1)} %settle.1.a_ref.own_ref.refs_2_), channel_id=1, source_target_pairs={{0,4},{1,5},{2,3},{3,2},{4,0},{5,1},{6,7},{7,6},{8,12},{9,13},{10,... | collective-permute-start | bytes 589832 | tf_op jit(solution)/shard_map/ppermute | solution.py:331
  25.1 9.1 %collective-permute-start.7 = (bf16[192,512]{1,0:T(8,128)(2,1)S(1)}, bf16[192,512]{1,0:T(8,128)(2,1)S(1)}, u32[]{:S(2)}, u32[]{:S(2)}) collective-permute-start(bf16[192,512]{1,0:T(8,128)(2,1)S(1)} %settle.1.a_ref.own_ref.refs_2_), channel_id=1, source_target_pairs={{0,8},{1,9},{2,10},{3,11},{4,12},{5,13},{6,14},{7,15},{8,0},{9,1},... | collective-permute-start | bytes 589832 | tf_op jit(solution)/shard_map/ppermute | solution.py:331
  32.5 10.0 %collective-permute-start.3 = (bf16[384,512]{1,0:T(8,128)(2,1)S(1)}, bf16[384,512]{1,0:T(8,128)(2,1)S(1)}, u32[]{:S(2)}, u32[]{:S(2)}) collective-permute-start(bf16[384,512]{1,0:T(8,128)(2,1)S(1)} %join.4), channel_id=1, source_target_pairs={{0,1},{1,0},{2,6},{3,7},{4,5},{5,4},{6,2},{7,3},{8,9},{9,8},{10,14... | collective-permute-start | bytes 1179656 | tf_op jit(solution)/shard_map/ppermute | solution.py:331
  34.2 7.6 %collective-permute-start.8 = (bf16[192,512]{1,0:T(8,128)(2,1)S(1)}, bf16[192,512]{1,0:T(8,128)(2,1)S(1)}, u32[]{:S(2)}, u32[]{:S(2)}) collective-permute-start(bf16[192,512]{1,0:T(8,128)(2,1)S(1)} %collective-permute-done.7.a_ref.refs_2_), channel_id=1, source_target_pairs={{0,4},{1,5},{2,3},{3,2},{4,0},{5,1},{6,7},{7,6},{8,12},{9,13},{10,... | collective-permute-start | bytes 589832 | tf_op jit(solution)/shard_map/ppermute | solution.py:331
  34.2 12.3 %collective-permute-start.11 = (bf16[192,512]{1,0:T(8,128)(2,1)S(1)}, bf16[192,512]{1,0:T(8,128)(2,1)S(1)}, u32[]{:S(2)}, u32[]{:S(2)}) collective-permute-start(bf16[192,512]{1,0:T(8,128)(2,1)S(1)} %settle.1.a_ref.own_ref.refs_2_), channel_id=1, source_target_pairs={{0,16},{1,17},{2,18},{3,19},{4,20},{5,21},{6,22},{7,23},{8,24},{9,... | collective-permute-start | bytes 589832 | tf_op jit(solution)/shard_map/ppermute | solution.py:331
  34.2 13.5 %collective-permute-start.5 = (bf16[192,512]{1,0:T(8,128)(2,1)S(1)}, bf16[192,512]{1,0:T(8,128)(2,1)S(1)}, u32[]{:S(2)}, u32[]{:S(2)}) collective-permute-start(bf16[192,512]{1,0:T(8,128)(2,1)S(1)} %settle.1.a_ref.own_ref.refs_2_), channel_id=1, source_target_pairs={{0,24},{1,25},{2,26},{3,27},{4,28},{5,29},{6,30},{7,31},{8,16},{9,... | collective-permute-start | bytes 589832 | tf_op jit(solution)/shard_map/ppermute | solution.py:331
  41.8 13.0 %collective-permute-start.9 = (bf16[384,512]{1,0:T(8,128)(2,1)S(1)}, bf16[384,512]{1,0:T(8,128)(2,1)S(1)}, u32[]{:S(2)}, u32[]{:S(2)}) collective-permute-start(bf16[384,512]{1,0:T(8,128)(2,1)S(1)} %join.5), channel_id=1, source_target_pairs={{0,1},{1,0},{2,6},{3,7},{4,5},{5,4},{6,2},{7,3},{8,9},{9,8},{10,14... | collective-permute-start | bytes 1179656 | tf_op jit(solution)/shard_map/ppermute | solution.py:331
  43.1 5.4 %collective-permute-start.4 = (bf16[192,512]{1,0:T(8,128)(2,1)S(1)}, bf16[192,512]{1,0:T(8,128)(2,1)S(1)}, u32[]{:S(2)}, u32[]{:S(2)}) collective-permute-start(bf16[192,512]{1,0:T(8,128)(2,1)S(1)} %get-tuple-element.13.refs_0_), channel_id=1, source_target_pairs={{0,2},{1,3},{2,0},{3,1},{4,6},{5,7},{6,4},{7,5},{8,10},{9,11},{10,... | collective-permute-start | bytes 589832 | tf_op jit(solution)/shard_map/ppermute | solution.py:331
  46.5 6.5 %collective-permute-start.12 = (bf16[192,512]{1,0:T(8,128)(2,1)S(1)}, bf16[192,512]{1,0:T(8,128)(2,1)S(1)}, u32[]{:S(2)}, u32[]{:S(2)}) collective-permute-start(bf16[192,512]{1,0:T(8,128)(2,1)S(1)} %collective-permute-done.11.a_ref.refs_2_), channel_id=1, source_target_pairs={{0,4},{1,5},{2,3},{3,2},{4,0},{5,1},{6,7},{7,6},{8,12},{9,13},{10,... | collective-permute-start | bytes 589832 | tf_op jit(solution)/shard_map/ppermute | solution.py:331
  47.7 11.8 %collective-permute-start.6 = (bf16[192,512]{1,0:T(8,128)(2,1)S(1)}, bf16[192,512]{1,0:T(8,128)(2,1)S(1)}, u32[]{:S(2)}, u32[]{:S(2)}) collective-permute-start(bf16[192,512]{1,0:T(8,128)(2,1)S(1)} %collective-permute-done.5.a_ref.refs_2_), channel_id=1, source_target_pairs={{0,4},{1,5},{2,3},{3,2},{4,0},{5,1},{6,7},{7,6},{8,12},{9,13},{10,... | collective-permute-start | bytes 589832 | tf_op jit(solution)/shard_map/ppermute | solution.py:331
  53.1 7.8 %collective-permute-start.13 = (bf16[384,512]{1,0:T(8,128)(2,1)S(1)}, bf16[384,512]{1,0:T(8,128)(2,1)S(1)}, u32[]{:S(2)}, u32[]{:S(2)}) collective-permute-start(bf16[384,512]{1,0:T(8,128)(2,1)S(1)} %join.7), channel_id=1, source_target_pairs={{0,1},{1,0},{2,6},{3,7},{4,5},{5,4},{6,2},{7,3},{8,9},{9,8},{10,14... | collective-permute-start | bytes 1179656 | tf_op jit(solution)/shard_map/ppermute | solution.py:331
  59.5 7.8 %collective-permute-start.10 = (bf16[384,512]{1,0:T(8,128)(2,1)S(1)}, bf16[384,512]{1,0:T(8,128)(2,1)S(1)}, u32[]{:S(2)}, u32[]{:S(2)}) collective-permute-start(bf16[384,512]{1,0:T(8,128)(2,1)S(1)} %join.6), channel_id=1, source_target_pairs={{0,1},{1,0},{2,6},{3,7},{4,5},{5,4},{6,2},{7,3},{8,9},{9,8},{10,14... | collective-permute-start | bytes 1179656 | tf_op jit(solution)/shard_map/ppermute | solution.py:331
  65.5 10.0 %copy-start = (bf16[1024,512]{1,0:T(8,128)(2,1)S(1)}, bf16[1024,512]{1,0:T(8,128)(2,1)}, u32[]{:S(2)}) copy-start(bf16[1024,512]{1,0:T(8,128)(2,1)} %param.15) | copy-start | bytes 3145732
  72.1 2.0 %collective-permute-start.14 = (f32[536,256]{1,0:T(8,128)S(1)}, f32[536,256]{1,0:T(8,128)S(1)}, u32[]{:S(2)}, u32[]{:S(2)}) collective-permute-start(f32[536,256]{1,0:T(8,128)S(1)} %slice.4), channel_id=1, source_target_pairs={{0,2},{1,3},{2,0},{3,1},{4,6},{5,7},{6,4},{7,5},{8,10},{9,11},{10,... | collective-permute-start | bytes 1646600 | tf_op jit(solution)/shard_map/ppermute | solution.py:331
  75.1 7.4 %collective-permute-start.15 = (bf16[208,512]{1,0:T(8,128)(2,1)S(1)}, bf16[208,512]{1,0:T(8,128)(2,1)S(1)}, u32[]{:S(2)}, u32[]{:S(2)}) collective-permute-start(bf16[208,512]{1,0:T(8,128)(2,1)S(1)} %combine.1.attended_ref), channel_id=1, source_target_pairs={{0,1},{1,0},{2,3},{3,2},{4,5},{5,4},{6,7},{7,6},{8,9},{9,8},{10,11... | collective-permute-start | bytes 638984 | tf_op jit(solution)/shard_map/ppermute | solution.py:331

commit v4 on v3

--- a/solution.py
+++ b/solution.py
@@ -39,88 +39,116 @@
     return lax.dot_general(a, b, (contract, ((), ())), preferred_element_type=F32)
 
 
-def pool_kernel(tiles, anchors_smem, anchors_ref, messages_ref, before_ref, own_ref, after_ref, sums):
-    step = pl.program_id(0)
+COPIES = 4
+GROUP = 8
+
+
+def pool_kernel(sides, anchors_hbm, messages_hbm, *refs):
+    outs = refs[: len(sides)]
+    anchors_smem, listed, anchors, messages, sems = refs[len(sides) :]
     partitions = lax.axis_size("ctx")
     center = lax.axis_index("ctx")
-
-    @pl.when(step == 0)
-    def _():
-        sums[...] = jnp.zeros_like(sums)
-
-    rows = lax.broadcasted_iota(jnp.int32, (LIVE_MAX, TILE), 0)
+    tiles = anchors.shape[0]
+    rows = tiles // COPIES * TILE
+    loads = [
+        pltpu.make_async_copy(anchors_hbm, anchors_smem, sems.at[COPIES]),
+        pltpu.make_async_copy(anchors_hbm, anchors, sems.at[COPIES + 1]),
+    ]
+    for part in range(COPIES):
+        at = pl.ds(part * rows, rows)
+        loads.append(pltpu.make_async_copy(messages_hbm.at[at], messages.at[at], sems.at[part]))
+    for load in loads:
+        load.start()
+    for out in outs:
+        out[...] = jnp.zeros_like(out)
+    slots = lax.broadcasted_iota(jnp.int32, (LIVE_MAX, TILE), 0)
+    loads[0].wait()
+    counts = [jnp.int32(0)] * len(sides)
     for tile in range(tiles):
-        index = step * tiles + tile
-        owner = anchors_smem[index * TILE] // ANCH_DEV
-        side = lax.rem(owner - center + 1 + partitions, partitions)
-        slot = anchors_ref[pl.ds(index, 1), :] % ANCH_DEV
-        onehot = jnp.where(rows == slot, 1.0, 0.0).astype(BF16)
-        part = dot(onehot, messages_ref[tile * TILE : (tile + 1) * TILE, :])
-        sums[side] += part
-
-    @pl.when(step == pl.num_programs(0) - 1)
-    def _():
-        before_ref[...] = sums[0]
-        own_ref[...] = sums[1]
-        after_ref[...] = sums[2]
-
-
-def pool(messages, node_anchor):
+        side = lax.rem(anchors_smem[tile, 0] // ANCH_DEV - center + 1 + partitions, partitions)
+        for index, name in enumerate(sides):
+            ahead = 1 if name == "own" else 2 * lax.rem(center, 2)
+            which = 2 - ahead if name == "near" else ahead
+            listed[index, counts[index]] = tile
+            counts[index] = counts[index] + jnp.where(side == which, 1, 0)
+    for load in loads[1:]:
+        load.wait()
+    for index, out in enumerate(outs):
+
+        def add(group, unused, index=index, out=out):
+            onehots, parts = [], []
+            for at in range(GROUP):
+                place = group * GROUP + at
+                wanted = place < counts[index]
+                tile = jnp.where(wanted, listed[index, jnp.minimum(place, tiles - 1)], 0)
+                slot = jnp.where(wanted, anchors[pl.ds(tile, 1), :] % ANCH_DEV, -1)
+                onehots.append(jnp.where(slots == slot, 1.0, 0.0).astype(BF16))
+                parts.append(messages[pl.ds(pl.multiple_of(tile * TILE, TILE), TILE), :])
+            out[...] += dot(jnp.concatenate(onehots, axis=1), jnp.concatenate(parts, axis=0))
+            return unused
+
+        lax.fori_loop(0, (counts[index] + GROUP - 1) // GROUP, add, 0)
+
+
+def pool(messages, node_anchor, sides):
     nodes, channels = messages.shape
-    steps = 8
-    tiles = nodes // TILE // steps
-    shape = jax.ShapeDtypeStruct((LIVE_MAX, channels), F32)
-    whole = pl.BlockSpec((LIVE_MAX, channels), lambda i, a: (0, 0))
-    return pl.pallas_call(
-        functools.partial(pool_kernel, tiles),
-        grid_spec=pltpu.PrefetchScalarGridSpec(
-            num_scalar_prefetch=1,
-            grid=(steps,),
-            in_specs=[
-                pl.BlockSpec((nodes // TILE, TILE), lambda i, a: (0, 0)),
-                pl.BlockSpec((tiles * TILE, channels), lambda i, a: (i, 0)),
-            ],
-            out_specs=[whole] * 3,
-            scratch_shapes=[pltpu.VMEM((3, LIVE_MAX, channels), F32)],
-        ),
-        out_shape=[shape] * 3,
+    tiles = nodes // TILE
+    hbm = pl.BlockSpec(memory_space=pltpu.MemorySpace.HBM)
+    return pl.pallas_call(
+        functools.partial(pool_kernel, sides),
+        in_specs=[hbm] * 2,
+        out_specs=vmem(len(sides)),
+        scratch_shapes=[
+            pltpu.SMEM((tiles, TILE), jnp.int32),
+            pltpu.SMEM((len(sides), tiles + 1), jnp.int32),
+            pltpu.VMEM((tiles, TILE), jnp.int32),
+            pltpu.VMEM((nodes, channels), BF16),
+            pltpu.SemaphoreType.DMA((COPIES + 2,)),
+        ],
+        out_shape=[jax.ShapeDtypeStruct((LIVE_MAX, channels), F32)] * len(sides),
         compiler_params=params(60),
+        cost_estimate=pl.CostEstimate(flops=10**9, bytes_accessed=5 * 10**6, transcendentals=0),
         name="pool",
-    )(node_anchor, node_anchor.reshape(nodes // TILE, TILE), messages)
-
-
-def settle_kernel(count_ref, own_ref, before_ref, after_ref, out_ref):
-    total = own_ref[...] + before_ref[...] + after_ref[...]
-    slot = lax.broadcasted_iota(jnp.int32, total.shape, 0)
-    out_ref[...] = jnp.where(slot < count_ref[0], total, MARK).astype(BF16)
+    )(node_anchor.reshape(tiles, TILE), messages)
+
+
+def after_kernel(a_ref, *rest):
+    rest[-1][...] = a_ref[...]
+
+
+def after(a, *others, cost=1):
+    return pl.pallas_call(
+        after_kernel,
+        in_specs=vmem(1) + [pl.BlockSpec(memory_space=pl.ANY)] * len(others),
+        out_specs=pl.BlockSpec(memory_space=pltpu.VMEM),
+        out_shape=jax.ShapeDtypeStruct(a.shape, a.dtype),
+        compiler_params=params(),
+        cost_estimate=pl.CostEstimate(flops=cost, bytes_accessed=1, transcendentals=0),
+        name="after",
+    )(a, *others)
 
 
 def settle(count, own, before, after):
-    return pl.pallas_call(
-        settle_kernel,
-        in_specs=[pl.BlockSpec(memory_space=pltpu.SMEM)] + vmem(3),
-        out_specs=pl.BlockSpec(memory_space=pltpu.VMEM),
-        out_shape=jax.ShapeDtypeStruct(own.shape, BF16),
-        compiler_params=params(),
-        name="settle",
-    )(count, own, before, after)
-
-
-def join_kernel(a_ref, b_ref, *rest):
+    slot = lax.broadcasted_iota(jnp.int32, own.shape, 0)
+    return jnp.where(slot < count, own + before + after, MARK).astype(BF16)
+
+
+def join_kernel(a_ref, b_ref, out_ref):
     rows = a_ref.shape[0]
-    rest[-1][:rows, :] = a_ref[...]
-    rest[-1][rows:, :] = b_ref[...]
-
-
-def join(a, b, *after):
+    out_ref[:rows, :] = a_ref[...]
+    out_ref[rows:, :] = b_ref[...]
+
+
+def join(a, b, cost=1):
     return pl.pallas_call(
         join_kernel,
-        in_specs=vmem(2) + [pl.BlockSpec(memory_space=pl.ANY)] * len(after),
+        in_specs=vmem(2),
         out_specs=pl.BlockSpec(memory_space=pltpu.VMEM),
         out_shape=jax.ShapeDtypeStruct((a.shape[0] + b.shape[0], a.shape[1]), a.dtype),
         compiler_params=params(),
+        cost_estimate=pl.CostEstimate(flops=cost, bytes_accessed=1, transcendentals=0),
         name="join",
-    )(a, b, *after)
+    )(a, b)
 
 
 def normalise(mine, other, gain_ref, x):
@@ -140,40 +168,40 @@
     return (dot(mine, w_ref[x]) + dot(other, w_ref[1 - x])).astype(BF16)
 
 
-def query_kernel(own_ref, first_ref, second_ref, gain_ref, wq_ref, query_ref, normed_ref):
+def query_kernel(first_ref, second_ref, gain_ref, wq_ref, query_ref, normed_ref):
     core = lax.rem(lax.axis_index("ctx"), 2)
     x = lax.axis_index("head")
-    other = jnp.where(core == 0, second_ref[:LIVE_MAX, :], first_ref[...])
-    mine, other, unused = normalise(own_ref[...], other, gain_ref, x)
+    other = jnp.where(core == 0, second_ref[:LIVE_MAX, :], first_ref[LIVE_MAX:, :])
+    mine, other, unused = normalise(first_ref[:LIVE_MAX, :], other, gain_ref, x)
     query_ref[...] = project(mine, other, wq_ref, x)
     normed_ref[...] = mine
 
 
-def make_queries(own, first, second, gain, wq):
-    channels = own.shape[1]
+def make_queries(first, second, gain, wq):
+    channels = first.shape[1]
     return pl.pallas_call(
         query_kernel,
-        in_specs=vmem(5),
+        in_specs=vmem(4),
         out_specs=vmem(2),
         out_shape=[jax.ShapeDtypeStruct((LIVE_MAX, channels), BF16)] * 2,
         compiler_params=params(),
-        cost_estimate=pl.CostEstimate(flops=4 * 10**8, bytes_accessed=2 * 10**6, transcendentals=0),
+        cost_estimate=pl.CostEstimate(flops=1, bytes_accessed=1, transcendentals=0),
         name="queries",
-    )(own, first, second, gain, wq)
+    )(first, second, gain, wq)
 
 
 def attend_kernel(first_call, *refs):
     if first_call:
-        qm, qr, own_ref, first_ref, second_ref, gain_ref, wk_ref, wv_ref, out_ref = refs
+        qm, qr, first_ref, second_ref, gain_ref, wk_ref, wv_ref, out_ref = refs
         state_ref = None
     else:
-        qm, qr, own_ref, first_ref, second_ref, gain_ref, wk_ref, wv_ref, state_ref, out_ref = refs
+        qm, qr, first_ref, second_ref, gain_ref, wk_ref, wv_ref, state_ref, out_ref = refs
     core = lax.rem(lax.axis_index("ctx"), 2)
     x = lax.axis_index("head")
-    channels = own_ref.shape[1]
+    channels = first_ref.shape[1]
     heads = channels // HD
-    one, two = first_ref[...], second_ref[:LIVE_MAX, :]
-    mine = jnp.concatenate([own_ref[...], jnp.where(core == 0, one, two)], axis=0)
+    one, two = first_ref[LIVE_MAX:, :], second_ref[:LIVE_MAX, :]
+    mine = jnp.concatenate([first_ref[:LIVE_MAX, :], jnp.where(core == 0, one, two)], axis=0)
     other = jnp.concatenate([jnp.where(core == 0, two, one), second_ref[LIVE_MAX:, :]], axis=0)
     mine, other, dead = normalise(mine, other, gain_ref, x)
     keys = project(mine, other, wk_ref, x)
@@ -194,40 +222,49 @@
 
     lane_k = lax.broadcasted_iota(jnp.int32, (keys.shape[0], 128), 1)
     lane_q = lax.broadcasted_iota(jnp.int32, (QROWS, 128), 1)
-    for pair in range(heads // 2):
+
+    def score(head):
+        pair, side = head // 2, head % 2
         at = slice(pair * 128, (pair + 1) * 128)
-        query = jnp.concatenate(
-            [qm[:, at], qr[128:, at], qr[:128, at]],
-            axis=0,
-        )
-        for side in range(2):
-            head = 2 * pair + side
-            hot = jnp.where(lane_q == (1 - side) * HD, 1.0, 0.0).astype(BF16)
-            q = jnp.where((lane_q // HD) == side, query, hot)
-            k = jnp.where((lane_k // HD) == side, keys[:, at], shut)
-            scores = dot(k, q, ((1,), (1,)))
-            top = jnp.max(scores, axis=0, keepdims=True)
-            at_top = slice(channels + head, channels + head + 1)
-            at_total = slice(channels + heads + head, channels + heads + head + 1)
-            if not first_call:
-                old_top = state_ref[at_top, :QROWS]
-                top = jnp.maximum(top, old_top)
-                fade = jnp.exp2((old_top - top) * RATE)
-            weights = jnp.exp2((scores - top) * RATE)
-            total = jnp.sum(weights, axis=0, keepdims=True)
-            at_head = slice(head * HD, (head + 1) * HD)
-            mixed = dot(values[at_head], weights.astype(BF16))
-            if not first_call:
-                total = total + state_ref[at_total, :QROWS] * fade
-                mixed = mixed + state_ref[at_head, :QROWS] * fade
-            out_ref[at_head, :QROWS] = mixed
-            out_ref[at_top, :QROWS] = top
-            out_ref[at_total, :QROWS] = total
-
-
-def attend(qm, qr, own, first, second, gain, wk, wv, state=None):
-    channels = own.shape[1]
-    args = [qm, qr, own, first, second, gain, wk, wv] + ([] if state is None else [state])
+        query = jnp.concatenate([qm[:, at], qr[128:, at], qr[:128, at]], axis=0)
+        hot = jnp.where(lane_q == (1 - side) * HD, 1.0, 0.0).astype(BF16)
+        q = jnp.where((lane_q // HD) == side, query, hot)
+        k = jnp.where((lane_k // HD) == side, keys[:, at], shut)
+        return dot(k, q, ((1,), (1,)))
+
+    def weigh(head, scores):
+        top = jnp.max(scores, axis=0, keepdims=True)
+        at_top = slice(channels + head, channels + head + 1)
+        at_total = slice(channels + heads + head, channels + heads + head + 1)
+        fade = None
+        if not first_call:
+            old_top = state_ref[at_top, :]
+            top = jnp.maximum(top, old_top)
+            fade = jnp.exp2((old_top - top) * RATE)
+        weights = jnp.exp2((scores - top) * RATE)
+        total = jnp.sum(weights, axis=0, keepdims=True)
+        if not first_call:
+            total = total + state_ref[at_total, :] * fade
+        out_ref[at_top, :] = top
+        out_ref[at_total, :] = total
+        return weights.astype(BF16), fade
+
+    def mix(head, weights, fade):
+        at = slice(head * HD, (head + 1) * HD)
+        mixed = dot(values[at], weights)
+        if not first_call:
+            mixed = mixed + state_ref[at, :] * fade
+        out_ref[at, :] = mixed
+
+    scores = [score(head) for head in range(heads)]
+    weights = [weigh(head, scores[head]) for head in range(heads)]
+    for head in range(heads):
+        mix(head, *weights[head])
+
+
+def attend(qm, qr, first, second, gain, wk, wv, state=None):
+    channels = first.shape[1]
+    args = [qm, qr, first, second, gain, wk, wv] + ([] if state is None else [state])
     keys = 2 * LIVE_MAX
     return pl.pallas_call(
         functools.partial(attend_kernel, state is None),
@@ -237,7 +274,7 @@
         input_output_aliases={} if state is None else {len(args) - 1: 0},
         compiler_params=params(),
         cost_estimate=pl.CostEstimate(
-            flops=2 * 10**9, bytes_accessed=4 * 10**6, transcendentals=QROWS * keys * channels // HD
+            flops=1, bytes_accessed=1, transcendentals=0
         ),
         name="attend",
     )(*args)
@@ -357,21 +394,27 @@
 
 def block_plan(messages, node_anchor, anchor_count, norm_gain, w_query, w_key, w_value, w_out):
     channels = messages.shape[1]
-    before, own, after = pool(messages, node_anchor)
-    from_next = shift(before, -1)
-    from_previous = shift(after, 1)
-    mine = settle(anchor_count, own, from_next, from_previous)
+    far, near = pool(messages, node_anchor, ("far", "near"))
+    (own,) = pool(messages, node_anchor, ("own",))
+    from_far = lax.ppermute(far, "ctx", [(i, (i + (1 if i % 2 else 15)) % 16) for i in range(16)])
+    from_near = send(near, across_core)
+    mine = settle(anchor_count, own, from_far, from_near)
     gain = norm_gain.reshape(2, 1, channels)
     wq, wk, wv, wo = halves(w_query), halves(w_key), halves(w_value), halves(w_out)
-    slices = [mine] + [send(mine, across_z(step)) for step in (1, 2, 3)]
-    states = []
-    for index, rows in enumerate(slices):
-        first = send(rows, across_first)
-        second = send(join(rows, first, *states[: max(index - 1, 0)][-1:]), across_second)
-        if index == 0:
-            query, normed = make_queries(rows, first, second, gain, wq)
-            swapped = send(query, across_core)
-        states.append(attend(query, swapped, rows, first, second, gain, wk, wv, *states[-1:]))
+    far_rows = [send(mine, across_z(step)) for step in (2, 3)]
+    first = join(mine, send(mine, across_first))
+    second = send(first, across_second)
+    query, normed = make_queries(first, second, gain, wq)
+    swapped = send(query, across_core)
+    beside = [send(first, across_z(1)), send(second, across_z(1))]
+    state = attend(query, swapped, first, second, gain, wk, wv)
+    states = [state, attend(query, swapped, *beside, gain, wk, wv, state)]
+    plane = first
+    for index, rows in enumerate(far_rows):
+        rows = after(rows, plane, cost=2*10**10)
+        first = join(rows, send(rows, across_first), cost=10**10)
+        second = send(first, across_second)
+        states.append(attend(query, swapped, first, second, gain, wk, wv, states[-1]))
     state = states[-1]
     other = send(state[:, QROWS - SENT :], across_core)
     attended = combine(state, other)

time: 83.8 us -> 74.5 us (0.89)
  waiting for transfers between devices: 37.6 us -> 27.9 us
  Pallas kernels: 29.7 us -> 23.1 us
  starting transfers between devices: 14.3 us -> 20.5 us
  other arithmetic: 0 us -> 1.1 us
  local copies, waits for them, and re-layouts: 1.05 us -> 0.07 us
    ppermute x2 -> x1, waiting for transfers between devices: 9.45 us -> 1.34 us  [block_plan(): lax.ppermute(far, 'ctx', [(i, (i + (1 if i % 2 else 15)) % 16) for i in r...]
    pallas_call x4, Pallas kernels: 18.3 us -> 12.1 us  [attend(): pl.pallas_call(functools.partial(attend_kernel, state is None), in_specs=...]
    ppermute x14, starting transfers between devices: 8.81 us -> 15 us  [send(): return lax.ppermute(array, ALL, pairs(move))]
    ppermute x14, waiting for transfers between devices: 28.2 us -> 26.5 us  [send(): return lax.ppermute(array, ALL, pairs(move))]
    convert_element_type x0 -> x1, other arithmetic: none -> 1.09 us  [settle(): return jnp.where(slot < count, own + before + after, MARK).astype(BF16)]
    unnamed x12 -> x10, local copies, waits for them, and re-layouts: 1.02 us -> 0.03 us
    pallas_call x7 -> x8, Pallas kernels: 9.15 us -> 8.74 us  [the longest x2 8.03 us: pool(): pl.pallas_call(functools.partial(pool_kernel, sides), in_specs=[hbm] * 2,...]
    ppermute x2 -> x1, starting transfers between devices: 5.46 us -> 5.51 us  [block_plan(): lax.ppermute(far, 'ctx', [(i, (i + (1 if i % 2 else 15)) % 16) for i in r...]
  transfers between devices with their start and end apart: 16 -> 15, of which waited for: 9 -> 8; matrix products, arithmetic and copies ran while one was open for 0% -> 0% of each run, Pallas kernels for 17% -> 19%
where the time goes in v4:
time: 74.5 us; the launch traced here: 73.5 us
  waiting for transfers between devices  27.9 us (37%)
  Pallas kernels  23.1 us (31%)
  starting transfers between devices  20.5 us (28%)
  other arithmetic  1.1 us (1%)
  between operations  0.87 us (1%)
    ppermute x14, waiting for transfers between devices, send(): return lax.ppermute(array, ALL, pairs(move))  26.5 us
    ppermute x14, starting transfers between devices, send(): return lax.ppermute(array, ALL, pairs(move))  15 us
    pallas_call x4, Pallas kernels, attend(): pl.pallas_call(functools.partial(attend_kernel, state is None), in_specs=...  12.1 us
    pallas_call x2, Pallas kernels, pool(): pl.pallas_call(functools.partial(pool_kernel, sides), in_specs=[hbm] * 2,...  8.03 us
    ppermute x1, starting transfers between devices, block_plan(): lax.ppermute(far, 'ctx', [(i, (i + (1 if i % 2 else 15)) % 16) for i in r...  5.51 us
  transfers between devices with their start and end apart: 15, of which 8 were waited for; matrix products, arithmetic and copies ran while one was open for 0% of the time, Pallas kernels for 19%

profile of v4, /device:TPU:0, one launch (start us, length us, event | category | flops | bytes accessed | tf_op | source)
XLA Modules:
  0.0 73.5 jit_solution(7129500979398171599)
XLA Ops:
  0.0 4.3 %pool.3 = (f32[192,512]{1,0:T(8,128)}, f32[192,512]{1,0:T(8,128)}) custom-call(s32[32,128]{1,0:T(8,128)} %bitcast.24, bf16[4096,512]{1,0:T(8,128)(2,1)} %messages_hbm.3), custom_call_target="tpu_custom_call" | custom-call | flops 1000000000 | bytes 5000000 | tf_op jit(solution)/shard_map/pool/pallas_call | solution.py:97
  4.3 5.5 %collective-permute-start = (f32[192,512]{1,0:T(8,128)}, f32[192,512]{1,0:T(8,128)S(1)}, u32[]{:S(2)}, u32[]{:S(2)}) collective-permute-start(f32[192,512]{1,0:T(8,128)} %get-tuple-element.9), channel_id=1, source_target_pairs={{0,30},{2,4},{4,2},{6,8},{8,6},{10,12},{12,10},{14,16},{16,14},{18... | collective-permute-start | bytes 1179656 | tf_op jit(solution)/shard_map/ppermute | solution.py:399
  9.8 0.0 collective-permute-start.1
  10.4 3.8 %pool.2 = f32[192,512]{1,0:T(8,128)} custom-call(s32[32,128]{1,0:T(8,128)} %bitcast.25, bf16[4096,512]{1,0:T(8,128)(2,1)} %messages_hbm.3), custom_call_target="tpu_custom_call" | custom-call | flops 1000000000 | bytes 5000000 | tf_op jit(solution)/shard_map/pool/pallas_call | solution.py:97
  14.2 1.3 %collective-permute-done = f32[192,512]{1,0:T(8,128)S(1)} collective-permute-done((f32[192,512]{1,0:T(8,128)}, f32[192,512]{1,0:T(8,128)S(1)}, u32[]{:S(2)}, u32[]{:S(2)}) %collective-permute-start) | collective-permute-done | bytes 393248 | tf_op jit(solution)/shard_map/ppermute | solution.py:399
  15.6 0.0 collective-permute-done.1
  15.6 1.1 %select_convert_fusion.a_ref = bf16[192,512]{1,0:T(8,128)(2,1)S(1)} fusion(f32[192,512]{1,0:T(8,128)S(1)} %collective-permute-done.1, f32[192,512]{1,0:T(8,128)} %pool.2, f32[192,512]{1,0:T(8,128)S(1)} %collective-permute-done, pred[192]{0:T(512)(128)(4,1)S(1)} %iota_compare_fusion), kind=kLoop, calls=%fused_computation | loop fusion | flops 393216 | bytes 1376448 | tf_op jit(solution)/shard_map/convert_element_type | solution.py:133
  16.7 3.4 %collective-permute-start.2 = (bf16[192,512]{1,0:T(8,128)(2,1)S(1)}, bf16[192,512]{1,0:T(8,128)(2,1)S(1)}, u32[]{:S(2)}, u32[]{:S(2)}) collective-permute-start(bf16[192,512]{1,0:T(8,128)(2,1)S(1)} %select_convert_fusion.a_ref), channel_id=1, source_target_pairs={{0,4},{1,5},{2,3},{3,2},{4,0},{5,1},{6,7},{7,6},{8,12},{9,13},{10,... | collective-permute-start | bytes 589832 | tf_op jit(solution)/shard_map/ppermute | solution.py:368
  20.1 2.6 %collective-permute-start.8 = (bf16[192,512]{1,0:T(8,128)(2,1)S(1)}, bf16[192,512]{1,0:T(8,128)(2,1)S(1)}, u32[]{:S(2)}, u32[]{:S(2)}) collective-permute-start(bf16[192,512]{1,0:T(8,128)(2,1)S(1)} %select_convert_fusion.a_ref), channel_id=1, source_target_pairs={{0,16},{1,17},{2,18},{3,19},{4,20},{5,21},{6,22},{7,23},{8,24},{9,... | collective-permute-start | bytes 589832 | tf_op jit(solution)/shard_map/ppermute | solution.py:368
  22.7 1.0 %collective-permute-start.5 = (bf16[192,512]{1,0:T(8,128)(2,1)S(1)}, bf16[192,512]{1,0:T(8,128)(2,1)S(1)}, u32[]{:S(2)}, u32[]{:S(2)}) collective-permute-start(bf16[192,512]{1,0:T(8,128)(2,1)S(1)} %select_convert_fusion.a_ref), channel_id=1, source_target_pairs={{0,24},{1,25},{2,26},{3,27},{4,28},{5,29},{6,30},{7,31},{8,16},{9,... | collective-permute-start | bytes 589832 | tf_op jit(solution)/shard_map/ppermute | solution.py:368
  23.7 0.1 collective-permute-done.2.b_ref
  23.8 1.6 %collective-permute-start.3 = (bf16[384,512]{1,0:T(8,128)(2,1)S(1)}, bf16[384,512]{1,0:T(8,128)(2,1)S(1)}, u32[]{:S(2)}, u32[]{:S(2)}) collective-permute-start(bf16[384,512]{1,0:T(8,128)(2,1)S(1)} %join.3.first_ref.rest_0_.refs_2_), channel_id=1, source_target_pairs={{0,1},{1,0},{2,6},{3,7},{4,5},{5,4},{6,2},{7,3},{8,9},{9,8},{10,14... | collective-permute-start | bytes 1179656 | tf_op jit(solution)/shard_map/ppermute | solution.py:368
  25.3 1.2 %collective-permute-start.11 = (bf16[384,512]{1,0:T(8,128)(2,1)S(1)}, bf16[384,512]{1,0:T(8,128)(2,1)S(1)}, u32[]{:S(2)}, u32[]{:S(2)}) collective-permute-start(bf16[384,512]{1,0:T(8,128)(2,1)S(1)} %join.3.first_ref.rest_0_.refs_2_), channel_id=1, source_target_pairs={{0,8},{1,9},{2,10},{3,11},{4,12},{5,13},{6,14},{7,15},{8,0},{9,1},... | collective-permute-start | bytes 1179656 | tf_op jit(solution)/shard_map/ppermute | solution.py:368
  26.5 10.4 %collective-permute-done.8.a_ref = bf16[192,512]{1,0:T(8,128)(2,1)S(1)} collective-permute-done((bf16[192,512]{1,0:T(8,128)(2,1)S(1)}, bf16[192,512]{1,0:T(8,128)(2,1)S(1)}, u32[]{:S(2)}, u32[]{:S(2)}) %collective-permute-start.8) | collective-permute-done | bytes 196640 | tf_op jit(solution)/shard_map/ppermute | solution.py:368
  37.0 0.1 collective-permute-start.9
  37.1 0.0 collective-permute-done.5.a_ref
  37.1 2.1 %collective-permute-start.6 = (bf16[192,512]{1,0:T(8,128)(2,1)S(1)}, bf16[192,512]{1,0:T(8,128)(2,1)S(1)}, u32[]{:S(2)}, u32[]{:S(2)}) collective-permute-start(bf16[192,512]{1,0:T(8,128)(2,1)S(1)} %after.2.a_ref), channel_id=1, source_target_pairs={{0,4},{1,5},{2,3},{3,2},{4,0},{5,1},{6,7},{7,6},{8,12},{9,13},{10,... | collective-permute-start | bytes 589832 | tf_op jit(solution)/shard_map/ppermute | solution.py:368
  39.2 3.7 %collective-permute-done.9.b_ref = bf16[192,512]{1,0:T(8,128)(2,1)S(1)} collective-permute-done((bf16[192,512]{1,0:T(8,128)(2,1)S(1)}, bf16[192,512]{1,0:T(8,128)(2,1)S(1)}, u32[]{:S(2)}, u32[]{:S(2)}) %collective-permute-start.9) | collective-permute-done | bytes 196640 | tf_op jit(solution)/shard_map/ppermute | solution.py:368
  42.9 0.0 copy-start.3
  42.9 0.0 copy-start.4
  43.0 0.0 copy-start
  43.0 0.0 copy-start.1
  43.0 0.6 collective-permute-start.10
  43.6 0.0 collective-permute-done.3.second_ref.refs_3_
  43.6 0.0 collective-permute-start.12
  43.6 3.5 %collective-permute-done.6.b_ref = bf16[192,512]{1,0:T(8,128)(2,1)S(1)} collective-permute-done((bf16[192,512]{1,0:T(8,128)(2,1)S(1)}, bf16[192,512]{1,0:T(8,128)(2,1)S(1)}, u32[]{:S(2)}, u32[]{:S(2)}) %collective-permute-start.6) | collective-permute-done | bytes 196640 | tf_op jit(solution)/shard_map/ppermute | solution.py:368
  47.1 0.6 collective-permute-start.7
  47.7 0.0 copy-done.3
  47.7 0.0 copy-done.4
  47.8 0.6 queries.1
  48.4 0.1 collective-permute-start.4
  48.4 1.4 %collective-permute-done.4.refs_1_ = bf16[192,512]{1,0:T(8,128)(2,1)S(1)} collective-permute-done((bf16[192,512]{1,0:T(8,128)(2,1)S(1)}, bf16[192,512]{1,0:T(8,128)(2,1)S(1)}, u32[]{:S(2)}, u32[]{:S(2)}) %collective-permute-start.4) | collective-permute-done | bytes 196640 | tf_op jit(solution)/shard_map/ppermute | solution.py:368
  49.9 0.0 copy-done
  49.9 0.0 copy-done.1
  49.9 2.9 %attend.4.refs_7_ = f32[536,384]{1,0:T(8,128)S(1)} custom-call(bf16[192,512]{1,0:T(8,128)(2,1)S(1)} %get-tuple-element.11.refs_0_, bf16[192,512]{1,0:T(8,128)(2,1)S(1)} %collective-permute-done.4.refs_1_, bf16[384,512]{1,0:T(8,128)(2,1)S(1)} %join.3.first_ref.rest_0_.refs_2_, bf16[384,512]{1,0:T(8,128)(2,1)S(1)} %collective-permute-done.3.second_ref.refs_3_, ...), custom_call_target="tpu_custom_call" | custom-call | flops 1 | bytes 1 | tf_op jit(solution)/shard_map/attend/pallas_call | solution.py:269
  52.8 0.0 collective-permute-done.11.refs_2_
  52.8 0.0 collective-permute-done.12.refs_3_
  52.8 3.1 %attend.5.refs_7_ = f32[536,384]{1,0:T(8,128)S(1)} custom-call(bf16[192,512]{1,0:T(8,128)(2,1)S(1)} %get-tuple-element.11.refs_0_, bf16[192,512]{1,0:T(8,128)(2,1)S(1)} %collective-permute-done.4.refs_1_, bf16[384,512]{1,0:T(8,128)(2,1)S(1)} %collective-permute-done.11.refs_2_, ...), custom_call_target="tpu_custom_call", output_to_operand_aliasing={{}: (7, {})} | custom-call | flops 1 | bytes 1 | tf_op jit(solution)/shard_map/attend/pallas_call | solution.py:269
  55.9 0.0 collective-permute-done.10.refs_3_
  55.9 3.1 %attend.6.refs_7_ = f32[536,384]{1,0:T(8,128)S(1)} custom-call(bf16[192,512]{1,0:T(8,128)(2,1)S(1)} %get-tuple-element.11.refs_0_, bf16[192,512]{1,0:T(8,128)(2,1)S(1)} %collective-permute-done.4.refs_1_, bf16[384,512]{1,0:T(8,128)(2,1)S(1)} %join.5.refs_2_, bf16[384,512]{1,0:T(8,128)(2,1)S(1)} %collective-permute-done.10.refs_3_, ...), custom_call_target="tpu_custom_call", output_to_operand_aliasing={{}: (7, {})} | custom-call | flops 1 | bytes 1 | tf_op jit(solution)/shard_map/attend/pallas_call | solution.py:269
  59.0 0.0 copy-start.2
  59.0 0.0 collective-permute-done.7.refs_3_
  59.0 3.1 %attend.7.mine_ref = f32[536,384]{1,0:T(8,128)S(1)} custom-call(bf16[192,512]{1,0:T(8,128)(2,1)S(1)} %get-tuple-element.11.refs_0_, bf16[192,512]{1,0:T(8,128)(2,1)S(1)} %collective-permute-done.4.refs_1_, bf16[384,512]{1,0:T(8,128)(2,1)S(1)} %join.4.refs_2_, bf16[384,512]{1,0:T(8,128)(2,1)S(1)} %collective-permute-done.7.refs_3_, ...), custom_call_target="tpu_custom_call", output_to_operand_aliasing={{}: (7, {})} | custom-call | flops 1 | bytes 1 | tf_op jit(solution)/shard_map/attend/pallas_call | solution.py:269
  62.1 0.2 collective-permute-start.13
  62.4 1.8 %collective-permute-done.13.other_ref = f32[536,256]{1,0:T(8,128)S(1)} collective-permute-done((f32[536,256]{1,0:T(8,128)S(1)}, f32[536,256]{1,0:T(8,128)S(1)}, u32[]{:S(2)}, u32[]{:S(2)}) %collective-permute-start.13) | collective-permute-done | bytes 548896 | tf_op jit(solution)/shard_map/ppermute | solution.py:368
  64.2 0.9 %combine.1.attended_ref = bf16[208,512]{1,0:T(8,128)(2,1)S(1)} custom-call(f32[536,384]{1,0:T(8,128)S(1)} %attend.7.mine_ref, f32[536,256]{1,0:T(8,128)S(1)} %collective-permute-done.13.other_ref), custom_call_target="tpu_custom_call" | custom-call | tf_op jit(solution)/shard_map/combine/pallas_call | solution.py:312
  65.1 1.6 %collective-permute-start.14 = (bf16[208,512]{1,0:T(8,128)(2,1)S(1)}, bf16[208,512]{1,0:T(8,128)(2,1)S(1)}, u32[]{:S(2)}, u32[]{:S(2)}) collective-permute-start(bf16[208,512]{1,0:T(8,128)(2,1)S(1)} %combine.1.attended_ref), channel_id=1, source_target_pairs={{0,1},{1,0},{2,3},{3,2},{4,5},{5,4},{6,7},{7,6},{8,9},{9,8},{10,11... | collective-permute-start | bytes 638984 | tf_op jit(solution)/shard_map/ppermute | solution.py:368
  66.7 0.0 copy-done.2
  66.7 0.3 own_branch.1.branch_ref
  66.9 5.5 %collective-permute-done.14.attended_ref = bf16[208,512]{1,0:T(8,128)(2,1)S(1)} collective-permute-done((bf16[208,512]{1,0:T(8,128)(2,1)S(1)}, bf16[208,512]{1,0:T(8,128)(2,1)S(1)}, u32[]{:S(2)}, u32[]{:S(2)}) %collective-permute-start.14) | collective-permute-done | bytes 213024 | tf_op jit(solution)/shard_map/ppermute | solution.py:368
  72.5 1.0 %finish.1 = bf16[256,512]{1,0:T(8,128)(2,1)} custom-call(f32[208,512]{1,0:T(8,128)S(1)} %own_branch.1.branch_ref, bf16[208,512]{1,0:T(8,128)(2,1)S(1)} %collective-permute-done.14.attended_ref, bf16[2,512,512]{2,1,0:T(8,128)(2,1)S(1)} %bitcast.17, bf16[192,512]{1,0:T(8,128)(2,1)S(1)} %get-tuple-element.12.normed_ref), custom_call_target="tpu_custom_call" | custom-call | tf_op jit(solution)/shard_map/finish/pallas_call | solution.py:346
  (7 shorter events, 0.2 us)
Async XLA Ops:
  4.3 11.3 %collective-permute-start = (f32[192,512]{1,0:T(8,128)}, f32[192,512]{1,0:T(8,128)S(1)}, u32[]{:S(2)}, u32[]{:S(2)}) collective-permute-start(f32[192,512]{1,0:T(8,128)} %get-tuple-element.9), channel_id=1, source_target_pairs={{0,30},{2,4},{4,2},{6,8},{8,6},{10,12},{12,10},{14,16},{16,14},{18... | collective-permute-start | bytes 1179656 | tf_op jit(solution)/shard_map/ppermute | solution.py:399
  9.8 5.8 %collective-permute-start.1 = (f32[192,512]{1,0:T(8,128)}, f32[192,512]{1,0:T(8,128)S(1)}, u32[]{:S(2)}, u32[]{:S(2)}) collective-permute-start(f32[192,512]{1,0:T(8,128)} %get-tuple-element.10), channel_id=1, source_target_pairs={{0,2},{1,3},{2,0},{3,1},{4,6},{5,7},{6,4},{7,5},{8,10},{9,11},{10,... | collective-permute-start | bytes 1179656 | tf_op jit(solution)/shard_map/ppermute | solution.py:368
  16.7 7.1 %collective-permute-start.2 = (bf16[192,512]{1,0:T(8,128)(2,1)S(1)}, bf16[192,512]{1,0:T(8,128)(2,1)S(1)}, u32[]{:S(2)}, u32[]{:S(2)}) collective-permute-start(bf16[192,512]{1,0:T(8,128)(2,1)S(1)} %select_convert_fusion.a_ref), channel_id=1, source_target_pairs={{0,4},{1,5},{2,3},{3,2},{4,0},{5,1},{6,7},{7,6},{8,12},{9,13},{10,... | collective-permute-start | bytes 589832 | tf_op jit(solution)/shard_map/ppermute | solution.py:368
  20.1 16.9 %collective-permute-start.8 = (bf16[192,512]{1,0:T(8,128)(2,1)S(1)}, bf16[192,512]{1,0:T(8,128)(2,1)S(1)}, u32[]{:S(2)}, u32[]{:S(2)}) collective-permute-start(bf16[192,512]{1,0:T(8,128)(2,1)S(1)} %select_convert_fusion.a_ref), channel_id=1, source_target_pairs={{0,16},{1,17},{2,18},{3,19},{4,20},{5,21},{6,22},{7,23},{8,24},{9,... | collective-permute-start | bytes 589832 | tf_op jit(solution)/shard_map/ppermute | solution.py:368
  22.7 14.4 %collective-permute-start.5 = (bf16[192,512]{1,0:T(8,128)(2,1)S(1)}, bf16[192,512]{1,0:T(8,128)(2,1)S(1)}, u32[]{:S(2)}, u32[]{:S(2)}) collective-permute-start(bf16[192,512]{1,0:T(8,128)(2,1)S(1)} %select_convert_fusion.a_ref), channel_id=1, source_target_pairs={{0,24},{1,25},{2,26},{3,27},{4,28},{5,29},{6,30},{7,31},{8,16},{9,... | collective-permute-start | bytes 589832 | tf_op jit(solution)/shard_map/ppermute | solution.py:368
  23.8 19.8 %collective-permute-start.3 = (bf16[384,512]{1,0:T(8,128)(2,1)S(1)}, bf16[384,512]{1,0:T(8,128)(2,1)S(1)}, u32[]{:S(2)}, u32[]{:S(2)}) collective-permute-start(bf16[384,512]{1,0:T(8,128)(2,1)S(1)} %join.3.first_ref.rest_0_.refs_2_), channel_id=1, source_target_pairs={{0,1},{1,0},{2,6},{3,7},{4,5},{5,4},{6,2},{7,3},{8,9},{9,8},{10,14... | collective-permute-start | bytes 1179656 | tf_op jit(solution)/shard_map/ppermute | solution.py:368
  25.3 27.4 %collective-permute-start.11 = (bf16[384,512]{1,0:T(8,128)(2,1)S(1)}, bf16[384,512]{1,0:T(8,128)(2,1)S(1)}, u32[]{:S(2)}, u32[]{:S(2)}) collective-permute-start(bf16[384,512]{1,0:T(8,128)(2,1)S(1)} %join.3.first_ref.rest_0_.refs_2_), channel_id=1, source_target_pairs={{0,8},{1,9},{2,10},{3,11},{4,12},{5,13},{6,14},{7,15},{8,0},{9,1},... | collective-permute-start | bytes 1179656 | tf_op jit(solution)/shard_map/ppermute | solution.py:368
  37.0 5.9 %collective-permute-start.9 = (bf16[192,512]{1,0:T(8,128)(2,1)S(1)}, bf16[192,512]{1,0:T(8,128)(2,1)S(1)}, u32[]{:S(2)}, u32[]{:S(2)}) collective-permute-start(bf16[192,512]{1,0:T(8,128)(2,1)S(1)} %after.3.a_ref), channel_id=1, source_target_pairs={{0,4},{1,5},{2,3},{3,2},{4,0},{5,1},{6,7},{7,6},{8,12},{9,13},{10,... | collective-permute-start | bytes 589832 | tf_op jit(solution)/shard_map/ppermute | solution.py:368
  37.1 10.0 %collective-permute-start.6 = (bf16[192,512]{1,0:T(8,128)(2,1)S(1)}, bf16[192,512]{1,0:T(8,128)(2,1)S(1)}, u32[]{:S(2)}, u32[]{:S(2)}) collective-permute-start(bf16[192,512]{1,0:T(8,128)(2,1)S(1)} %after.2.a_ref), channel_id=1, source_target_pairs={{0,4},{1,5},{2,3},{3,2},{4,0},{5,1},{6,7},{7,6},{8,12},{9,13},{10,... | collective-permute-start | bytes 589832 | tf_op jit(solution)/shard_map/ppermute | solution.py:368
  42.9 4.8 %copy-start.3 = (bf16[1024,512]{1,0:T(8,128)(2,1)S(1)}, bf16[1024,512]{1,0:T(8,128)(2,1)}, u32[]{:S(2)}) copy-start(bf16[1024,512]{1,0:T(8,128)(2,1)} %param.12) | copy-start | bytes 3145732
  42.9 4.8 %copy-start.4 = (f32[1024]{0:T(1024)S(1)}, f32[1024]{0:T(1024)}, u32[]{:S(2)}) copy-start(f32[1024]{0:T(1024)} %param.11) | copy-start | bytes 12292
  43.0 6.9 %copy-start = (bf16[1024,512]{1,0:T(8,128)(2,1)S(1)}, bf16[1024,512]{1,0:T(8,128)(2,1)}, u32[]{:S(2)}) copy-start(bf16[1024,512]{1,0:T(8,128)(2,1)} %param.13) | copy-start | bytes 3145732
  43.0 6.9 %copy-start.1 = (bf16[1024,512]{1,0:T(8,128)(2,1)S(1)}, bf16[1024,512]{1,0:T(8,128)(2,1)}, u32[]{:S(2)}) copy-start(bf16[1024,512]{1,0:T(8,128)(2,1)} %param.14) | copy-start | bytes 3145732
  43.0 12.9 %collective-permute-start.10 = (bf16[384,512]{1,0:T(8,128)(2,1)S(1)}, bf16[384,512]{1,0:T(8,128)(2,1)S(1)}, u32[]{:S(2)}, u32[]{:S(2)}) collective-permute-start(bf16[384,512]{1,0:T(8,128)(2,1)S(1)} %join.5.refs_2_), channel_id=1, source_target_pairs={{0,1},{1,0},{2,6},{3,7},{4,5},{5,4},{6,2},{7,3},{8,9},{9,8},{10,14... | collective-permute-start | bytes 1179656 | tf_op jit(solution)/shard_map/ppermute | solution.py:368
  43.6 9.2 %collective-permute-start.12 = (bf16[384,512]{1,0:T(8,128)(2,1)S(1)}, bf16[384,512]{1,0:T(8,128)(2,1)S(1)}, u32[]{:S(2)}, u32[]{:S(2)}) collective-permute-start(bf16[384,512]{1,0:T(8,128)(2,1)S(1)} %collective-permute-done.3.second_ref.refs_3_), channel_id=1, source_target_pairs={{0,8},{1,9},{2,10},{3,11},{4,12},{5,13},{6,14},{7,15},{8,0},{9,1},... | collective-permute-start | bytes 1179656 | tf_op jit(solution)/shard_map/ppermute | solution.py:368
  47.1 11.9 %collective-permute-start.7 = (bf16[384,512]{1,0:T(8,128)(2,1)S(1)}, bf16[384,512]{1,0:T(8,128)(2,1)S(1)}, u32[]{:S(2)}, u32[]{:S(2)}) collective-permute-start(bf16[384,512]{1,0:T(8,128)(2,1)S(1)} %join.4.refs_2_), channel_id=1, source_target_pairs={{0,1},{1,0},{2,6},{3,7},{4,5},{5,4},{6,2},{7,3},{8,9},{9,8},{10,14... | collective-permute-start | bytes 1179656 | tf_op jit(solution)/shard_map/ppermute | solution.py:368
  48.4 1.5 %collective-permute-start.4 = (bf16[192,512]{1,0:T(8,128)(2,1)S(1)}, bf16[192,512]{1,0:T(8,128)(2,1)S(1)}, u32[]{:S(2)}, u32[]{:S(2)}) collective-permute-start(bf16[192,512]{1,0:T(8,128)(2,1)S(1)} %get-tuple-element.11.refs_0_), channel_id=1, source_target_pairs={{0,2},{1,3},{2,0},{3,1},{4,6},{5,7},{6,4},{7,5},{8,10},{9,11},{10,... | collective-permute-start | bytes 589832 | tf_op jit(solution)/shard_map/ppermute | solution.py:368
  59.0 7.7 %copy-start.2 = (bf16[1024,512]{1,0:T(8,128)(2,1)S(1)}, bf16[1024,512]{1,0:T(8,128)(2,1)}, u32[]{:S(2)}) copy-start(bf16[1024,512]{1,0:T(8,128)(2,1)} %param.15) | copy-start | bytes 3145732
  62.1 2.0 %collective-permute-start.13 = (f32[536,256]{1,0:T(8,128)S(1)}, f32[536,256]{1,0:T(8,128)S(1)}, u32[]{:S(2)}, u32[]{:S(2)}) collective-permute-start(f32[536,256]{1,0:T(8,128)S(1)} %slice.4), channel_id=1, source_target_pairs={{0,2},{1,3},{2,0},{3,1},{4,6},{5,7},{6,4},{7,5},{8,10},{9,11},{10,... | collective-permute-start | bytes 1646600 | tf_op jit(solution)/shard_map/ppermute | solution.py:368
  65.1 7.4 %collective-permute-start.14 = (bf16[208,512]{1,0:T(8,128)(2,1)S(1)}, bf16[208,512]{1,0:T(8,128)(2,1)S(1)}, u32[]{:S(2)}, u32[]{:S(2)}) collective-permute-start(bf16[208,512]{1,0:T(8,128)(2,1)S(1)} %combine.1.attended_ref), channel_id=1, source_target_pairs={{0,1},{1,0},{2,3},{3,2},{4,5},{5,4},{6,7},{7,6},{8,9},{9,8},{10,11... | collective-permute-start | bytes 638984 | tf_op jit(solution)/shard_map/ppermute | solution.py:368

commit v5 on v4

--- a/solution.py
+++ b/solution.py
@@ -18,8 +18,8 @@
 
 EPS = 1e-06
 NEG = -1e30
-MARK = 2.0**100
-MARKED = 2.0**90
+MARK = 2.0**50
+MARKED = 2.0**40
 RATE = HD**-0.5 * math.log2(math.e)
 
 ALL = ("ctx", "head")
@@ -106,7 +106,7 @@
             pltpu.SemaphoreType.DMA((COPIES + 2,)),
         ],
         out_shape=[jax.ShapeDtypeStruct((LIVE_MAX, channels), F32)] * len(sides),
-        compiler_params=params(60),
+        compiler_params=params(56),
         cost_estimate=pl.CostEstimate(flops=10**9, bytes_accessed=5 * 10**6, transcendentals=0),
         name="pool",
     )(node_anchor.reshape(tiles, TILE), messages)
@@ -128,37 +128,48 @@
     )(a, *others)
 
 
-def settle(count, own, before, after):
-    slot = lax.broadcasted_iota(jnp.int32, own.shape, 0)
-    return jnp.where(slot < count, own + before + after, MARK).astype(BF16)
-
-
-def join_kernel(a_ref, b_ref, out_ref):
+def settle_kernel(count_ref, own_ref, far_ref, near_ref, out_ref):
+    total = own_ref[...] + far_ref[...] + near_ref[...]
+    slot = lax.broadcasted_iota(jnp.int32, total.shape, 0)
+    out_ref[...] = jnp.where(slot < count_ref[0], total, MARK).astype(BF16)
+
+
+def settle(count, own, far, near):
+    return pl.pallas_call(
+        settle_kernel,
+        in_specs=[pl.BlockSpec(memory_space=pltpu.SMEM)] + vmem(3),
+        out_specs=pl.BlockSpec(memory_space=pltpu.VMEM),
+        out_shape=jax.ShapeDtypeStruct(own.shape, BF16),
+        compiler_params=params(),
+        name="settle",
+    )(count, own, far, near)
+
+
+def join_kernel(a_ref, b_ref, *rest):
+    out_ref = rest[-1]
     rows = a_ref.shape[0]
     out_ref[:rows, :] = a_ref[...]
     out_ref[rows:, :] = b_ref[...]
 
 
-def join(a, b, cost=1):
+def join(a, b, *others, cost=1):
     return pl.pallas_call(
         join_kernel,
-        in_specs=vmem(2),
+        in_specs=vmem(2) + [pl.BlockSpec(memory_space=pl.ANY)] * len(others),
         out_specs=pl.BlockSpec(memory_space=pltpu.VMEM),
         out_shape=jax.ShapeDtypeStruct((a.shape[0] + b.shape[0], a.shape[1]), a.dtype),
         compiler_params=params(),
         cost_estimate=pl.CostEstimate(flops=cost, bytes_accessed=1, transcendentals=0),
         name="join",
-    )(a, b)
+    )(a, b, *others)
 
 
 def normalise(mine, other, gain_ref, x):
     channels = mine.shape[1]
     mine, other = mine.astype(F32), other.astype(F32)
     dead = mine[:, :1] > MARKED
-    mine = jnp.where(dead, 0.0, mine)
-    other = jnp.where(dead, 0.0, other)
     square = jnp.sum(mine * mine + other * other, axis=1, keepdims=True)
-    inverse = lax.rsqrt(square * (1.0 / (2 * channels)) + EPS)
+    inverse = jnp.where(dead, 0.0, lax.rsqrt(square * (1.0 / (2 * channels)) + EPS))
     mine = (mine * inverse * gain_ref[x]).astype(BF16)
     other = (other * inverse * gain_ref[1 - x]).astype(BF16)
     return mine, other, dead
@@ -185,7 +196,7 @@
         out_specs=vmem(2),
         out_shape=[jax.ShapeDtypeStruct((LIVE_MAX, channels), BF16)] * 2,
         compiler_params=params(),
-        cost_estimate=pl.CostEstimate(flops=1, bytes_accessed=1, transcendentals=0),
+        cost_estimate=pl.CostEstimate(flops=10**10, bytes_accessed=1, transcendentals=0),
         name="queries",
     )(first, second, gain, wq)
 
@@ -274,7 +285,7 @@
         input_output_aliases={} if state is None else {len(args) - 1: 0},
         compiler_params=params(),
         cost_estimate=pl.CostEstimate(
-            flops=1, bytes_accessed=1, transcendentals=0
+            flops=2*10**9, bytes_accessed=1, transcendentals=0
         ),
         name="attend",
     )(*args)
@@ -409,10 +420,10 @@
     beside = [send(first, across_z(1)), send(second, across_z(1))]
     state = attend(query, swapped, first, second, gain, wk, wv)
     states = [state, attend(query, swapped, *beside, gain, wk, wv, state)]
-    plane = first
+    gates = (first, query)
     for index, rows in enumerate(far_rows):
-        rows = after(rows, plane, cost=2*10**10)
-        first = join(rows, send(rows, across_first), cost=10**10)
+        rows = after(rows, gates[index], cost=(2 * 10**10, 5 * 10**9)[index])
+        first = join(rows, send(rows, across_first), *([] if index else [state]), cost=3 * 10**10)
         second = send(first, across_second)
         states.append(attend(query, swapped, first, second, gain, wk, wv, states[-1]))
     state = states[-1]

time: 74.5 us -> 71 us (0.953); the launches traced: 73.5 us -> 70.7 us
  waiting for transfers between devices: 27.9 us -> 23.7 us
  starting transfers between devices: 20.5 us -> 22.3 us
  other arithmetic: 1.1 us -> 0 us
  local copies, waits for them, and re-layouts: 0.07 us -> 1.07 us
    ppermute x14, waiting for transfers between devices: 26.5 us -> 22.3 us  [send(): return lax.ppermute(array, ALL, pairs(move))]
    ppermute x14, starting transfers between devices: 15 us -> 16.8 us  [send(): return lax.ppermute(array, ALL, pairs(move))]
    convert_element_type x1 -> x0, other arithmetic: 1.09 us -> none  [settle(): return jnp.where(slot < count, own + before + after, MARK).astype(BF16)]
    unnamed x10 -> x12, local copies, waits for them, and re-layouts: 0.03 us -> 1.03 us
  transfers between devices with their start and end apart: 15 -> 15, of which waited for: 8 -> 6; matrix products, arithmetic and copies ran while one was open for 0% -> 0% of each run, Pallas kernels for 19% -> 19%
where the time goes in v5:
time: 71 us; the launch traced here: 70.7 us
  waiting for transfers between devices  23.7 us (33%)
  Pallas kernels  22.8 us (32%)
  starting transfers between devices  22.3 us (31%)
  local copies, waits for them, and re-layouts  1.07 us (2%)
  between operations  0.88 us (1%)
    ppermute x14, waiting for transfers between devices, send(): return lax.ppermute(array, ALL, pairs(move))  22.3 us
    ppermute x14, starting transfers between devices, send(): return lax.ppermute(array, ALL, pairs(move))  16.8 us
    pallas_call x4, Pallas kernels, attend(): pl.pallas_call(functools.partial(attend_kernel, state is None), in_specs=...  11.8 us
    pallas_call x2, Pallas kernels, pool(): pl.pallas_call(functools.partial(pool_kernel, sides), in_specs=[hbm] * 2,...  8.03 us
    ppermute x1, starting transfers between devices, block_plan(): lax.ppermute(far, 'ctx', [(i, (i + (1 if i % 2 else 15)) % 16) for i in r...  5.51 us
  transfers between devices with their start and end apart: 15, of which 6 were waited for; matrix products, arithmetic and copies ran while one was open for 0% of the time, Pallas kernels for 19%

profile of v5, /device:TPU:0, one launch (start us, length us, event | category | flops | bytes accessed | tf_op | source)
XLA Modules:
  0.0 70.7 jit_solution(10281405304824214535)
XLA Ops:
  0.0 4.3 %pool.3 = (f32[192,512]{1,0:T(8,128)}, f32[192,512]{1,0:T(8,128)}) custom-call(s32[32,128]{1,0:T(8,128)} %bitcast.22, bf16[4096,512]{1,0:T(8,128)(2,1)} %messages_hbm.3), custom_call_target="tpu_custom_call" | custom-call | flops 1000000000 | bytes 5000000 | tf_op jit(solution)/shard_map/pool/pallas_call | solution.py:97
  4.3 5.5 %collective-permute-start = (f32[192,512]{1,0:T(8,128)}, f32[192,512]{1,0:T(8,128)S(1)}, u32[]{:S(2)}, u32[]{:S(2)}) collective-permute-start(f32[192,512]{1,0:T(8,128)} %get-tuple-element.9), channel_id=1, source_target_pairs={{0,30},{2,4},{4,2},{6,8},{8,6},{10,12},{12,10},{14,16},{16,14},{18... | collective-permute-start | bytes 1179656 | tf_op jit(solution)/shard_map/ppermute | solution.py:410
  9.8 0.0 collective-permute-start.1
  10.5 3.7 %pool.2.own_ref = f32[192,512]{1,0:T(8,128)} custom-call(s32[32,128]{1,0:T(8,128)} %bitcast.23, bf16[4096,512]{1,0:T(8,128)(2,1)} %messages_hbm.3), custom_call_target="tpu_custom_call" | custom-call | flops 1000000000 | bytes 5000000 | tf_op jit(solution)/shard_map/pool/pallas_call | solution.py:97
  14.2 1.4 %collective-permute-done.far_ref = f32[192,512]{1,0:T(8,128)S(1)} collective-permute-done((f32[192,512]{1,0:T(8,128)}, f32[192,512]{1,0:T(8,128)S(1)}, u32[]{:S(2)}, u32[]{:S(2)}) %collective-permute-start) | collective-permute-done | bytes 393248 | tf_op jit(solution)/shard_map/ppermute | solution.py:410
  15.6 0.0 collective-permute-done.1.near_ref
  15.6 0.0 copy-start.1
  15.6 1.0 %copy-done.1 = f32[192,512]{1,0:T(8,128)S(1)} copy-done((f32[192,512]{1,0:T(8,128)S(1)}, f32[192,512]{1,0:T(8,128)}, u32[]{:S(2)}) %copy-start.1) | copy-done | bytes 393240
  16.6 0.1 settle.1.a_ref
  16.6 3.4 %collective-permute-start.2 = (bf16[192,512]{1,0:T(8,128)(2,1)S(1)}, bf16[192,512]{1,0:T(8,128)(2,1)S(1)}, u32[]{:S(2)}, u32[]{:S(2)}) collective-permute-start(bf16[192,512]{1,0:T(8,128)(2,1)S(1)} %settle.1.a_ref), channel_id=1, source_target_pairs={{0,4},{1,5},{2,3},{3,2},{4,0},{5,1},{6,7},{7,6},{8,12},{9,13},{10,... | collective-permute-start | bytes 589832 | tf_op jit(solution)/shard_map/ppermute | solution.py:379
  20.1 2.6 %collective-permute-start.8 = (bf16[192,512]{1,0:T(8,128)(2,1)S(1)}, bf16[192,512]{1,0:T(8,128)(2,1)S(1)}, u32[]{:S(2)}, u32[]{:S(2)}) collective-permute-start(bf16[192,512]{1,0:T(8,128)(2,1)S(1)} %settle.1.a_ref), channel_id=1, source_target_pairs={{0,16},{1,17},{2,18},{3,19},{4,20},{5,21},{6,22},{7,23},{8,24},{9,... | collective-permute-start | bytes 589832 | tf_op jit(solution)/shard_map/ppermute | solution.py:379
  22.7 1.4 %collective-permute-start.5 = (bf16[192,512]{1,0:T(8,128)(2,1)S(1)}, bf16[192,512]{1,0:T(8,128)(2,1)S(1)}, u32[]{:S(2)}, u32[]{:S(2)}) collective-permute-start(bf16[192,512]{1,0:T(8,128)(2,1)S(1)} %settle.1.a_ref), channel_id=1, source_target_pairs={{0,24},{1,25},{2,26},{3,27},{4,28},{5,29},{6,30},{7,31},{8,16},{9,... | collective-permute-start | bytes 589832 | tf_op jit(solution)/shard_map/ppermute | solution.py:379
  24.0 0.0 collective-permute-done.2.b_ref
  24.1 0.0 copy-start.2
  24.1 0.0 copy-start.5
  24.1 1.6 %collective-permute-start.3 = (bf16[384,512]{1,0:T(8,128)(2,1)S(1)}, bf16[384,512]{1,0:T(8,128)(2,1)S(1)}, u32[]{:S(2)}, u32[]{:S(2)}) collective-permute-start(bf16[384,512]{1,0:T(8,128)(2,1)S(1)} %join.3.first_ref.rest_0_.refs_2_), channel_id=1, source_target_pairs={{0,1},{1,0},{2,6},{3,7},{4,5},{5,4},{6,2},{7,3},{8,9},{9,8},{10,14... | collective-permute-start | bytes 1179656 | tf_op jit(solution)/shard_map/ppermute | solution.py:379
  25.6 1.3 %collective-permute-start.11 = (bf16[384,512]{1,0:T(8,128)(2,1)S(1)}, bf16[384,512]{1,0:T(8,128)(2,1)S(1)}, u32[]{:S(2)}, u32[]{:S(2)}) collective-permute-start(bf16[384,512]{1,0:T(8,128)(2,1)S(1)} %join.3.first_ref.rest_0_.refs_2_), channel_id=1, source_target_pairs={{0,8},{1,9},{2,10},{3,11},{4,12},{5,13},{6,14},{7,15},{8,0},{9,1},... | collective-permute-start | bytes 1179656 | tf_op jit(solution)/shard_map/ppermute | solution.py:379
  26.9 10.1 %collective-permute-done.8.a_ref = bf16[192,512]{1,0:T(8,128)(2,1)S(1)} collective-permute-done((bf16[192,512]{1,0:T(8,128)(2,1)S(1)}, bf16[192,512]{1,0:T(8,128)(2,1)S(1)}, u32[]{:S(2)}, u32[]{:S(2)}) %collective-permute-start.8) | collective-permute-done | bytes 196640 | tf_op jit(solution)/shard_map/ppermute | solution.py:379
  37.0 0.1 collective-permute-start.9
  37.1 0.0 collective-permute-done.3.second_ref.refs_3_
  37.1 0.0 copy-done.2
  37.1 0.0 copy-done.5
  37.1 0.6 queries.1
  37.7 0.0 copy-start.3
  37.7 0.0 copy-start.4
  37.8 0.1 collective-permute-start.4
  37.8 0.0 collective-permute-done.5.a_ref
  37.9 2.1 %collective-permute-start.6 = (bf16[192,512]{1,0:T(8,128)(2,1)S(1)}, bf16[192,512]{1,0:T(8,128)(2,1)S(1)}, u32[]{:S(2)}, u32[]{:S(2)}) collective-permute-start(bf16[192,512]{1,0:T(8,128)(2,1)S(1)} %after.2.a_ref), channel_id=1, source_target_pairs={{0,4},{1,5},{2,3},{3,2},{4,0},{5,1},{6,7},{7,6},{8,12},{9,13},{10,... | collective-permute-start | bytes 589832 | tf_op jit(solution)/shard_map/ppermute | solution.py:379
  39.9 1.0 %collective-permute-start.12 = (bf16[384,512]{1,0:T(8,128)(2,1)S(1)}, bf16[384,512]{1,0:T(8,128)(2,1)S(1)}, u32[]{:S(2)}, u32[]{:S(2)}) collective-permute-start(bf16[384,512]{1,0:T(8,128)(2,1)S(1)} %collective-permute-done.3.second_ref.refs_3_), channel_id=1, source_target_pairs={{0,8},{1,9},{2,10},{3,11},{4,12},{5,13},{6,14},{7,15},{8,0},{9,1},... | collective-permute-start | bytes 1179656 | tf_op jit(solution)/shard_map/ppermute | solution.py:379
  40.9 0.0 collective-permute-done.4.refs_1_
  40.9 0.0 copy-done.3
  40.9 0.0 copy-done.4
  40.9 2.9 %attend.4.rest_0_.refs_7_ = f32[536,384]{1,0:T(8,128)S(1)} custom-call(bf16[192,512]{1,0:T(8,128)(2,1)S(1)} %get-tuple-element.11.rest_0_.refs_0_, bf16[192,512]{1,0:T(8,128)(2,1)S(1)} %collective-permute-done.4.refs_1_, bf16[384,512]{1,0:T(8,128)(2,1)S(1)} %join.3.first_ref.rest_0_.refs_2_, bf16[384,512]{1,0:T(8,128)(2,1)S(1)} %collective-permute-done.3.second_ref.refs_3_, ...), custom_call_target="tpu_custom_call" | custom-call | flops 2000000000 | bytes 1 | tf_op jit(solution)/shard_map/attend/pallas_call | solution.py:280
  43.8 0.0 collective-permute-done.9.b_ref
  43.8 0.6 collective-permute-start.10
  44.4 0.5 collective-permute-done.6.b_ref
  44.9 1.1 %collective-permute-start.7 = (bf16[384,512]{1,0:T(8,128)(2,1)S(1)}, bf16[384,512]{1,0:T(8,128)(2,1)S(1)}, u32[]{:S(2)}, u32[]{:S(2)}) collective-permute-start(bf16[384,512]{1,0:T(8,128)(2,1)S(1)} %join.4.refs_2_), channel_id=1, source_target_pairs={{0,1},{1,0},{2,6},{3,7},{4,5},{5,4},{6,2},{7,3},{8,9},{9,8},{10,14... | collective-permute-start | bytes 1179656 | tf_op jit(solution)/shard_map/ppermute | solution.py:379
  46.0 0.0 collective-permute-done.11.refs_2_
  46.0 4.3 %collective-permute-done.12.refs_3_ = bf16[384,512]{1,0:T(8,128)(2,1)S(1)} collective-permute-done((bf16[384,512]{1,0:T(8,128)(2,1)S(1)}, bf16[384,512]{1,0:T(8,128)(2,1)S(1)}, u32[]{:S(2)}, u32[]{:S(2)}) %collective-permute-start.12) | collective-permute-done | bytes 393248 | tf_op jit(solution)/shard_map/ppermute | solution.py:379
  50.4 3.0 %attend.5.refs_7_ = f32[536,384]{1,0:T(8,128)S(1)} custom-call(bf16[192,512]{1,0:T(8,128)(2,1)S(1)} %get-tuple-element.11.rest_0_.refs_0_, bf16[192,512]{1,0:T(8,128)(2,1)S(1)} %collective-permute-done.4.refs_1_, bf16[384,512]{1,0:T(8,128)(2,1)S(1)} %collective-permute-done.11.refs_2_, ...), custom_call_target="tpu_custom_call", output_to_operand_aliasing={{}: (7, {})} | custom-call | flops 2000000000 | bytes 1 | tf_op jit(solution)/shard_map/attend/pallas_call | solution.py:280
  53.3 0.0 collective-permute-done.10.refs_3_
  53.4 3.0 %attend.6.refs_7_ = f32[536,384]{1,0:T(8,128)S(1)} custom-call(bf16[192,512]{1,0:T(8,128)(2,1)S(1)} %get-tuple-element.11.rest_0_.refs_0_, bf16[192,512]{1,0:T(8,128)(2,1)S(1)} %collective-permute-done.4.refs_1_, bf16[384,512]{1,0:T(8,128)(2,1)S(1)} %join.5.refs_2_, ...), custom_call_target="tpu_custom_call", output_to_operand_aliasing={{}: (7, {})} | custom-call | flops 2000000000 | bytes 1 | tf_op jit(solution)/shard_map/attend/pallas_call | solution.py:280
  56.4 0.0 copy-start
  56.4 0.0 collective-permute-done.7.refs_3_
  56.4 3.0 %attend.7.mine_ref = f32[536,384]{1,0:T(8,128)S(1)} custom-call(bf16[192,512]{1,0:T(8,128)(2,1)S(1)} %get-tuple-element.11.rest_0_.refs_0_, bf16[192,512]{1,0:T(8,128)(2,1)S(1)} %collective-permute-done.4.refs_1_, bf16[384,512]{1,0:T(8,128)(2,1)S(1)} %join.4.refs_2_, ...), custom_call_target="tpu_custom_call", output_to_operand_aliasing={{}: (7, {})} | custom-call | flops 2000000000 | bytes 1 | tf_op jit(solution)/shard_map/attend/pallas_call | solution.py:280
  59.4 0.1 collective-permute-start.13
  59.5 1.9 %collective-permute-done.13.other_ref = f32[536,256]{1,0:T(8,128)S(1)} collective-permute-done((f32[536,256]{1,0:T(8,128)S(1)}, f32[536,256]{1,0:T(8,128)S(1)}, u32[]{:S(2)}, u32[]{:S(2)}) %collective-permute-start.13) | collective-permute-done | bytes 548896 | tf_op jit(solution)/shard_map/ppermute | solution.py:379
  61.4 0.9 %combine.1.attended_ref = bf16[208,512]{1,0:T(8,128)(2,1)S(1)} custom-call(f32[536,384]{1,0:T(8,128)S(1)} %attend.7.mine_ref, f32[536,256]{1,0:T(8,128)S(1)} %collective-permute-done.13.other_ref), custom_call_target="tpu_custom_call" | custom-call | tf_op jit(solution)/shard_map/combine/pallas_call | solution.py:323
  62.4 1.6 %collective-permute-start.14 = (bf16[208,512]{1,0:T(8,128)(2,1)S(1)}, bf16[208,512]{1,0:T(8,128)(2,1)S(1)}, u32[]{:S(2)}, u32[]{:S(2)}) collective-permute-start(bf16[208,512]{1,0:T(8,128)(2,1)S(1)} %combine.1.attended_ref), channel_id=1, source_target_pairs={{0,1},{1,0},{2,3},{3,2},{4,5},{5,4},{6,7},{7,6},{8,9},{9,8},{10,11... | collective-permute-start | bytes 638984 | tf_op jit(solution)/shard_map/ppermute | solution.py:379
  64.0 0.0 copy-done
  64.0 0.3 own_branch.1.branch_ref
  64.3 5.4 %collective-permute-done.14.attended_ref = bf16[208,512]{1,0:T(8,128)(2,1)S(1)} collective-permute-done((bf16[208,512]{1,0:T(8,128)(2,1)S(1)}, bf16[208,512]{1,0:T(8,128)(2,1)S(1)}, u32[]{:S(2)}, u32[]{:S(2)}) %collective-permute-start.14) | collective-permute-done | bytes 213024 | tf_op jit(solution)/shard_map/ppermute | solution.py:379
  69.7 1.0 %finish.1 = bf16[256,512]{1,0:T(8,128)(2,1)} custom-call(f32[208,512]{1,0:T(8,128)S(1)} %own_branch.1.branch_ref, bf16[208,512]{1,0:T(8,128)(2,1)S(1)} %collective-permute-done.14.attended_ref, bf16[2,512,512]{2,1,0:T(8,128)(2,1)S(1)} %bitcast.7, bf16[192,512]{1,0:T(8,128)(2,1)S(1)} %get-tuple-element.12.normed_ref), custom_call_target="tpu_custom_call" | custom-call | tf_op jit(solution)/shard_map/finish/pallas_call | solution.py:357
  (6 shorter events, 0.1 us)
Async XLA Ops:
  4.3 11.3 %collective-permute-start = (f32[192,512]{1,0:T(8,128)}, f32[192,512]{1,0:T(8,128)S(1)}, u32[]{:S(2)}, u32[]{:S(2)}) collective-permute-start(f32[192,512]{1,0:T(8,128)} %get-tuple-element.9), channel_id=1, source_target_pairs={{0,30},{2,4},{4,2},{6,8},{8,6},{10,12},{12,10},{14,16},{16,14},{18... | collective-permute-start | bytes 1179656 | tf_op jit(solution)/shard_map/ppermute | solution.py:410
  9.8 5.8 %collective-permute-start.1 = (f32[192,512]{1,0:T(8,128)}, f32[192,512]{1,0:T(8,128)S(1)}, u32[]{:S(2)}, u32[]{:S(2)}) collective-permute-start(f32[192,512]{1,0:T(8,128)} %get-tuple-element.10), channel_id=1, source_target_pairs={{0,2},{1,3},{2,0},{3,1},{4,6},{5,7},{6,4},{7,5},{8,10},{9,11},{10,... | collective-permute-start | bytes 1179656 | tf_op jit(solution)/shard_map/ppermute | solution.py:379
  15.6 1.0 %copy-start.1 = (f32[192,512]{1,0:T(8,128)S(1)}, f32[192,512]{1,0:T(8,128)}, u32[]{:S(2)}) copy-start(f32[192,512]{1,0:T(8,128)} %pool.2.own_ref) | copy-start | bytes 1179652
  16.6 7.4 %collective-permute-start.2 = (bf16[192,512]{1,0:T(8,128)(2,1)S(1)}, bf16[192,512]{1,0:T(8,128)(2,1)S(1)}, u32[]{:S(2)}, u32[]{:S(2)}) collective-permute-start(bf16[192,512]{1,0:T(8,128)(2,1)S(1)} %settle.1.a_ref), channel_id=1, source_target_pairs={{0,4},{1,5},{2,3},{3,2},{4,0},{5,1},{6,7},{7,6},{8,12},{9,13},{10,... | collective-permute-start | bytes 589832 | tf_op jit(solution)/shard_map/ppermute | solution.py:379
  20.1 16.9 %collective-permute-start.8 = (bf16[192,512]{1,0:T(8,128)(2,1)S(1)}, bf16[192,512]{1,0:T(8,128)(2,1)S(1)}, u32[]{:S(2)}, u32[]{:S(2)}) collective-permute-start(bf16[192,512]{1,0:T(8,128)(2,1)S(1)} %settle.1.a_ref), channel_id=1, source_target_pairs={{0,16},{1,17},{2,18},{3,19},{4,20},{5,21},{6,22},{7,23},{8,24},{9,... | collective-permute-start | bytes 589832 | tf_op jit(solution)/shard_map/ppermute | solution.py:379
  22.7 15.2 %collective-permute-start.5 = (bf16[192,512]{1,0:T(8,128)(2,1)S(1)}, bf16[192,512]{1,0:T(8,128)(2,1)S(1)}, u32[]{:S(2)}, u32[]{:S(2)}) collective-permute-start(bf16[192,512]{1,0:T(8,128)(2,1)S(1)} %settle.1.a_ref), channel_id=1, source_target_pairs={{0,24},{1,25},{2,26},{3,27},{4,28},{5,29},{6,30},{7,31},{8,16},{9,... | collective-permute-start | bytes 589832 | tf_op jit(solution)/shard_map/ppermute | solution.py:379
  24.1 13.1 %copy-start.2 = (bf16[1024,512]{1,0:T(8,128)(2,1)S(1)}, bf16[1024,512]{1,0:T(8,128)(2,1)}, u32[]{:S(2)}) copy-start(bf16[1024,512]{1,0:T(8,128)(2,1)} %param.12) | copy-start | bytes 3145732
  24.1 13.1 %copy-start.5 = (f32[1024]{0:T(1024)S(1)}, f32[1024]{0:T(1024)}, u32[]{:S(2)}) copy-start(f32[1024]{0:T(1024)} %param.11) | copy-start | bytes 12292
  24.1 13.0 %collective-permute-start.3 = (bf16[384,512]{1,0:T(8,128)(2,1)S(1)}, bf16[384,512]{1,0:T(8,128)(2,1)S(1)}, u32[]{:S(2)}, u32[]{:S(2)}) collective-permute-start(bf16[384,512]{1,0:T(8,128)(2,1)S(1)} %join.3.first_ref.rest_0_.refs_2_), channel_id=1, source_target_pairs={{0,1},{1,0},{2,6},{3,7},{4,5},{5,4},{6,2},{7,3},{8,9},{9,8},{10,14... | collective-permute-start | bytes 1179656 | tf_op jit(solution)/shard_map/ppermute | solution.py:379
  25.6 20.4 %collective-permute-start.11 = (bf16[384,512]{1,0:T(8,128)(2,1)S(1)}, bf16[384,512]{1,0:T(8,128)(2,1)S(1)}, u32[]{:S(2)}, u32[]{:S(2)}) collective-permute-start(bf16[384,512]{1,0:T(8,128)(2,1)S(1)} %join.3.first_ref.rest_0_.refs_2_), channel_id=1, source_target_pairs={{0,8},{1,9},{2,10},{3,11},{4,12},{5,13},{6,14},{7,15},{8,0},{9,1},... | collective-permute-start | bytes 1179656 | tf_op jit(solution)/shard_map/ppermute | solution.py:379
  37.0 6.8 %collective-permute-start.9 = (bf16[192,512]{1,0:T(8,128)(2,1)S(1)}, bf16[192,512]{1,0:T(8,128)(2,1)S(1)}, u32[]{:S(2)}, u32[]{:S(2)}) collective-permute-start(bf16[192,512]{1,0:T(8,128)(2,1)S(1)} %after.3.a_ref), channel_id=1, source_target_pairs={{0,4},{1,5},{2,3},{3,2},{4,0},{5,1},{6,7},{7,6},{8,12},{9,13},{10,... | collective-permute-start | bytes 589832 | tf_op jit(solution)/shard_map/ppermute | solution.py:379
  37.7 3.2 %copy-start.3 = (bf16[1024,512]{1,0:T(8,128)(2,1)S(1)}, bf16[1024,512]{1,0:T(8,128)(2,1)}, u32[]{:S(2)}) copy-start(bf16[1024,512]{1,0:T(8,128)(2,1)} %param.13) | copy-start | bytes 3145732
  37.7 3.2 %copy-start.4 = (bf16[1024,512]{1,0:T(8,128)(2,1)S(1)}, bf16[1024,512]{1,0:T(8,128)(2,1)}, u32[]{:S(2)}) copy-start(bf16[1024,512]{1,0:T(8,128)(2,1)} %param.14) | copy-start | bytes 3145732
  37.8 3.1 %collective-permute-start.4 = (bf16[192,512]{1,0:T(8,128)(2,1)S(1)}, bf16[192,512]{1,0:T(8,128)(2,1)S(1)}, u32[]{:S(2)}, u32[]{:S(2)}) collective-permute-start(bf16[192,512]{1,0:T(8,128)(2,1)S(1)} %get-tuple-element.11.rest_0_.refs_0_), channel_id=1, source_target_pairs={{0,2},{1,3},{2,0},{3,1},{4,6},{5,7},{6,4},{7,5},{8,10},{9,11},{10,... | collective-permute-start | bytes 589832 | tf_op jit(solution)/shard_map/ppermute | solution.py:379
  37.9 7.0 %collective-permute-start.6 = (bf16[192,512]{1,0:T(8,128)(2,1)S(1)}, bf16[192,512]{1,0:T(8,128)(2,1)S(1)}, u32[]{:S(2)}, u32[]{:S(2)}) collective-permute-start(bf16[192,512]{1,0:T(8,128)(2,1)S(1)} %after.2.a_ref), channel_id=1, source_target_pairs={{0,4},{1,5},{2,3},{3,2},{4,0},{5,1},{6,7},{7,6},{8,12},{9,13},{10,... | collective-permute-start | bytes 589832 | tf_op jit(solution)/shard_map/ppermute | solution.py:379
  39.9 10.4 %collective-permute-start.12 = (bf16[384,512]{1,0:T(8,128)(2,1)S(1)}, bf16[384,512]{1,0:T(8,128)(2,1)S(1)}, u32[]{:S(2)}, u32[]{:S(2)}) collective-permute-start(bf16[384,512]{1,0:T(8,128)(2,1)S(1)} %collective-permute-done.3.second_ref.refs_3_), channel_id=1, source_target_pairs={{0,8},{1,9},{2,10},{3,11},{4,12},{5,13},{6,14},{7,15},{8,0},{9,1},... | collective-permute-start | bytes 1179656 | tf_op jit(solution)/shard_map/ppermute | solution.py:379
  43.8 9.5 %collective-permute-start.10 = (bf16[384,512]{1,0:T(8,128)(2,1)S(1)}, bf16[384,512]{1,0:T(8,128)(2,1)S(1)}, u32[]{:S(2)}, u32[]{:S(2)}) collective-permute-start(bf16[384,512]{1,0:T(8,128)(2,1)S(1)} %join.5.refs_2_), channel_id=1, source_target_pairs={{0,1},{1,0},{2,6},{3,7},{4,5},{5,4},{6,2},{7,3},{8,9},{9,8},{10,14... | collective-permute-start | bytes 1179656 | tf_op jit(solution)/shard_map/ppermute | solution.py:379
  44.9 11.5 %collective-permute-start.7 = (bf16[384,512]{1,0:T(8,128)(2,1)S(1)}, bf16[384,512]{1,0:T(8,128)(2,1)S(1)}, u32[]{:S(2)}, u32[]{:S(2)}) collective-permute-start(bf16[384,512]{1,0:T(8,128)(2,1)S(1)} %join.4.refs_2_), channel_id=1, source_target_pairs={{0,1},{1,0},{2,6},{3,7},{4,5},{5,4},{6,2},{7,3},{8,9},{9,8},{10,14... | collective-permute-start | bytes 1179656 | tf_op jit(solution)/shard_map/ppermute | solution.py:379
  56.4 7.7 %copy-start = (bf16[1024,512]{1,0:T(8,128)(2,1)S(1)}, bf16[1024,512]{1,0:T(8,128)(2,1)}, u32[]{:S(2)}) copy-start(bf16[1024,512]{1,0:T(8,128)(2,1)} %param.15) | copy-start | bytes 3145732
  59.4 2.0 %collective-permute-start.13 = (f32[536,256]{1,0:T(8,128)S(1)}, f32[536,256]{1,0:T(8,128)S(1)}, u32[]{:S(2)}, u32[]{:S(2)}) collective-permute-start(f32[536,256]{1,0:T(8,128)S(1)} %slice.4), channel_id=1, source_target_pairs={{0,2},{1,3},{2,0},{3,1},{4,6},{5,7},{6,4},{7,5},{8,10},{9,11},{10,... | collective-permute-start | bytes 1646600 | tf_op jit(solution)/shard_map/ppermute | solution.py:379
  62.4 7.4 %collective-permute-start.14 = (bf16[208,512]{1,0:T(8,128)(2,1)S(1)}, bf16[208,512]{1,0:T(8,128)(2,1)S(1)}, u32[]{:S(2)}, u32[]{:S(2)}) collective-permute-start(bf16[208,512]{1,0:T(8,128)(2,1)S(1)} %combine.1.attended_ref), channel_id=1, source_target_pairs={{0,1},{1,0},{2,3},{3,2},{4,5},{5,4},{6,7},{7,6},{8,9},{9,8},{10,11... | collective-permute-start | bytes 638984 | tf_op jit(solution)/shard_map/ppermute | solution.py:379

commit v6 on v5

--- a/solution.py
+++ b/solution.py
@@ -63,31 +63,35 @@
         out[...] = jnp.zeros_like(out)
     slots = lax.broadcasted_iota(jnp.int32, (LIVE_MAX, TILE), 0)
     loads[0].wait()
-    counts = [jnp.int32(0)] * len(sides)
-    for tile in range(tiles):
-        side = lax.rem(anchors_smem[tile, 0] // ANCH_DEV - center + 1 + partitions, partitions)
-        for index, name in enumerate(sides):
-            ahead = 1 if name == "own" else 2 * lax.rem(center, 2)
-            which = 2 - ahead if name == "near" else ahead
-            listed[index, counts[index]] = tile
-            counts[index] = counts[index] + jnp.where(side == which, 1, 0)
-    for load in loads[1:]:
-        load.wait()
-    for index, out in enumerate(outs):
-
-        def add(group, unused, index=index, out=out):
-            onehots, parts = [], []
-            for at in range(GROUP):
-                place = group * GROUP + at
-                wanted = place < counts[index]
-                tile = jnp.where(wanted, listed[index, jnp.minimum(place, tiles - 1)], 0)
-                slot = jnp.where(wanted, anchors[pl.ds(tile, 1), :] % ANCH_DEV, -1)
-                onehots.append(jnp.where(slots == slot, 1.0, 0.0).astype(BF16))
-                parts.append(messages[pl.ds(pl.multiple_of(tile * TILE, TILE), TILE), :])
-            out[...] += dot(jnp.concatenate(onehots, axis=1), jnp.concatenate(parts, axis=0))
-            return unused
-
-        lax.fori_loop(0, (counts[index] + GROUP - 1) // GROUP, add, 0)
+    half = tiles // 2
+    for part in range(2):
+        counts = [jnp.int32(0)] * len(sides)
+        for tile in range(part * half, (part + 1) * half):
+            side = lax.rem(anchors_smem[tile, 0] // ANCH_DEV - center + 1 + partitions, partitions)
+            for index, name in enumerate(sides):
+                ahead = 1 if name == "own" else 2 * lax.rem(center, 2)
+                which = 2 - ahead if name == "near" else ahead
+                listed[index, counts[index]] = tile
+                counts[index] = counts[index] + jnp.where(side == which, 1, 0)
+        if part == 0:
+            loads[1].wait()
+        for load in loads[2 + part * COPIES // 2 : 2 + (part + 1) * COPIES // 2]:
+            load.wait()
+        for index, out in enumerate(outs):
+
+            def add(group, unused, index=index, out=out, count=counts[index]):
+                onehots, parts = [], []
+                for at in range(GROUP):
+                    place = group * GROUP + at
+                    wanted = place < count
+                    tile = jnp.where(wanted, listed[index, jnp.minimum(place, half - 1)], 0)
+                    slot = jnp.where(wanted, anchors[pl.ds(tile, 1), :] % ANCH_DEV, -1)
+                    onehots.append(jnp.where(slots == slot, 1.0, 0.0).astype(BF16))
+                    parts.append(messages[pl.ds(pl.multiple_of(tile * TILE, TILE), TILE), :])
+                out[...] += dot(jnp.concatenate(onehots, axis=1), jnp.concatenate(parts, axis=0))
+                return unused
+
+            lax.fori_loop(0, (counts[index] + GROUP - 1) // GROUP, add, 0)
 
 
 def pool(messages, node_anchor, sides):
@@ -267,8 +271,12 @@
             mixed = mixed + state_ref[at, :] * fade
         out_ref[at, :] = mixed
 
-    scores = [score(head) for head in range(heads)]
-    weights = [weigh(head, scores[head]) for head in range(heads)]
+    scores = [score(head) for head in range(heads // 2)]
+    weights = []
+    for head in range(heads):
+        weights.append(weigh(head, scores[head]))
+        if len(scores) < heads:
+            scores.append(score(len(scores)))
     for head in range(heads):
         mix(head, *weights[head])
 
@@ -307,7 +315,7 @@
         top = jnp.maximum(a, b)
         a, b = jnp.exp2((a - top) * RATE), jnp.exp2((b - top) * RATE)
         total = mine_ref[at_total, :SENT] * a + theirs(at_total) * b
-        mixed = (mine_ref[at, :SENT] * a + theirs(at) * b) / total
+        mixed = mine_ref[at, :SENT] * (a / total) + theirs(at) * (b / total)
         out_ref[:LIVE_MAX, at] = mixed.T[:LIVE_MAX].astype(BF16)
     extra = channels + 2 * heads
     sums = mine_ref[extra : extra + 8, QROWS - SENT :] + other_ref[extra : extra + 8, :]
@@ -409,6 +417,7 @@
     (own,) = pool(messages, node_anchor, ("own",))
     from_far = lax.ppermute(far, "ctx", [(i, (i + (1 if i % 2 else 15)) % 16) for i in range(16)])
     from_near = send(near, across_core)
+    own = after(own, cost=10**9)
     mine = settle(anchor_count, own, from_far, from_near)
     gain = norm_gain.reshape(2, 1, channels)
     wq, wk, wv, wo = halves(w_query), halves(w_key), halves(w_value), halves(w_out)

time: 71 us -> 70.1 us (0.987)
  waiting for transfers between devices: 23.7 us -> 22.4 us
    ppermute x1, waiting for transfers between devices: 1.37 us -> 0.01 us  [block_plan(): lax.ppermute(far, 'ctx', [(i, (i + (1 if i % 2 else 15)) % 16) for i in r...]
  transfers between devices with their start and end apart: 15 -> 15, of which waited for: 6 -> 5; matrix products, arithmetic and copies ran while one was open for 0% -> 0% of each run, Pallas kernels for 19% -> 20%
where the time goes in v6:
time: 70.1 us; the launch traced here: 69.8 us
  Pallas kernels  23.3 us (33%)
  waiting for transfers between devices  22.4 us (32%)
  starting transfers between devices  22.1 us (32%)
  local copies, waits for them, and re-layouts  1.06 us (2%)
  between operations  0.91 us (1%)
    ppermute x14, waiting for transfers between devices, send(): return lax.ppermute(array, ALL, pairs(move))  22.4 us
    ppermute x14, starting transfers between devices, send(): return lax.ppermute(array, ALL, pairs(move))  16.6 us
    pallas_call x4, Pallas kernels, attend(): pl.pallas_call(functools.partial(attend_kernel, state is None), in_specs=...  11.9 us
    pallas_call x2, Pallas kernels, pool(): pl.pallas_call(functools.partial(pool_kernel, sides), in_specs=[hbm] * 2,...  8.45 us
    ppermute x1, starting transfers between devices, block_plan(): lax.ppermute(far, 'ctx', [(i, (i + (1 if i % 2 else 15)) % 16) for i in r...  5.5 us
  transfers between devices with their start and end apart: 15, of which 5 were waited for; matrix products, arithmetic and copies ran while one was open for 0% of the time, Pallas kernels for 20%

profile of v6, /device:TPU:0, one launch (start us, length us, event | category | flops | bytes accessed | tf_op | source)
XLA Modules:
  0.0 69.8 jit_solution(3812459316478994296)
XLA Ops:
  0.0 4.2 %pool.3 = (f32[192,512]{1,0:T(8,128)}, f32[192,512]{1,0:T(8,128)}) custom-call(s32[32,128]{1,0:T(8,128)} %bitcast.22, bf16[4096,512]{1,0:T(8,128)(2,1)} %messages_hbm.3), custom_call_target="tpu_custom_call" | custom-call | flops 1000000000 | bytes 5000000 | tf_op jit(solution)/shard_map/pool/pallas_call | solution.py:101
  4.3 5.5 %collective-permute-start = (f32[192,512]{1,0:T(8,128)}, f32[192,512]{1,0:T(8,128)S(1)}, u32[]{:S(2)}, u32[]{:S(2)}) collective-permute-start(f32[192,512]{1,0:T(8,128)} %get-tuple-element.9), channel_id=1, source_target_pairs={{0,30},{2,4},{4,2},{6,8},{8,6},{10,12},{12,10},{14,16},{16,14},{18... | collective-permute-start | bytes 1179656 | tf_op jit(solution)/shard_map/ppermute | solution.py:418
  9.7 0.0 collective-permute-start.1
  10.4 4.2 %pool.2.a_ref = f32[192,512]{1,0:T(8,128)} custom-call(s32[32,128]{1,0:T(8,128)} %bitcast.23, bf16[4096,512]{1,0:T(8,128)(2,1)} %messages_hbm.3), custom_call_target="tpu_custom_call" | custom-call | flops 1000000000 | bytes 5000000 | tf_op jit(solution)/shard_map/pool/pallas_call | solution.py:101
  14.6 0.0 copy-start.1
  14.6 1.0 %copy-done.1 = f32[192,512]{1,0:T(8,128)S(1)} copy-done((f32[192,512]{1,0:T(8,128)S(1)}, f32[192,512]{1,0:T(8,128)}, u32[]{:S(2)}) %copy-start.1) | copy-done | bytes 393240
  15.6 0.0 collective-permute-done.far_ref
  15.7 0.0 collective-permute-done.1.near_ref
  15.7 0.1 settle.1.a_ref
  15.7 3.3 %collective-permute-start.2 = (bf16[192,512]{1,0:T(8,128)(2,1)S(1)}, bf16[192,512]{1,0:T(8,128)(2,1)S(1)}, u32[]{:S(2)}, u32[]{:S(2)}) collective-permute-start(bf16[192,512]{1,0:T(8,128)(2,1)S(1)} %settle.1.a_ref), channel_id=1, source_target_pairs={{0,4},{1,5},{2,3},{3,2},{4,0},{5,1},{6,7},{7,6},{8,12},{9,13},{10,... | collective-permute-start | bytes 589832 | tf_op jit(solution)/shard_map/ppermute | solution.py:387
  19.0 2.6 %collective-permute-start.8 = (bf16[192,512]{1,0:T(8,128)(2,1)S(1)}, bf16[192,512]{1,0:T(8,128)(2,1)S(1)}, u32[]{:S(2)}, u32[]{:S(2)}) collective-permute-start(bf16[192,512]{1,0:T(8,128)(2,1)S(1)} %settle.1.a_ref), channel_id=1, source_target_pairs={{0,16},{1,17},{2,18},{3,19},{4,20},{5,21},{6,22},{7,23},{8,24},{9,... | collective-permute-start | bytes 589832 | tf_op jit(solution)/shard_map/ppermute | solution.py:387
  21.6 1.3 %collective-permute-start.5 = (bf16[192,512]{1,0:T(8,128)(2,1)S(1)}, bf16[192,512]{1,0:T(8,128)(2,1)S(1)}, u32[]{:S(2)}, u32[]{:S(2)}) collective-permute-start(bf16[192,512]{1,0:T(8,128)(2,1)S(1)} %settle.1.a_ref), channel_id=1, source_target_pairs={{0,24},{1,25},{2,26},{3,27},{4,28},{5,29},{6,30},{7,31},{8,16},{9,... | collective-permute-start | bytes 589832 | tf_op jit(solution)/shard_map/ppermute | solution.py:387
  23.0 0.0 collective-permute-done.2.b_ref
  23.0 0.0 copy-start.2
  23.0 0.0 copy-start.5
  23.0 1.6 %collective-permute-start.3 = (bf16[384,512]{1,0:T(8,128)(2,1)S(1)}, bf16[384,512]{1,0:T(8,128)(2,1)S(1)}, u32[]{:S(2)}, u32[]{:S(2)}) collective-permute-start(bf16[384,512]{1,0:T(8,128)(2,1)S(1)} %join.3.first_ref.rest_0_.refs_2_), channel_id=1, source_target_pairs={{0,1},{1,0},{2,6},{3,7},{4,5},{5,4},{6,2},{7,3},{8,9},{9,8},{10,14... | collective-permute-start | bytes 1179656 | tf_op jit(solution)/shard_map/ppermute | solution.py:387
  24.6 1.3 %collective-permute-start.11 = (bf16[384,512]{1,0:T(8,128)(2,1)S(1)}, bf16[384,512]{1,0:T(8,128)(2,1)S(1)}, u32[]{:S(2)}, u32[]{:S(2)}) collective-permute-start(bf16[384,512]{1,0:T(8,128)(2,1)S(1)} %join.3.first_ref.rest_0_.refs_2_), channel_id=1, source_target_pairs={{0,8},{1,9},{2,10},{3,11},{4,12},{5,13},{6,14},{7,15},{8,0},{9,1},... | collective-permute-start | bytes 1179656 | tf_op jit(solution)/shard_map/ppermute | solution.py:387
  25.9 10.1 %collective-permute-done.8.a_ref = bf16[192,512]{1,0:T(8,128)(2,1)S(1)} collective-permute-done((bf16[192,512]{1,0:T(8,128)(2,1)S(1)}, bf16[192,512]{1,0:T(8,128)(2,1)S(1)}, u32[]{:S(2)}, u32[]{:S(2)}) %collective-permute-start.8) | collective-permute-done | bytes 196640 | tf_op jit(solution)/shard_map/ppermute | solution.py:387
  36.0 0.1 collective-permute-start.9
  36.1 0.0 collective-permute-done.3.second_ref.refs_3_
  36.1 0.0 copy-done.2
  36.1 0.0 copy-done.5
  36.1 0.6 queries.1
  36.7 0.0 copy-start.3
  36.7 0.0 copy-start.4
  36.7 0.1 collective-permute-start.4
  36.8 0.0 collective-permute-done.5.a_ref
  36.8 2.1 %collective-permute-start.6 = (bf16[192,512]{1,0:T(8,128)(2,1)S(1)}, bf16[192,512]{1,0:T(8,128)(2,1)S(1)}, u32[]{:S(2)}, u32[]{:S(2)}) collective-permute-start(bf16[192,512]{1,0:T(8,128)(2,1)S(1)} %after.4.a_ref), channel_id=1, source_target_pairs={{0,4},{1,5},{2,3},{3,2},{4,0},{5,1},{6,7},{7,6},{8,12},{9,13},{10,... | collective-permute-start | bytes 589832 | tf_op jit(solution)/shard_map/ppermute | solution.py:387
  38.9 1.0 %collective-permute-start.12 = (bf16[384,512]{1,0:T(8,128)(2,1)S(1)}, bf16[384,512]{1,0:T(8,128)(2,1)S(1)}, u32[]{:S(2)}, u32[]{:S(2)}) collective-permute-start(bf16[384,512]{1,0:T(8,128)(2,1)S(1)} %collective-permute-done.3.second_ref.refs_3_), channel_id=1, source_target_pairs={{0,8},{1,9},{2,10},{3,11},{4,12},{5,13},{6,14},{7,15},{8,0},{9,1},... | collective-permute-start | bytes 1179656 | tf_op jit(solution)/shard_map/ppermute | solution.py:387
  39.8 0.0 collective-permute-done.4.refs_1_
  39.9 0.0 copy-done.3
  39.9 0.0 copy-done.4
  39.9 2.8 %attend.4.rest_0_.refs_7_ = f32[536,384]{1,0:T(8,128)S(1)} custom-call(bf16[192,512]{1,0:T(8,128)(2,1)S(1)} %get-tuple-element.11.rest_0_.refs_0_, bf16[192,512]{1,0:T(8,128)(2,1)S(1)} %collective-permute-done.4.refs_1_, bf16[384,512]{1,0:T(8,128)(2,1)S(1)} %join.3.first_ref.rest_0_.refs_2_, bf16[384,512]{1,0:T(8,128)(2,1)S(1)} %collective-permute-done.3.second_ref.refs_3_, ...), custom_call_target="tpu_custom_call" | custom-call | flops 2000000000 | bytes 1 | tf_op jit(solution)/shard_map/attend/pallas_call | solution.py:288
  42.7 0.0 collective-permute-done.9.b_ref
  42.7 0.6 collective-permute-start.10
  43.4 0.5 collective-permute-done.6.b_ref
  43.9 1.1 %collective-permute-start.7 = (bf16[384,512]{1,0:T(8,128)(2,1)S(1)}, bf16[384,512]{1,0:T(8,128)(2,1)S(1)}, u32[]{:S(2)}, u32[]{:S(2)}) collective-permute-start(bf16[384,512]{1,0:T(8,128)(2,1)S(1)} %join.4.refs_2_), channel_id=1, source_target_pairs={{0,1},{1,0},{2,6},{3,7},{4,5},{5,4},{6,2},{7,3},{8,9},{9,8},{10,14... | collective-permute-start | bytes 1179656 | tf_op jit(solution)/shard_map/ppermute | solution.py:387
  44.9 0.0 collective-permute-done.11.refs_2_
  44.9 4.4 %collective-permute-done.12.refs_3_ = bf16[384,512]{1,0:T(8,128)(2,1)S(1)} collective-permute-done((bf16[384,512]{1,0:T(8,128)(2,1)S(1)}, bf16[384,512]{1,0:T(8,128)(2,1)S(1)}, u32[]{:S(2)}, u32[]{:S(2)}) %collective-permute-start.12) | collective-permute-done | bytes 393248 | tf_op jit(solution)/shard_map/ppermute | solution.py:387
  49.3 3.0 %attend.5.refs_7_ = f32[536,384]{1,0:T(8,128)S(1)} custom-call(bf16[192,512]{1,0:T(8,128)(2,1)S(1)} %get-tuple-element.11.rest_0_.refs_0_, bf16[192,512]{1,0:T(8,128)(2,1)S(1)} %collective-permute-done.4.refs_1_, bf16[384,512]{1,0:T(8,128)(2,1)S(1)} %collective-permute-done.11.refs_2_, ...), custom_call_target="tpu_custom_call", output_to_operand_aliasing={{}: (7, {})} | custom-call | flops 2000000000 | bytes 1 | tf_op jit(solution)/shard_map/attend/pallas_call | solution.py:288
  52.3 0.0 collective-permute-done.10.refs_3_
  52.3 3.0 %attend.6.refs_7_ = f32[536,384]{1,0:T(8,128)S(1)} custom-call(bf16[192,512]{1,0:T(8,128)(2,1)S(1)} %get-tuple-element.11.rest_0_.refs_0_, bf16[192,512]{1,0:T(8,128)(2,1)S(1)} %collective-permute-done.4.refs_1_, bf16[384,512]{1,0:T(8,128)(2,1)S(1)} %join.5.refs_2_, ...), custom_call_target="tpu_custom_call", output_to_operand_aliasing={{}: (7, {})} | custom-call | flops 2000000000 | bytes 1 | tf_op jit(solution)/shard_map/attend/pallas_call | solution.py:288
  55.4 0.0 copy-start
  55.4 0.0 collective-permute-done.7.refs_3_
  55.4 3.0 %attend.7.mine_ref = f32[536,384]{1,0:T(8,128)S(1)} custom-call(bf16[192,512]{1,0:T(8,128)(2,1)S(1)} %get-tuple-element.11.rest_0_.refs_0_, bf16[192,512]{1,0:T(8,128)(2,1)S(1)} %collective-permute-done.4.refs_1_, bf16[384,512]{1,0:T(8,128)(2,1)S(1)} %join.4.refs_2_, ...), custom_call_target="tpu_custom_call", output_to_operand_aliasing={{}: (7, {})} | custom-call | flops 2000000000 | bytes 1 | tf_op jit(solution)/shard_map/attend/pallas_call | solution.py:288
  58.4 0.1 collective-permute-start.13
  58.5 1.9 %collective-permute-done.13.other_ref = f32[536,256]{1,0:T(8,128)S(1)} collective-permute-done((f32[536,256]{1,0:T(8,128)S(1)}, f32[536,256]{1,0:T(8,128)S(1)}, u32[]{:S(2)}, u32[]{:S(2)}) %collective-permute-start.13) | collective-permute-done | bytes 548896 | tf_op jit(solution)/shard_map/ppermute | solution.py:387
  60.4 1.0 %combine.1.attended_ref = bf16[208,512]{1,0:T(8,128)(2,1)S(1)} custom-call(f32[536,384]{1,0:T(8,128)S(1)} %attend.7.mine_ref, f32[536,256]{1,0:T(8,128)S(1)} %collective-permute-done.13.other_ref), custom_call_target="tpu_custom_call" | custom-call | tf_op jit(solution)/shard_map/combine/pallas_call | solution.py:331
  61.4 1.6 %collective-permute-start.14 = (bf16[208,512]{1,0:T(8,128)(2,1)S(1)}, bf16[208,512]{1,0:T(8,128)(2,1)S(1)}, u32[]{:S(2)}, u32[]{:S(2)}) collective-permute-start(bf16[208,512]{1,0:T(8,128)(2,1)S(1)} %combine.1.attended_ref), channel_id=1, source_target_pairs={{0,1},{1,0},{2,3},{3,2},{4,5},{5,4},{6,7},{7,6},{8,9},{9,8},{10,11... | collective-permute-start | bytes 638984 | tf_op jit(solution)/shard_map/ppermute | solution.py:387
  63.0 0.0 copy-done
  63.0 0.3 own_branch.1.branch_ref
  63.3 5.5 %collective-permute-done.14.attended_ref = bf16[208,512]{1,0:T(8,128)(2,1)S(1)} collective-permute-done((bf16[208,512]{1,0:T(8,128)(2,1)S(1)}, bf16[208,512]{1,0:T(8,128)(2,1)S(1)}, u32[]{:S(2)}, u32[]{:S(2)}) %collective-permute-start.14) | collective-permute-done | bytes 213024 | tf_op jit(solution)/shard_map/ppermute | solution.py:387
  68.8 1.0 %finish.1 = bf16[256,512]{1,0:T(8,128)(2,1)} custom-call(f32[208,512]{1,0:T(8,128)S(1)} %own_branch.1.branch_ref, bf16[208,512]{1,0:T(8,128)(2,1)S(1)} %collective-permute-done.14.attended_ref, bf16[2,512,512]{2,1,0:T(8,128)(2,1)S(1)} %bitcast.7, bf16[192,512]{1,0:T(8,128)(2,1)S(1)} %get-tuple-element.12.normed_ref), custom_call_target="tpu_custom_call" | custom-call | tf_op jit(solution)/shard_map/finish/pallas_call | solution.py:365
  (7 shorter events, 0.2 us)
Async XLA Ops:
  4.3 11.4 %collective-permute-start = (f32[192,512]{1,0:T(8,128)}, f32[192,512]{1,0:T(8,128)S(1)}, u32[]{:S(2)}, u32[]{:S(2)}) collective-permute-start(f32[192,512]{1,0:T(8,128)} %get-tuple-element.9), channel_id=1, source_target_pairs={{0,30},{2,4},{4,2},{6,8},{8,6},{10,12},{12,10},{14,16},{16,14},{18... | collective-permute-start | bytes 1179656 | tf_op jit(solution)/shard_map/ppermute | solution.py:418
  9.7 5.9 %collective-permute-start.1 = (f32[192,512]{1,0:T(8,128)}, f32[192,512]{1,0:T(8,128)S(1)}, u32[]{:S(2)}, u32[]{:S(2)}) collective-permute-start(f32[192,512]{1,0:T(8,128)} %get-tuple-element.10), channel_id=1, source_target_pairs={{0,2},{1,3},{2,0},{3,1},{4,6},{5,7},{6,4},{7,5},{8,10},{9,11},{10,... | collective-permute-start | bytes 1179656 | tf_op jit(solution)/shard_map/ppermute | solution.py:387
  14.6 1.0 %copy-start.1 = (f32[192,512]{1,0:T(8,128)S(1)}, f32[192,512]{1,0:T(8,128)}, u32[]{:S(2)}) copy-start(f32[192,512]{1,0:T(8,128)} %pool.2.a_ref) | copy-start | bytes 1179652
  15.7 7.2 %collective-permute-start.2 = (bf16[192,512]{1,0:T(8,128)(2,1)S(1)}, bf16[192,512]{1,0:T(8,128)(2,1)S(1)}, u32[]{:S(2)}, u32[]{:S(2)}) collective-permute-start(bf16[192,512]{1,0:T(8,128)(2,1)S(1)} %settle.1.a_ref), channel_id=1, source_target_pairs={{0,4},{1,5},{2,3},{3,2},{4,0},{5,1},{6,7},{7,6},{8,12},{9,13},{10,... | collective-permute-start | bytes 589832 | tf_op jit(solution)/shard_map/ppermute | solution.py:387
  19.0 16.9 %collective-permute-start.8 = (bf16[192,512]{1,0:T(8,128)(2,1)S(1)}, bf16[192,512]{1,0:T(8,128)(2,1)S(1)}, u32[]{:S(2)}, u32[]{:S(2)}) collective-permute-start(bf16[192,512]{1,0:T(8,128)(2,1)S(1)} %settle.1.a_ref), channel_id=1, source_target_pairs={{0,16},{1,17},{2,18},{3,19},{4,20},{5,21},{6,22},{7,23},{8,24},{9,... | collective-permute-start | bytes 589832 | tf_op jit(solution)/shard_map/ppermute | solution.py:387
  21.6 15.1 %collective-permute-start.5 = (bf16[192,512]{1,0:T(8,128)(2,1)S(1)}, bf16[192,512]{1,0:T(8,128)(2,1)S(1)}, u32[]{:S(2)}, u32[]{:S(2)}) collective-permute-start(bf16[192,512]{1,0:T(8,128)(2,1)S(1)} %settle.1.a_ref), channel_id=1, source_target_pairs={{0,24},{1,25},{2,26},{3,27},{4,28},{5,29},{6,30},{7,31},{8,16},{9,... | collective-permute-start | bytes 589832 | tf_op jit(solution)/shard_map/ppermute | solution.py:387
  23.0 13.1 %copy-start.2 = (bf16[1024,512]{1,0:T(8,128)(2,1)S(1)}, bf16[1024,512]{1,0:T(8,128)(2,1)}, u32[]{:S(2)}) copy-start(bf16[1024,512]{1,0:T(8,128)(2,1)} %param.12) | copy-start | bytes 3145732
  23.0 13.1 %copy-start.5 = (f32[1024]{0:T(1024)S(1)}, f32[1024]{0:T(1024)}, u32[]{:S(2)}) copy-start(f32[1024]{0:T(1024)} %param.11) | copy-start | bytes 12292
  23.0 13.0 %collective-permute-start.3 = (bf16[384,512]{1,0:T(8,128)(2,1)S(1)}, bf16[384,512]{1,0:T(8,128)(2,1)S(1)}, u32[]{:S(2)}, u32[]{:S(2)}) collective-permute-start(bf16[384,512]{1,0:T(8,128)(2,1)S(1)} %join.3.first_ref.rest_0_.refs_2_), channel_id=1, source_target_pairs={{0,1},{1,0},{2,6},{3,7},{4,5},{5,4},{6,2},{7,3},{8,9},{9,8},{10,14... | collective-permute-start | bytes 1179656 | tf_op jit(solution)/shard_map/ppermute | solution.py:387
  24.6 20.3 %collective-permute-start.11 = (bf16[384,512]{1,0:T(8,128)(2,1)S(1)}, bf16[384,512]{1,0:T(8,128)(2,1)S(1)}, u32[]{:S(2)}, u32[]{:S(2)}) collective-permute-start(bf16[384,512]{1,0:T(8,128)(2,1)S(1)} %join.3.first_ref.rest_0_.refs_2_), channel_id=1, source_target_pairs={{0,8},{1,9},{2,10},{3,11},{4,12},{5,13},{6,14},{7,15},{8,0},{9,1},... | collective-permute-start | bytes 1179656 | tf_op jit(solution)/shard_map/ppermute | solution.py:387
  36.0 6.7 %collective-permute-start.9 = (bf16[192,512]{1,0:T(8,128)(2,1)S(1)}, bf16[192,512]{1,0:T(8,128)(2,1)S(1)}, u32[]{:S(2)}, u32[]{:S(2)}) collective-permute-start(bf16[192,512]{1,0:T(8,128)(2,1)S(1)} %after.5.a_ref), channel_id=1, source_target_pairs={{0,4},{1,5},{2,3},{3,2},{4,0},{5,1},{6,7},{7,6},{8,12},{9,13},{10,... | collective-permute-start | bytes 589832 | tf_op jit(solution)/shard_map/ppermute | solution.py:387
  36.7 3.2 %copy-start.3 = (bf16[1024,512]{1,0:T(8,128)(2,1)S(1)}, bf16[1024,512]{1,0:T(8,128)(2,1)}, u32[]{:S(2)}) copy-start(bf16[1024,512]{1,0:T(8,128)(2,1)} %param.13) | copy-start | bytes 3145732
  36.7 3.2 %copy-start.4 = (bf16[1024,512]{1,0:T(8,128)(2,1)S(1)}, bf16[1024,512]{1,0:T(8,128)(2,1)}, u32[]{:S(2)}) copy-start(bf16[1024,512]{1,0:T(8,128)(2,1)} %param.14) | copy-start | bytes 3145732
  36.7 3.2 %collective-permute-start.4 = (bf16[192,512]{1,0:T(8,128)(2,1)S(1)}, bf16[192,512]{1,0:T(8,128)(2,1)S(1)}, u32[]{:S(2)}, u32[]{:S(2)}) collective-permute-start(bf16[192,512]{1,0:T(8,128)(2,1)S(1)} %get-tuple-element.11.rest_0_.refs_0_), channel_id=1, source_target_pairs={{0,2},{1,3},{2,0},{3,1},{4,6},{5,7},{6,4},{7,5},{8,10},{9,11},{10,... | collective-permute-start | bytes 589832 | tf_op jit(solution)/shard_map/ppermute | solution.py:387
  36.8 7.0 %collective-permute-start.6 = (bf16[192,512]{1,0:T(8,128)(2,1)S(1)}, bf16[192,512]{1,0:T(8,128)(2,1)S(1)}, u32[]{:S(2)}, u32[]{:S(2)}) collective-permute-start(bf16[192,512]{1,0:T(8,128)(2,1)S(1)} %after.4.a_ref), channel_id=1, source_target_pairs={{0,4},{1,5},{2,3},{3,2},{4,0},{5,1},{6,7},{7,6},{8,12},{9,13},{10,... | collective-permute-start | bytes 589832 | tf_op jit(solution)/shard_map/ppermute | solution.py:387
  38.9 10.4 %collective-permute-start.12 = (bf16[384,512]{1,0:T(8,128)(2,1)S(1)}, bf16[384,512]{1,0:T(8,128)(2,1)S(1)}, u32[]{:S(2)}, u32[]{:S(2)}) collective-permute-start(bf16[384,512]{1,0:T(8,128)(2,1)S(1)} %collective-permute-done.3.second_ref.refs_3_), channel_id=1, source_target_pairs={{0,8},{1,9},{2,10},{3,11},{4,12},{5,13},{6,14},{7,15},{8,0},{9,1},... | collective-permute-start | bytes 1179656 | tf_op jit(solution)/shard_map/ppermute | solution.py:387
  42.7 9.6 %collective-permute-start.10 = (bf16[384,512]{1,0:T(8,128)(2,1)S(1)}, bf16[384,512]{1,0:T(8,128)(2,1)S(1)}, u32[]{:S(2)}, u32[]{:S(2)}) collective-permute-start(bf16[384,512]{1,0:T(8,128)(2,1)S(1)} %join.5.refs_2_), channel_id=1, source_target_pairs={{0,1},{1,0},{2,6},{3,7},{4,5},{5,4},{6,2},{7,3},{8,9},{9,8},{10,14... | collective-permute-start | bytes 1179656 | tf_op jit(solution)/shard_map/ppermute | solution.py:387
  43.9 11.5 %collective-permute-start.7 = (bf16[384,512]{1,0:T(8,128)(2,1)S(1)}, bf16[384,512]{1,0:T(8,128)(2,1)S(1)}, u32[]{:S(2)}, u32[]{:S(2)}) collective-permute-start(bf16[384,512]{1,0:T(8,128)(2,1)S(1)} %join.4.refs_2_), channel_id=1, source_target_pairs={{0,1},{1,0},{2,6},{3,7},{4,5},{5,4},{6,2},{7,3},{8,9},{9,8},{10,14... | collective-permute-start | bytes 1179656 | tf_op jit(solution)/shard_map/ppermute | solution.py:387
  55.4 7.6 %copy-start = (bf16[1024,512]{1,0:T(8,128)(2,1)S(1)}, bf16[1024,512]{1,0:T(8,128)(2,1)}, u32[]{:S(2)}) copy-start(bf16[1024,512]{1,0:T(8,128)(2,1)} %param.15) | copy-start | bytes 3145732
  58.4 2.0 %collective-permute-start.13 = (f32[536,256]{1,0:T(8,128)S(1)}, f32[536,256]{1,0:T(8,128)S(1)}, u32[]{:S(2)}, u32[]{:S(2)}) collective-permute-start(f32[536,256]{1,0:T(8,128)S(1)} %slice.4), channel_id=1, source_target_pairs={{0,2},{1,3},{2,0},{3,1},{4,6},{5,7},{6,4},{7,5},{8,10},{9,11},{10,... | collective-permute-start | bytes 1646600 | tf_op jit(solution)/shard_map/ppermute | solution.py:387
  61.4 7.4 %collective-permute-start.14 = (bf16[208,512]{1,0:T(8,128)(2,1)S(1)}, bf16[208,512]{1,0:T(8,128)(2,1)S(1)}, u32[]{:S(2)}, u32[]{:S(2)}) collective-permute-start(bf16[208,512]{1,0:T(8,128)(2,1)S(1)} %combine.1.attended_ref), channel_id=1, source_target_pairs={{0,1},{1,0},{2,3},{3,2},{4,5},{5,4},{6,7},{7,6},{8,9},{9,8},{10,11... | collective-permute-start | bytes 638984 | tf_op jit(solution)/shard_map/ppermute | solution.py:387

commit v7 on v6

--- a/solution.py
+++ b/solution.py
@@ -39,7 +39,7 @@
     return lax.dot_general(a, b, (contract, ((), ())), preferred_element_type=F32)
 
 
-COPIES = 4
+COPIES = 2
 GROUP = 8
 
 
@@ -354,19 +354,31 @@
     )(attended, w_out)
 
 
-def finish_kernel(branch_ref, attended_ref, w_ref, normed_ref, out_ref):
-    branch = branch_ref[...] + dot(attended_ref[...], w_ref[1 - lax.axis_index("head")])
-    out_ref[:LIVE_MAX, :] = (branch[:LIVE_MAX] + normed_ref[...].astype(F32)).astype(BF16)
-    rest = out_ref.shape[0] - LIVE_MAX
-    out_ref[LIVE_MAX:, :] = jnp.broadcast_to(branch[LIVE_MAX : LIVE_MAX + 1], (rest, branch.shape[1])).astype(BF16)
+def finish_kernel(branch_ref, attended_ref, w_ref, normed_ref, out_hbm, out, sems):
+    w = w_ref.at[1 - lax.axis_index("head")]
+    parts = sems.shape[0]
+    width = out.shape[1] // parts
+    rest = out.shape[0] - LIVE_MAX
+    stores = []
+    for part in range(parts):
+        at = slice(part * width, (part + 1) * width)
+        branch = branch_ref[:, at] + dot(attended_ref[...], w[:, at])
+        out[:LIVE_MAX, at] = (branch[:LIVE_MAX] + normed_ref[:, at].astype(F32)).astype(BF16)
+        out[LIVE_MAX:, at] = jnp.broadcast_to(branch[LIVE_MAX : LIVE_MAX + 1], (rest, width)).astype(BF16)
+        stores.append(pltpu.make_async_copy(out.at[:, at], out_hbm.at[:, at], sems.at[part]))
+        stores[-1].start()
+    for store in stores:
+        store.wait()
 
 
 def finish(branch, attended, w_out, normed):
+    shape = (ANCH_DEV, branch.shape[1])
     return pl.pallas_call(
         finish_kernel,
         in_specs=vmem(4),
-        out_specs=pl.BlockSpec(memory_space=pltpu.VMEM),
-        out_shape=jax.ShapeDtypeStruct((ANCH_DEV, branch.shape[1]), BF16),
+        out_specs=pl.BlockSpec(memory_space=pl.ANY),
+        out_shape=jax.ShapeDtypeStruct(shape, BF16),
+        scratch_shapes=[pltpu.VMEM(shape, BF16), pltpu.SemaphoreType.DMA((2,))],
         compiler_params=params(),
         name="finish",
     )(branch, attended, w_out, normed)

time: 70.1 us -> 70.3 us (level)
  transfers between devices with their start and end apart: 15 -> 15, of which waited for: 5 -> 6; matrix products, arithmetic and copies ran while one was open for 0% -> 0% of each run, Pallas kernels for 20% -> 19%
where the time goes in v7:
time: 70.3 us; the launch traced here: 70 us
  waiting for transfers between devices  22.8 us (32%)
  Pallas kernels  22.7 us (32%)
  starting transfers between devices  22.3 us (32%)
  local copies, waits for them, and re-layouts  1.06 us (2%)
  between operations  1.05 us (1%)
    ppermute x14, waiting for transfers between devices, send(): return lax.ppermute(array, ALL, pairs(move))  22.4 us
    ppermute x14, starting transfers between devices, send(): return lax.ppermute(array, ALL, pairs(move))  16.8 us
    pallas_call x4, Pallas kernels, attend(): pl.pallas_call(functools.partial(attend_kernel, state is None), in_specs=...  11.9 us
    pallas_call x2, Pallas kernels, pool(): pl.pallas_call(functools.partial(pool_kernel, sides), in_specs=[hbm] * 2,...  7.86 us
    ppermute x1, starting transfers between devices, block_plan(): lax.ppermute(far, 'ctx', [(i, (i + (1 if i % 2 else 15)) % 16) for i in r...  5.51 us
  transfers between devices with their start and end apart: 15, of which 6 were waited for; matrix products, arithmetic and copies ran while one was open for 0% of the time, Pallas kernels for 19%

profile of v7, /device:TPU:0, one launch (start us, length us, event | category | flops | bytes accessed | tf_op | source)
XLA Modules:
  0.0 70.0 jit_solution(16603237006264241424)
XLA Ops:
  0.0 4.3 %pool.3 = (f32[192,512]{1,0:T(8,128)}, f32[192,512]{1,0:T(8,128)}) custom-call(s32[32,128]{1,0:T(8,128)} %bitcast.22, bf16[4096,512]{1,0:T(8,128)(2,1)} %messages_hbm.3), custom_call_target="tpu_custom_call" | custom-call | flops 1000000000 | bytes 5000000 | tf_op jit(solution)/shard_map/pool/pallas_call | solution.py:101
  4.3 5.5 %collective-permute-start = (f32[192,512]{1,0:T(8,128)}, f32[192,512]{1,0:T(8,128)S(1)}, u32[]{:S(2)}, u32[]{:S(2)}) collective-permute-start(f32[192,512]{1,0:T(8,128)} %get-tuple-element.9), channel_id=1, source_target_pairs={{0,30},{2,4},{4,2},{6,8},{8,6},{10,12},{12,10},{14,16},{16,14},{18... | collective-permute-start | bytes 1179656 | tf_op jit(solution)/shard_map/ppermute | solution.py:430
  9.8 0.0 collective-permute-start.1
  10.4 3.6 %pool.2.a_ref = f32[192,512]{1,0:T(8,128)} custom-call(s32[32,128]{1,0:T(8,128)} %bitcast.23, bf16[4096,512]{1,0:T(8,128)(2,1)} %messages_hbm.3), custom_call_target="tpu_custom_call" | custom-call | flops 1000000000 | bytes 5000000 | tf_op jit(solution)/shard_map/pool/pallas_call | solution.py:101
  14.0 0.0 copy-start.1
  14.1 1.0 %copy-done.1 = f32[192,512]{1,0:T(8,128)S(1)} copy-done((f32[192,512]{1,0:T(8,128)S(1)}, f32[192,512]{1,0:T(8,128)}, u32[]{:S(2)}) %copy-start.1) | copy-done | bytes 393240
  15.1 0.5 collective-permute-done.far_ref
  15.6 0.0 collective-permute-done.1.near_ref
  15.6 0.1 settle.1.a_ref
  15.6 3.4 %collective-permute-start.2 = (bf16[192,512]{1,0:T(8,128)(2,1)S(1)}, bf16[192,512]{1,0:T(8,128)(2,1)S(1)}, u32[]{:S(2)}, u32[]{:S(2)}) collective-permute-start(bf16[192,512]{1,0:T(8,128)(2,1)S(1)} %settle.1.a_ref), channel_id=1, source_target_pairs={{0,4},{1,5},{2,3},{3,2},{4,0},{5,1},{6,7},{7,6},{8,12},{9,13},{10,... | collective-permute-start | bytes 589832 | tf_op jit(solution)/shard_map/ppermute | solution.py:399
  19.1 2.6 %collective-permute-start.8 = (bf16[192,512]{1,0:T(8,128)(2,1)S(1)}, bf16[192,512]{1,0:T(8,128)(2,1)S(1)}, u32[]{:S(2)}, u32[]{:S(2)}) collective-permute-start(bf16[192,512]{1,0:T(8,128)(2,1)S(1)} %settle.1.a_ref), channel_id=1, source_target_pairs={{0,16},{1,17},{2,18},{3,19},{4,20},{5,21},{6,22},{7,23},{8,24},{9,... | collective-permute-start | bytes 589832 | tf_op jit(solution)/shard_map/ppermute | solution.py:399
  21.7 1.3 %collective-permute-start.5 = (bf16[192,512]{1,0:T(8,128)(2,1)S(1)}, bf16[192,512]{1,0:T(8,128)(2,1)S(1)}, u32[]{:S(2)}, u32[]{:S(2)}) collective-permute-start(bf16[192,512]{1,0:T(8,128)(2,1)S(1)} %settle.1.a_ref), channel_id=1, source_target_pairs={{0,24},{1,25},{2,26},{3,27},{4,28},{5,29},{6,30},{7,31},{8,16},{9,... | collective-permute-start | bytes 589832 | tf_op jit(solution)/shard_map/ppermute | solution.py:399
  23.0 0.0 collective-permute-done.2.b_ref
  23.0 0.0 copy-start.2
  23.0 0.0 copy-start.5
  23.1 1.6 %collective-permute-start.3 = (bf16[384,512]{1,0:T(8,128)(2,1)S(1)}, bf16[384,512]{1,0:T(8,128)(2,1)S(1)}, u32[]{:S(2)}, u32[]{:S(2)}) collective-permute-start(bf16[384,512]{1,0:T(8,128)(2,1)S(1)} %join.3.first_ref.rest_0_.refs_2_), channel_id=1, source_target_pairs={{0,1},{1,0},{2,6},{3,7},{4,5},{5,4},{6,2},{7,3},{8,9},{9,8},{10,14... | collective-permute-start | bytes 1179656 | tf_op jit(solution)/shard_map/ppermute | solution.py:399
  24.6 1.3 %collective-permute-start.11 = (bf16[384,512]{1,0:T(8,128)(2,1)S(1)}, bf16[384,512]{1,0:T(8,128)(2,1)S(1)}, u32[]{:S(2)}, u32[]{:S(2)}) collective-permute-start(bf16[384,512]{1,0:T(8,128)(2,1)S(1)} %join.3.first_ref.rest_0_.refs_2_), channel_id=1, source_target_pairs={{0,8},{1,9},{2,10},{3,11},{4,12},{5,13},{6,14},{7,15},{8,0},{9,1},... | collective-permute-start | bytes 1179656 | tf_op jit(solution)/shard_map/ppermute | solution.py:399
  25.9 10.1 %collective-permute-done.8.a_ref = bf16[192,512]{1,0:T(8,128)(2,1)S(1)} collective-permute-done((bf16[192,512]{1,0:T(8,128)(2,1)S(1)}, bf16[192,512]{1,0:T(8,128)(2,1)S(1)}, u32[]{:S(2)}, u32[]{:S(2)}) %collective-permute-start.8) | collective-permute-done | bytes 196640 | tf_op jit(solution)/shard_map/ppermute | solution.py:399
  36.0 0.1 collective-permute-start.9
  36.1 0.0 collective-permute-done.3.second_ref.refs_3_
  36.1 0.0 copy-done.2
  36.1 0.0 copy-done.5
  36.1 0.6 queries.1
  36.7 0.0 copy-start.3
  36.7 0.0 copy-start.4
  36.7 0.1 collective-permute-start.4
  36.8 0.0 collective-permute-done.5.a_ref
  36.8 2.1 %collective-permute-start.6 = (bf16[192,512]{1,0:T(8,128)(2,1)S(1)}, bf16[192,512]{1,0:T(8,128)(2,1)S(1)}, u32[]{:S(2)}, u32[]{:S(2)}) collective-permute-start(bf16[192,512]{1,0:T(8,128)(2,1)S(1)} %after.4.a_ref), channel_id=1, source_target_pairs={{0,4},{1,5},{2,3},{3,2},{4,0},{5,1},{6,7},{7,6},{8,12},{9,13},{10,... | collective-permute-start | bytes 589832 | tf_op jit(solution)/shard_map/ppermute | solution.py:399
  38.9 1.0 %collective-permute-start.12 = (bf16[384,512]{1,0:T(8,128)(2,1)S(1)}, bf16[384,512]{1,0:T(8,128)(2,1)S(1)}, u32[]{:S(2)}, u32[]{:S(2)}) collective-permute-start(bf16[384,512]{1,0:T(8,128)(2,1)S(1)} %collective-permute-done.3.second_ref.refs_3_), channel_id=1, source_target_pairs={{0,8},{1,9},{2,10},{3,11},{4,12},{5,13},{6,14},{7,15},{8,0},{9,1},... | collective-permute-start | bytes 1179656 | tf_op jit(solution)/shard_map/ppermute | solution.py:399
  39.9 0.0 collective-permute-done.4.refs_1_
  39.9 0.0 copy-done.3
  39.9 0.0 copy-done.4
  39.9 2.8 %attend.4.rest_0_.refs_7_ = f32[536,384]{1,0:T(8,128)S(1)} custom-call(bf16[192,512]{1,0:T(8,128)(2,1)S(1)} %get-tuple-element.11.rest_0_.refs_0_, bf16[192,512]{1,0:T(8,128)(2,1)S(1)} %collective-permute-done.4.refs_1_, bf16[384,512]{1,0:T(8,128)(2,1)S(1)} %join.3.first_ref.rest_0_.refs_2_, bf16[384,512]{1,0:T(8,128)(2,1)S(1)} %collective-permute-done.3.second_ref.refs_3_, ...), custom_call_target="tpu_custom_call" | custom-call | flops 2000000000 | bytes 1 | tf_op jit(solution)/shard_map/attend/pallas_call | solution.py:288
  42.7 0.0 collective-permute-done.9.b_ref
  42.8 0.6 collective-permute-start.10
  43.4 0.5 collective-permute-done.6.b_ref
  43.9 1.1 %collective-permute-start.7 = (bf16[384,512]{1,0:T(8,128)(2,1)S(1)}, bf16[384,512]{1,0:T(8,128)(2,1)S(1)}, u32[]{:S(2)}, u32[]{:S(2)}) collective-permute-start(bf16[384,512]{1,0:T(8,128)(2,1)S(1)} %join.4.refs_2_), channel_id=1, source_target_pairs={{0,1},{1,0},{2,6},{3,7},{4,5},{5,4},{6,2},{7,3},{8,9},{9,8},{10,14... | collective-permute-start | bytes 1179656 | tf_op jit(solution)/shard_map/ppermute | solution.py:399
  45.0 0.0 collective-permute-done.11.refs_2_
  45.0 4.4 %collective-permute-done.12.refs_3_ = bf16[384,512]{1,0:T(8,128)(2,1)S(1)} collective-permute-done((bf16[384,512]{1,0:T(8,128)(2,1)S(1)}, bf16[384,512]{1,0:T(8,128)(2,1)S(1)}, u32[]{:S(2)}, u32[]{:S(2)}) %collective-permute-start.12) | collective-permute-done | bytes 393248 | tf_op jit(solution)/shard_map/ppermute | solution.py:399
  49.4 3.0 %attend.5.refs_7_ = f32[536,384]{1,0:T(8,128)S(1)} custom-call(bf16[192,512]{1,0:T(8,128)(2,1)S(1)} %get-tuple-element.11.rest_0_.refs_0_, bf16[192,512]{1,0:T(8,128)(2,1)S(1)} %collective-permute-done.4.refs_1_, bf16[384,512]{1,0:T(8,128)(2,1)S(1)} %collective-permute-done.11.refs_2_, ...), custom_call_target="tpu_custom_call", output_to_operand_aliasing={{}: (7, {})} | custom-call | flops 2000000000 | bytes 1 | tf_op jit(solution)/shard_map/attend/pallas_call | solution.py:288
  52.4 0.0 collective-permute-done.10.refs_3_
  52.4 3.0 %attend.6.refs_7_ = f32[536,384]{1,0:T(8,128)S(1)} custom-call(bf16[192,512]{1,0:T(8,128)(2,1)S(1)} %get-tuple-element.11.rest_0_.refs_0_, bf16[192,512]{1,0:T(8,128)(2,1)S(1)} %collective-permute-done.4.refs_1_, bf16[384,512]{1,0:T(8,128)(2,1)S(1)} %join.5.refs_2_, ...), custom_call_target="tpu_custom_call", output_to_operand_aliasing={{}: (7, {})} | custom-call | flops 2000000000 | bytes 1 | tf_op jit(solution)/shard_map/attend/pallas_call | solution.py:288
  55.4 0.0 copy-start
  55.4 0.0 collective-permute-done.7.refs_3_
  55.4 3.0 %attend.7.mine_ref = f32[536,384]{1,0:T(8,128)S(1)} custom-call(bf16[192,512]{1,0:T(8,128)(2,1)S(1)} %get-tuple-element.11.rest_0_.refs_0_, bf16[192,512]{1,0:T(8,128)(2,1)S(1)} %collective-permute-done.4.refs_1_, bf16[384,512]{1,0:T(8,128)(2,1)S(1)} %join.4.refs_2_, ...), custom_call_target="tpu_custom_call", output_to_operand_aliasing={{}: (7, {})} | custom-call | flops 2000000000 | bytes 1 | tf_op jit(solution)/shard_map/attend/pallas_call | solution.py:288
  58.5 0.1 collective-permute-start.13
  58.5 1.9 %collective-permute-done.13.other_ref = f32[536,256]{1,0:T(8,128)S(1)} collective-permute-done((f32[536,256]{1,0:T(8,128)S(1)}, f32[536,256]{1,0:T(8,128)S(1)}, u32[]{:S(2)}, u32[]{:S(2)}) %collective-permute-start.13) | collective-permute-done | bytes 548896 | tf_op jit(solution)/shard_map/ppermute | solution.py:399
  60.5 1.0 %combine.1.attended_ref = bf16[208,512]{1,0:T(8,128)(2,1)S(1)} custom-call(f32[536,384]{1,0:T(8,128)S(1)} %attend.7.mine_ref, f32[536,256]{1,0:T(8,128)S(1)} %collective-permute-done.13.other_ref), custom_call_target="tpu_custom_call" | custom-call | tf_op jit(solution)/shard_map/combine/pallas_call | solution.py:331
  61.4 1.6 %collective-permute-start.14 = (bf16[208,512]{1,0:T(8,128)(2,1)S(1)}, bf16[208,512]{1,0:T(8,128)(2,1)S(1)}, u32[]{:S(2)}, u32[]{:S(2)}) collective-permute-start(bf16[208,512]{1,0:T(8,128)(2,1)S(1)} %combine.1.attended_ref), channel_id=1, source_target_pairs={{0,1},{1,0},{2,3},{3,2},{4,5},{5,4},{6,7},{7,6},{8,9},{9,8},{10,11... | collective-permute-start | bytes 638984 | tf_op jit(solution)/shard_map/ppermute | solution.py:399
  63.0 0.0 copy-done
  63.0 0.3 own_branch.1.branch_ref
  63.3 5.5 %collective-permute-done.14.attended_ref = bf16[208,512]{1,0:T(8,128)(2,1)S(1)} collective-permute-done((bf16[208,512]{1,0:T(8,128)(2,1)S(1)}, bf16[208,512]{1,0:T(8,128)(2,1)S(1)}, u32[]{:S(2)}, u32[]{:S(2)}) %collective-permute-start.14) | collective-permute-done | bytes 213024 | tf_op jit(solution)/shard_map/ppermute | solution.py:399
  68.8 1.0 %finish.1 = bf16[256,512]{1,0:T(8,128)(2,1)} custom-call(f32[208,512]{1,0:T(8,128)S(1)} %own_branch.1.branch_ref, bf16[208,512]{1,0:T(8,128)(2,1)S(1)} %collective-permute-done.14.attended_ref, bf16[2,512,512]{2,1,0:T(8,128)(2,1)S(1)} %bitcast.7, bf16[192,512]{1,0:T(8,128)(2,1)S(1)} %get-tuple-element.12.normed_ref), custom_call_target="tpu_custom_call" | custom-call | tf_op jit(solution)/shard_map/finish/pallas_call | solution.py:376
  (7 shorter events, 0.2 us)
Async XLA Ops:
  4.3 11.3 %collective-permute-start = (f32[192,512]{1,0:T(8,128)}, f32[192,512]{1,0:T(8,128)S(1)}, u32[]{:S(2)}, u32[]{:S(2)}) collective-permute-start(f32[192,512]{1,0:T(8,128)} %get-tuple-element.9), channel_id=1, source_target_pairs={{0,30},{2,4},{4,2},{6,8},{8,6},{10,12},{12,10},{14,16},{16,14},{18... | collective-permute-start | bytes 1179656 | tf_op jit(solution)/shard_map/ppermute | solution.py:430
  9.8 5.8 %collective-permute-start.1 = (f32[192,512]{1,0:T(8,128)}, f32[192,512]{1,0:T(8,128)S(1)}, u32[]{:S(2)}, u32[]{:S(2)}) collective-permute-start(f32[192,512]{1,0:T(8,128)} %get-tuple-element.10), channel_id=1, source_target_pairs={{0,2},{1,3},{2,0},{3,1},{4,6},{5,7},{6,4},{7,5},{8,10},{9,11},{10,... | collective-permute-start | bytes 1179656 | tf_op jit(solution)/shard_map/ppermute | solution.py:399
  14.0 1.0 %copy-start.1 = (f32[192,512]{1,0:T(8,128)S(1)}, f32[192,512]{1,0:T(8,128)}, u32[]{:S(2)}) copy-start(f32[192,512]{1,0:T(8,128)} %pool.2.a_ref) | copy-start | bytes 1179652
  15.6 7.4 %collective-permute-start.2 = (bf16[192,512]{1,0:T(8,128)(2,1)S(1)}, bf16[192,512]{1,0:T(8,128)(2,1)S(1)}, u32[]{:S(2)}, u32[]{:S(2)}) collective-permute-start(bf16[192,512]{1,0:T(8,128)(2,1)S(1)} %settle.1.a_ref), channel_id=1, source_target_pairs={{0,4},{1,5},{2,3},{3,2},{4,0},{5,1},{6,7},{7,6},{8,12},{9,13},{10,... | collective-permute-start | bytes 589832 | tf_op jit(solution)/shard_map/ppermute | solution.py:399
  19.1 16.9 %collective-permute-start.8 = (bf16[192,512]{1,0:T(8,128)(2,1)S(1)}, bf16[192,512]{1,0:T(8,128)(2,1)S(1)}, u32[]{:S(2)}, u32[]{:S(2)}) collective-permute-start(bf16[192,512]{1,0:T(8,128)(2,1)S(1)} %settle.1.a_ref), channel_id=1, source_target_pairs={{0,16},{1,17},{2,18},{3,19},{4,20},{5,21},{6,22},{7,23},{8,24},{9,... | collective-permute-start | bytes 589832 | tf_op jit(solution)/shard_map/ppermute | solution.py:399
  21.7 15.1 %collective-permute-start.5 = (bf16[192,512]{1,0:T(8,128)(2,1)S(1)}, bf16[192,512]{1,0:T(8,128)(2,1)S(1)}, u32[]{:S(2)}, u32[]{:S(2)}) collective-permute-start(bf16[192,512]{1,0:T(8,128)(2,1)S(1)} %settle.1.a_ref), channel_id=1, source_target_pairs={{0,24},{1,25},{2,26},{3,27},{4,28},{5,29},{6,30},{7,31},{8,16},{9,... | collective-permute-start | bytes 589832 | tf_op jit(solution)/shard_map/ppermute | solution.py:399
  23.0 13.1 %copy-start.2 = (bf16[1024,512]{1,0:T(8,128)(2,1)S(1)}, bf16[1024,512]{1,0:T(8,128)(2,1)}, u32[]{:S(2)}) copy-start(bf16[1024,512]{1,0:T(8,128)(2,1)} %param.12) | copy-start | bytes 3145732
  23.0 13.1 %copy-start.5 = (f32[1024]{0:T(1024)S(1)}, f32[1024]{0:T(1024)}, u32[]{:S(2)}) copy-start(f32[1024]{0:T(1024)} %param.11) | copy-start | bytes 12292
  23.1 13.0 %collective-permute-start.3 = (bf16[384,512]{1,0:T(8,128)(2,1)S(1)}, bf16[384,512]{1,0:T(8,128)(2,1)S(1)}, u32[]{:S(2)}, u32[]{:S(2)}) collective-permute-start(bf16[384,512]{1,0:T(8,128)(2,1)S(1)} %join.3.first_ref.rest_0_.refs_2_), channel_id=1, source_target_pairs={{0,1},{1,0},{2,6},{3,7},{4,5},{5,4},{6,2},{7,3},{8,9},{9,8},{10,14... | collective-permute-start | bytes 1179656 | tf_op jit(solution)/shard_map/ppermute | solution.py:399
  24.6 20.4 %collective-permute-start.11 = (bf16[384,512]{1,0:T(8,128)(2,1)S(1)}, bf16[384,512]{1,0:T(8,128)(2,1)S(1)}, u32[]{:S(2)}, u32[]{:S(2)}) collective-permute-start(bf16[384,512]{1,0:T(8,128)(2,1)S(1)} %join.3.first_ref.rest_0_.refs_2_), channel_id=1, source_target_pairs={{0,8},{1,9},{2,10},{3,11},{4,12},{5,13},{6,14},{7,15},{8,0},{9,1},... | collective-permute-start | bytes 1179656 | tf_op jit(solution)/shard_map/ppermute | solution.py:399
  36.0 6.7 %collective-permute-start.9 = (bf16[192,512]{1,0:T(8,128)(2,1)S(1)}, bf16[192,512]{1,0:T(8,128)(2,1)S(1)}, u32[]{:S(2)}, u32[]{:S(2)}) collective-permute-start(bf16[192,512]{1,0:T(8,128)(2,1)S(1)} %after.5.a_ref), channel_id=1, source_target_pairs={{0,4},{1,5},{2,3},{3,2},{4,0},{5,1},{6,7},{7,6},{8,12},{9,13},{10,... | collective-permute-start | bytes 589832 | tf_op jit(solution)/shard_map/ppermute | solution.py:399
  36.7 3.2 %copy-start.3 = (bf16[1024,512]{1,0:T(8,128)(2,1)S(1)}, bf16[1024,512]{1,0:T(8,128)(2,1)}, u32[]{:S(2)}) copy-start(bf16[1024,512]{1,0:T(8,128)(2,1)} %param.13) | copy-start | bytes 3145732
  36.7 3.2 %copy-start.4 = (bf16[1024,512]{1,0:T(8,128)(2,1)S(1)}, bf16[1024,512]{1,0:T(8,128)(2,1)}, u32[]{:S(2)}) copy-start(bf16[1024,512]{1,0:T(8,128)(2,1)} %param.14) | copy-start | bytes 3145732
  36.7 3.2 %collective-permute-start.4 = (bf16[192,512]{1,0:T(8,128)(2,1)S(1)}, bf16[192,512]{1,0:T(8,128)(2,1)S(1)}, u32[]{:S(2)}, u32[]{:S(2)}) collective-permute-start(bf16[192,512]{1,0:T(8,128)(2,1)S(1)} %get-tuple-element.11.rest_0_.refs_0_), channel_id=1, source_target_pairs={{0,2},{1,3},{2,0},{3,1},{4,6},{5,7},{6,4},{7,5},{8,10},{9,11},{10,... | collective-permute-start | bytes 589832 | tf_op jit(solution)/shard_map/ppermute | solution.py:399
  36.8 7.0 %collective-permute-start.6 = (bf16[192,512]{1,0:T(8,128)(2,1)S(1)}, bf16[192,512]{1,0:T(8,128)(2,1)S(1)}, u32[]{:S(2)}, u32[]{:S(2)}) collective-permute-start(bf16[192,512]{1,0:T(8,128)(2,1)S(1)} %after.4.a_ref), channel_id=1, source_target_pairs={{0,4},{1,5},{2,3},{3,2},{4,0},{5,1},{6,7},{7,6},{8,12},{9,13},{10,... | collective-permute-start | bytes 589832 | tf_op jit(solution)/shard_map/ppermute | solution.py:399
  38.9 10.5 %collective-permute-start.12 = (bf16[384,512]{1,0:T(8,128)(2,1)S(1)}, bf16[384,512]{1,0:T(8,128)(2,1)S(1)}, u32[]{:S(2)}, u32[]{:S(2)}) collective-permute-start(bf16[384,512]{1,0:T(8,128)(2,1)S(1)} %collective-permute-done.3.second_ref.refs_3_), channel_id=1, source_target_pairs={{0,8},{1,9},{2,10},{3,11},{4,12},{5,13},{6,14},{7,15},{8,0},{9,1},... | collective-permute-start | bytes 1179656 | tf_op jit(solution)/shard_map/ppermute | solution.py:399
  42.8 9.6 %collective-permute-start.10 = (bf16[384,512]{1,0:T(8,128)(2,1)S(1)}, bf16[384,512]{1,0:T(8,128)(2,1)S(1)}, u32[]{:S(2)}, u32[]{:S(2)}) collective-permute-start(bf16[384,512]{1,0:T(8,128)(2,1)S(1)} %join.5.refs_2_), channel_id=1, source_target_pairs={{0,1},{1,0},{2,6},{3,7},{4,5},{5,4},{6,2},{7,3},{8,9},{9,8},{10,14... | collective-permute-start | bytes 1179656 | tf_op jit(solution)/shard_map/ppermute | solution.py:399
  43.9 11.5 %collective-permute-start.7 = (bf16[384,512]{1,0:T(8,128)(2,1)S(1)}, bf16[384,512]{1,0:T(8,128)(2,1)S(1)}, u32[]{:S(2)}, u32[]{:S(2)}) collective-permute-start(bf16[384,512]{1,0:T(8,128)(2,1)S(1)} %join.4.refs_2_), channel_id=1, source_target_pairs={{0,1},{1,0},{2,6},{3,7},{4,5},{5,4},{6,2},{7,3},{8,9},{9,8},{10,14... | collective-permute-start | bytes 1179656 | tf_op jit(solution)/shard_map/ppermute | solution.py:399
  55.4 7.7 %copy-start = (bf16[1024,512]{1,0:T(8,128)(2,1)S(1)}, bf16[1024,512]{1,0:T(8,128)(2,1)}, u32[]{:S(2)}) copy-start(bf16[1024,512]{1,0:T(8,128)(2,1)} %param.15) | copy-start | bytes 3145732
  58.5 2.0 %collective-permute-start.13 = (f32[536,256]{1,0:T(8,128)S(1)}, f32[536,256]{1,0:T(8,128)S(1)}, u32[]{:S(2)}, u32[]{:S(2)}) collective-permute-start(f32[536,256]{1,0:T(8,128)S(1)} %slice.4), channel_id=1, source_target_pairs={{0,2},{1,3},{2,0},{3,1},{4,6},{5,7},{6,4},{7,5},{8,10},{9,11},{10,... | collective-permute-start | bytes 1646600 | tf_op jit(solution)/shard_map/ppermute | solution.py:399
  61.4 7.4 %collective-permute-start.14 = (bf16[208,512]{1,0:T(8,128)(2,1)S(1)}, bf16[208,512]{1,0:T(8,128)(2,1)S(1)}, u32[]{:S(2)}, u32[]{:S(2)}) collective-permute-start(bf16[208,512]{1,0:T(8,128)(2,1)S(1)} %combine.1.attended_ref), channel_id=1, source_target_pairs={{0,1},{1,0},{2,3},{3,2},{4,5},{5,4},{6,7},{7,6},{8,9},{9,8},{10,11... | collective-permute-start | bytes 638984 | tf_op jit(solution)/shard_map/ppermute | solution.py:399
